TPU v7x, 32 devices: a whole 2x2x4 slice. The times are simulated.
32 devices in a mesh: dp: 2 (over x), context: 4 (over z), tensor: 4 (over y, core).
Axes of the slice: x: 2, y: 2, z: 4, core: 2. Of those that a mesh axis runs over, the one named last changes fastest.
Arguments:
- streams: bfloat16 [2048, 3, 8192], P(('dp', 'context'), None, 'tensor'), parts along dimension 0, may hold values from -6 to 6
- short_filter: float32 [3, 3, 8192], P(None, None, 'tensor'), may hold values from -3 to 3
- decay_rate: float32 [8192, 16], P('tensor'), as said below
- residue: float32 [8192, 16], P('tensor'), may hold values from -0.26 to 0.26
- bias: float32 [8192], P('tensor'), may hold values from -4 to 4
Outputs:
- gated: bfloat16 [2048, 8192], P(('dp', 'context'), 'tensor'), parts along dimension 0
There are 2 independent parts, one for each index of `dp`. A program takes and returns all parts, laid end to end along the dimension named above; an argument that names none is the same for every part. Nothing has to cross between parts.
Inputs may be any that keep to these rules, and one draw needn't show every extreme that they name: `decay_rate`: positive.
All inputs are finite; a program needn't handle non-finite values.
Results may differ from a plain program's by a relative error of at most 0.0058.
Values may be sent and summed in bfloat16 or wider, within the bound.
No kernel may reach another device: no remote copies, remote signals or barrier semaphores. Data moves between devices by JAX's collectives and lax.ppermute only.
A program may use at most 384 MiB of HBM per device.

v0:
```python
import jax
import jax.numpy as jnp
from jax import lax
from jax.sharding import PartitionSpec as P

HIGH = lax.Precision.HIGHEST


def passed_along(value, axis, by):
    peers = lax.axis_size(axis)
    pairs = [(i, i + by) for i in range(peers) if 0 <= i + by < peers]
    return lax.ppermute(value, axis, pairs)


def featurize(raw, rim_rows, weights):
    extended = jnp.concatenate([rim_rows, raw], axis=0)
    return weights[0] * raw + weights[1] * extended[1:-1] + weights[2] * extended[:-2]


def block_terms(signal, rate, residue):
    channels, block_count, block_len = signal.shape
    log_pole = -rate
    positions = jnp.arange(block_len, dtype=jnp.float32)
    filter_taps = jnp.sum(
        residue[:, None, :] * jnp.exp(positions[None, :, None] * log_pole[:, None, :]), axis=2
    )
    offsets = jnp.arange(block_len, dtype=jnp.int32)
    lag_table = offsets[:, None] - offsets[None, :]
    toeplitz = jnp.where(
        lag_table[None] >= 0, jnp.take(filter_taps, jnp.maximum(lag_table, 0), axis=1), 0.0
    )
    within = jnp.einsum("cab,cnb->cna", toeplitz, signal, precision=HIGH)
    end_pow = jnp.exp((block_len - 1.0 - positions)[None, :, None] * log_pole[:, None, :])
    end_states = jnp.einsum("cbm,cnb->cnm", end_pow, signal, precision=HIGH)
    block_order = jnp.arange(block_count, dtype=jnp.float32)
    block_gaps = block_order[:, None] - 1.0 - block_order[None, :]
    span_pow = jnp.exp(
        block_len * jnp.maximum(block_gaps, 0.0)[None, None] * log_pole[:, :, None, None]
    )
    span_pow = jnp.where(block_gaps[None, None] >= 0.0, span_pow, 0.0)
    entering = jnp.einsum("cmnk,ckm->cnm", span_pow, end_states, precision=HIGH)
    out_pow = residue[:, None, :] * jnp.exp((positions + 1.0)[None, :, None] * log_pole[:, None, :])
    carried = jnp.einsum("cam,cnm->cna", out_pow, entering, precision=HIGH)
    tail_pow = jnp.exp(
        block_len * (block_count - 1.0 - block_order)[None, :, None] * log_pole[:, None, :]
    )
    end_state = jnp.sum(tail_pow * end_states, axis=1)
    return (within + carried, end_state)


def body(streams, short_filter, decay_rate, residue, bias):
    channels = streams.shape[2]
    context_size = lax.axis_size("context")
    context_rank = lax.axis_index("context")
    rim_rows = passed_along(streams[-2:], "context", 1).astype(jnp.float32)
    query_feat = featurize(streams[:, 0].astype(jnp.float32), rim_rows[:, 0], short_filter[0])
    key_feat = featurize(streams[:, 1].astype(jnp.float32), rim_rows[:, 1], short_filter[1])
    value_feat = featurize(streams[:, 2].astype(jnp.float32), rim_rows[:, 2], short_filter[2])
    product_rows = (key_feat * value_feat).astype(jnp.bfloat16)
    chan_dev = channels // context_size
    key_value = lax.all_to_all(product_rows, "context", split_axis=1, concat_axis=0, tiled=True)
    seq_len = key_value.shape[0]
    block_len = 256
    rate_dev = lax.dynamic_slice_in_dim(decay_rate, context_rank * chan_dev, chan_dev, 0)
    residue_dev = lax.dynamic_slice_in_dim(residue, context_rank * chan_dev, chan_dev, 0)
    bias_dev = lax.dynamic_slice_in_dim(bias, context_rank * chan_dev, chan_dev, 0)
    widened = key_value.astype(jnp.float32)
    signal = widened.T.reshape(chan_dev, seq_len // block_len, block_len)
    convolved, end_state = block_terms(signal, rate_dev, residue_dev)
    convolved = convolved.reshape(chan_dev, seq_len).T
    mixed = (convolved + bias_dev * widened).astype(jnp.bfloat16)
    returned = lax.all_to_all(mixed, "context", split_axis=0, concat_axis=1, tiled=True)
    return (query_feat * returned.astype(jnp.float32)).astype(jnp.bfloat16)


def solution(mesh):
    in_specs = (
        P(("dp", "context"), None, "tensor"),
        P(None, None, "tensor"),
        P("tensor", None),
        P("tensor", None),
        P("tensor"),
    )
    out_specs = P(("dp", "context"), "tensor")
    return jax.shard_map(body, mesh=mesh, in_specs=in_specs, out_specs=out_specs, check_vma=False)
```

profile of v0, /device:TPU:0, one launch (start us, length us, event | category | flops | bytes accessed | tf_op | source)
XLA Modules:
  0.0 568.8 jit_solution(4657880203588240285)
XLA Ops:
  0.0 0.9 slice.90
  0.9 0.0 copy-start.7
  0.9 5.1 collective-permute-start
  6.0 3.1 fusion.50
  9.1 0.0 copy-done.7
  9.1 0.6 fusion.51
  9.8 0.5 copy.79
  10.3 1.3 copy.80
  11.6 2.9 bitcast_convert_fusion
  14.5 0.1 copy.83
  14.6 0.0 collective-permute-done
  14.6 1.6 copy.57
  16.3 1.6 convert_element_type.44
  17.9 0.0 copy-start
  17.9 1.2 slice_bitcast_fusion.1
  19.1 0.8 copy-done
  19.8 4.9 fusion.25
  24.8 1.3 copy.60
  26.1 4.4 all-to-all-start
  30.6 0.8 dynamic-slice_negate_fusion
  31.4 0.1 copy.63
  31.5 0.0 copy-start.5
  31.6 0.1 copy.62
  31.7 0.3 copy-done.3
  32.0 0.2 copy-done.5
  32.3 11.1 %multiply_reduce_fusion = f32[512,256]{1,0:T(8,128)S(1)} fusion(f32[512,16]{1,0:T(8,128)S(1)} %copy.63, f32[512,16]{1,0:T(8,128)S(1)} %copy.62), kind=kLoop, calls=%fused_computation.16 | loop fusion | flops 6160384 | bytes 589824 | tf_op jit(solution)/shard_map/reduce_sum | solution.py:24
  43.4 0.2 copy.64
  43.6 0.0 copy-done.6
  43.6 255.1 %gather_fusion = f32[65536,512]{1,0:T(8,128)} fusion(f32[512,256]{0,1:T(8,128)S(1)} %copy.64, s32[65536]{0:T(1024)S(1)} %broadcast_clamp_fusion), kind=kCustom, calls=%fused_computation | custom fusion | bytes 268697600 | tf_op jit(solution)/shard_map/jit(_take)/gather | solution.py:30
  298.7 132.7 %copy.65 = f32[256,256,512]{1,0,2:T(8,128)} copy(f32[256,256,512]{2,1,0:T(8,128)} %bitcast.24) | data formatting | bytes 268435456 | tf_op jit(solution)/shard_map/jit(_take)/gather | solution.py:30
  431.4 0.8 dynamic_slice.11
  432.2 0.1 maximum_compare_fusion
  432.2 0.1 fusion.47
  432.3 0.1 maximum_multiply_fusion
  432.4 0.0 all-to-all-done
  432.4 1.5 copy.61
  433.9 0.8 reshape.143
  434.7 0.0 copy-start.1
  434.7 0.0 copy-start.4
  434.7 6.3 %fusion.43 = f32[512,16,4]{1,2,0:T(4,128)S(1)} fusion(bf16[512,4,256]{2,1,0:T(4,128)(2,1)S(1)} %reshape.143, f32[256]{0:T(256)S(1)} %iota_subtract_fusion.2, f32[512,16]{1,0:T(8,128)} %copy-done.5), kind=kOutput, calls=%fused_computation.53 | convolution fusion | flops 102760448 | bytes 1213440 | tf_op jit(solution)/shard_map/cbm,cnb->cnm/dot_general | solution.py:34
  441.0 0.0 copy-done.1
  441.0 0.3 copy.81
  441.4 0.0 copy-done.4
  441.4 0.2 multiply_reduce_fusion.1
  441.6 0.4 copy.77
  442.0 8.6 %fusion.8 = f32[512,4,256]{2,1,0:T(4,128)} fusion(f32[512,16,4]{1,2,0:T(4,128)S(1)} %copy.77, f32[256]{0:T(256)S(1)} %iota_add_fusion, f32[512,16]{1,0:T(8,128)} %copy-done.5, f32[512,16]{1,0:T(8,128)} %copy-done.6), kind=kOutput, calls=%fused_computation.9 | convolution fusion | flops 104857600 | bytes 2294784 | tf_op jit(solution)/shard_map/cam,cnm->cna/dot_general | solution.py:43
  450.5 77.4 %fusion.40 = f32[512,4,256]{2,1,0:T(4,128)S(1)} fusion(f32[512,4,256]{2,1,0:T(4,128)} %fusion.8, bf16[512,4,256]{2,1,0:T(4,128)(2,1)} %copy-done.1, f32[256,256,512]{1,0,2:T(8,128)} %copy.65, pred[256,256]{1,0:T(8,128)(4,1)S(1)} %get-tuple-element.25, pred[256,256]{1,0:T(8,128)(4,1)S(1)} %get-tuple-element.24), kind=kOutput, calls=%fused_computation.52 | convolution fusion | flops 1678245888 | bytes 139591680 | tf_op jit(solution)/shard_map/cab,cnb->cna/dot_general | solution.py:32
  528.0 0.5 copy.84
  528.4 0.4 fusion.39
  528.8 0.0 copy-start.2
  528.8 1.4 copy.67
  530.2 4.9 all-to-all-start.1
  535.0 0.0 copy-done.2
  535.0 0.5 copy.78
  535.5 0.0 copy-start.8
  535.6 0.0 copy-start.9
  535.6 0.2 bitcast_convert_fusion.2
  535.7 24.5 %all-to-all-done.1 = bf16[4,256,512]{2,1,0:T(8,128)(2,1)} async-done(((bf16[4,256,512]{2,1,0:T(8,128)(2,1)}), bf16[4,256,512]{2,1,0:T(8,128)(2,1)}, u32[]{:S(2)}, u32[]{:S(2)}) %all-to-all-start.1) | async-done | bytes 1048608 | tf_op jit(solution)/shard_map/all_to_all | solution.py:72
  560.3 1.5 copy.68
  561.8 0.0 copy-done.8
  561.8 0.0 copy-done.9
  561.8 0.0 copy-done.10
  561.8 4.7 fusion.35
  566.5 2.3 copy.69
  (8 shorter events, 0.1 us)
Async XLA Ops:
  0.9 8.2 %copy-start.7 = (f32[3,3,2048]{2,1,0:T(4,128)S(1)}, f32[3,3,2048]{2,1,0:T(4,128)}, u32[]{:S(2)}) copy-start(f32[3,3,2048]{2,1,0:T(4,128)} %param.6) | copy-start | bytes 221188
  0.9 13.7 %collective-permute-start = (bf16[2,3,2048]{2,0,1:T(2,128)(2,1)S(1)}, bf16[2,3,2048]{2,0,1:T(2,128)(2,1)S(1)}, u32[]{:S(2)}, u32[]{:S(2)}) collective-permute-start(bf16[2,3,2048]{2,0,1:T(2,128)(2,1)S(1)} %slice.90), channel_id=1, source_target_pairs={{0,4},{4,8},{8,12},{1,5},{5,9},{9,13},{2,6},{6,10},{10,14},{3,7},{... | collective-permute-start | bytes 73736 | tf_op jit(solution)/shard_map/ppermute | solution.py:12
  17.9 2.0 copy-start
  26.1 406.2 %all-to-all-start = ((bf16[256,4,512]{2,0,1:T(8,128)(2,1)}), bf16[256,4,512]{2,0,1:T(8,128)(2,1)}, u32[]{:S(2)}, u32[]{:S(2)}) async-start(bf16[256,4,512]{2,0,1:T(8,128)(2,1)} %copy.60), calls=%async_computation | async-start | bytes 2097152 | tf_op jit(solution)/shard_map/all_to_all | solution.py:61
  31.4 0.6 copy-start.3
  31.5 0.7 copy-start.5
  32.3 11.3 %copy-start.6 = (f32[512,16]{1,0:T(8,128)}, f32[512,16]{1,0:T(8,128)S(1)}, u32[]{:S(2)}) copy-start(f32[512,16]{1,0:T(8,128)S(1)} %copy.62) | copy-start | bytes 98308
  434.7 6.4 %copy-start.1 = (bf16[512,4,256]{2,1,0:T(4,128)(2,1)}, bf16[512,4,256]{2,1,0:T(4,128)(2,1)S(1)}, u32[]{:S(2)}) copy-start(bf16[512,4,256]{2,1,0:T(4,128)(2,1)S(1)} %reshape.143) | copy-start | bytes 3145732
  434.7 6.7 %copy-start.4 = (f32[512,16]{0,1:T(8,128)S(1)}, f32[512,16]{0,1:T(8,128)}, u32[]{:S(2)}) copy-start(f32[512,16]{0,1:T(8,128)} %copy-done.3) | copy-start | bytes 98308
  528.8 6.2 %copy-start.2 = (bf16[256,1,2048]{2,0,1:T(8,128)(2,1)S(1)}, bf16[256,1,2048]{2,0,1:T(8,128)(2,1)}, u32[]{:S(2)}) copy-start(bf16[256,1,2048]{2,0,1:T(8,128)(2,1)} %get-tuple-element.6) | copy-start | bytes 3145732
  530.2 30.1 %all-to-all-start.1 = ((bf16[4,256,512]{2,1,0:T(8,128)(2,1)}), bf16[4,256,512]{2,1,0:T(8,128)(2,1)}, u32[]{:S(2)}, u32[]{:S(2)}) async-start(bf16[4,256,512]{2,1,0:T(8,128)(2,1)} %bitcast.28), calls=%async_computation.1 | async-start | bytes 2097152 | tf_op jit(solution)/shard_map/all_to_all | solution.py:72
  535.5 26.2 %copy-start.8 = (f32[1,1,2048]{2,1,0:T(1,128)S(1)}, f32[1,1,2048]{2,1,0:T(1,128)}, u32[]{:S(2)}) copy-start(f32[1,1,2048]{2,1,0:T(1,128)} %get-tuple-element.15) | copy-start | bytes 24580
  535.6 26.2 %copy-start.9 = (f32[1,1,2048]{2,1,0:T(1,128)S(1)}, f32[1,1,2048]{2,1,0:T(1,128)}, u32[]{:S(2)}) copy-start(f32[1,1,2048]{2,1,0:T(1,128)} %get-tuple-element.16) | copy-start | bytes 24580
  535.6 26.2 %copy-start.10 = (f32[1,1,2048]{2,1,0:T(1,128)S(1)}, f32[1,1,2048]{2,1,0:T(1,128)}, u32[]{:S(2)}) copy-start(f32[1,1,2048]{2,1,0:T(1,128)} %get-tuple-element.17) | copy-start | bytes 24580
where the time goes:
time: 571 us; the launch traced here: 569 us
  local copies, waits for them, and re-layouts  410 us (72%)
  matrix products  92.3 us (16%)
  other arithmetic  27 us (5%)
  waiting for transfers between devices  24.6 us (4%)
  starting transfers between devices  14.4 us (3%)
    gather x2, local copies, waits for them, and re-layouts, block_terms(): jnp.take(filter_taps, jnp.maximum(lag_table, 0), axis=1)  388 us
    dot_general x1, matrix products, block_terms(): within = jnp.einsum('cab,cnb->cna', toeplitz, signal, precision=HIGH)  77.4 us
    all_to_all x1, waiting for transfers between devices, body(): lax.all_to_all(mixed, 'context', split_axis=0, concat_axis=1, tiled=True)  24.5 us
  transfers between devices with their start and end apart: 3, of which 1 were waited for; matrix products, arithmetic and copies ran while one was open for 72% of the time, Pallas kernels for 0%

commit v1 on v0

v1 whole, which is shorter than its diff:
```python
import functools

import jax
import jax.numpy as jnp
from jax import lax
from jax.experimental import pallas as pl
from jax.experimental.pallas import tpu as pltpu
from jax.sharding import PartitionSpec as P

F32 = jnp.float32
BF16 = jnp.bfloat16
LANES = 128
SUB = 8
GROUP = LANES * SUB
CHUNK = 16
PAD = 8


def total(values):
    values = list(values)
    while len(values) > 1:
        pairs = [values[i] + values[i + 1] for i in range(0, len(values) - 1, 2)]
        values = pairs + ([values[-1]] if len(values) % 2 else [])
    return values[0]


def lay_rows(scratch, stride, source, rows, base=0):
    for j in range(SUB):
        scratch[pl.ds(j * stride + base, rows), :] = source(j)


def row(scratch, stride, t):
    return scratch[pl.ds(t, SUB, stride=stride), :]


def lanes(j):
    return pl.ds(j * LANES, LANES)


def state_kernel(k_ref, v_ref, w_ref, rate_ref, kv_ref, states_ref, end_ref, rate_out_ref, ks, vs, small, power):
    tokens, modes = k_ref.shape[1], rate_ref.shape[0]
    stride = tokens + PAD
    small_stride = modes + PAD
    lay_rows(ks, stride, lambda j: k_ref[0, :, lanes(j)].astype(F32), tokens)
    lay_rows(vs, stride, lambda j: v_ref[0, :, lanes(j)].astype(F32), tokens)
    lay_rows(small, small_stride, lambda j: rate_ref[:, lanes(j)], modes)
    p = []
    for m in range(modes):
        rate = row(small, small_stride, m)
        rate_out_ref[0, m] = rate
        p.append(jnp.exp(-rate))
        power[m] = jnp.exp(-CHUNK * rate)
        end_ref[0, m] = jnp.zeros((SUB, LANES), F32)
    for stream in (1, 2):
        lay_rows(small, small_stride, lambda j: w_ref[stream, :, lanes(j)], 3, base=3 * (stream - 1))
    wk = [row(small, small_stride, i) for i in range(3)]
    wv = [row(small, small_stride, 3 + i) for i in range(3)]

    def chunk(c, carry):
        k1, k2, v1, v2 = carry
        acc = None
        for i in range(CHUNK):
            t = c * CHUNK + i
            k, v = row(ks, stride, t), row(vs, stride, t)
            key = wk[0] * k + wk[1] * k1 + wk[2] * k2
            value = wv[0] * v + wv[1] * v1 + wv[2] * v2
            k1, k2, v1, v2 = k, k1, v, v1
            product = (key * value).astype(BF16).astype(F32)
            if i < 2:
                product = jnp.where(c > 0, product, 0.0)
            kv_ref[0, t] = product
            acc = [product] * modes if acc is None else [a * b + product for a, b in zip(acc, p)]
        for m in range(modes):
            states_ref[0, c, m] = acc[m]
            end_ref[0, m] = end_ref[0, m] * power[m] + acc[m]
        return k1, k2, v1, v2

    zero = jnp.zeros((SUB, LANES), F32)
    lax.fori_loop(0, tokens // CHUNK, chunk, (zero,) * 4)


def near_kernel(q_ref, w_ref, rate_ref, residue_ref, bias_ref, kv_ref, near_ref, query_ref, gains_ref, qs, small, taps):
    tokens, modes = q_ref.shape[1], residue_ref.shape[0]
    stride = tokens + PAD
    small_stride = modes + PAD
    lay_rows(qs, stride, lambda j: q_ref[0, :, lanes(j)].astype(F32), tokens)
    lay_rows(small, small_stride, lambda j: residue_ref[:, lanes(j)], modes)
    lay_rows(small, small_stride, lambda j: bias_ref[:, lanes(j)], 1, base=modes)
    lay_rows(small, small_stride, lambda j: w_ref[0, :, lanes(j)], 3, base=modes + 1)
    bias = row(small, small_stride, modes)
    gains_ref[0, modes] = bias
    gain = []
    for m in range(modes):
        residue = row(small, small_stride, m)
        gains_ref[0, m] = residue
        gain.append(residue)
    p = [jnp.exp(-rate_ref[0, m]) for m in range(modes)]
    taps[0] = total(gain) + bias
    for i in range(1, CHUNK):
        gain = [a * b for a, b in zip(gain, p)]
        taps[i] = total(gain)
    w = [row(small, small_stride, modes + 1 + i) for i in range(3)]
    h = [taps[i] for i in range(CHUNK)]

    def chunk(c, carry):
        q1, q2 = carry
        window = []
        for i in range(CHUNK):
            t = c * CHUNK + i
            q = row(qs, stride, t)
            query_ref[0, t] = w[0] * q + w[1] * q1 + w[2] * q2
            q1, q2 = q, q1
            window.append(kv_ref[0, t])
            near_ref[0, t] = total(h[n] * window[i - n] for n in range(i + 1))
        return q1, q2

    zero = jnp.zeros((SUB, LANES), F32)
    lax.fori_loop(0, tokens // CHUNK, chunk, (zero, zero))


def emit_kernel(near_ref, query_ref, states_ref, entering_ref, rate_ref, gains_ref, rim_ref, out_ref, power, state, turned):
    tokens, modes = near_ref.shape[1], rate_ref.shape[1]
    stride = CHUNK + PAD
    p = []
    for m in range(modes):
        rate = rate_ref[0, m]
        p.append(jnp.exp(-rate))
        power[m] = jnp.exp(-CHUNK * rate)
        state[m] = entering_ref[0, m]
    kv0, kv1, query0, query1 = (rim_ref[i, 0] for i in range(4))

    def chunk(c, first):
        g = [gains_ref[0, m] * state[m] for m in range(modes)]
        for i in range(CHUNK):
            t = c * CHUNK + i
            g = [a * b for a, b in zip(g, p)]
            near, query = near_ref[0, t], query_ref[0, t]
            if first and i < 2:
                kv = (kv0, kv1)[i]
                g = [a + gains_ref[0, m] * kv for m, a in enumerate(g)]
                near = near + gains_ref[0, modes] * kv
                query = query + (query0, query1)[i]
            mixed = (near + total(g)).astype(BF16).astype(F32)
            turned[pl.ds(i, SUB, stride=stride), :] = query * mixed
        for m in range(modes):
            held = state[m]
            if first:
                held = (held * p[m] + kv0) * p[m] + kv1
                held = held * jnp.exp(-(CHUNK - 2) * rate_ref[0, m])
            else:
                held = held * power[m]
            state[m] = held + states_ref[0, c, m]
        rows = pl.ds(c * CHUNK if first else pl.multiple_of(c * CHUNK, CHUNK), CHUNK)
        for j in range(SUB):
            out_ref[rows, lanes(j)] = turned[pl.ds(j * stride, CHUNK), :].astype(BF16)

    chunk(0, True)

    def later(c, carry):
        chunk(c, False)
        return carry

    lax.fori_loop(1, tokens // CHUNK, later, 0)


def whole(shape):
    return pl.BlockSpec((1,) + shape[1:], lambda g: (g,) + (0,) * (len(shape) - 1))


def params():
    return pltpu.CompilerParams(vmem_limit_bytes=48 * 2**20)


def cost(flops, nbytes):
    return pl.CostEstimate(flops=flops, bytes_accessed=nbytes, transcendentals=0)


def body(streams, short_filter, decay_rate, residue, bias):
    tokens, _, channels = streams.shape
    modes = decay_rate.shape[1]
    groups = channels // GROUP
    chunks = tokens // CHUNK
    size = lax.axis_size("context")
    rank = lax.axis_index("context")
    by_stream = streams.transpose(1, 0, 2)
    rate_rows, residue_rows, bias_row = decay_rate.T, residue.T, bias.reshape(1, channels)

    ring = [(i, (i + 1) % size) for i in range(size)]
    rim = lax.ppermute(streams[-2:], "context", ring)

    def stream_spec(which):
        return pl.BlockSpec((1, tokens, GROUP), lambda g: (which, 0, g))

    def column_spec(rows):
        return pl.BlockSpec((rows, GROUP), lambda g: (0, g))

    filter_spec = pl.BlockSpec((3, 3, GROUP), lambda g: (0, 0, g))
    kv_shape = (groups, tokens, SUB, LANES)
    states_shape = (groups, chunks, modes, SUB, LANES)
    mode_shape = (groups, modes, SUB, LANES)
    gains_shape = (groups, modes + 1, SUB, LANES)
    shape = functools.partial(jax.ShapeDtypeStruct, dtype=F32)
    turn = pltpu.VMEM((SUB * (tokens + PAD), LANES), F32)
    small = pltpu.VMEM((SUB * (modes + PAD), LANES), F32)
    key_value, states, end, rate = pl.pallas_call(
        state_kernel,
        grid=(groups,),
        in_specs=[stream_spec(1), stream_spec(2), filter_spec, column_spec(modes)],
        out_specs=[whole(kv_shape), whole(states_shape), whole(mode_shape), whole(mode_shape)],
        out_shape=[shape(kv_shape), shape(states_shape), shape(mode_shape), shape(mode_shape)],
        scratch_shapes=[turn, turn, small, pltpu.VMEM((modes, SUB, LANES), F32)],
        compiler_params=params(),
        cost_estimate=cost(48 * tokens * channels, 6 * 2**20),
        name="states",
    )(by_stream, by_stream, short_filter, rate_rows)

    edge = jnp.where(rank == 0, 0.0, rim.astype(F32))
    head = streams[:2].astype(F32)
    rows = jnp.concatenate([edge, head], axis=0)
    features = [
        [
            short_filter[i, 0] * rows[2 + t, i] + short_filter[i, 1] * rows[1 + t, i] + short_filter[i, 2] * rows[t, i]
            for t in range(2)
        ]
        for i in (1, 2)
    ]
    kv_head = [lax.reduce_precision(features[0][t] * features[1][t], 8, 7) for t in range(2)]
    query_head = [
        short_filter[0, 1] * edge[1, 0] + short_filter[0, 2] * edge[0, 0],
        short_filter[0, 2] * edge[1, 0],
    ]
    tiled = [x.reshape(groups, SUB, LANES) for x in kv_head + query_head]
    rim_terms = jnp.stack(tiled)
    end = end + jnp.exp(-(tokens - 1.0) * rate) * tiled[0][:, None] + jnp.exp(-(tokens - 2.0) * rate) * tiled[1][:, None]

    entering = jnp.zeros_like(end)
    span = 1
    near = None
    while span < size:
        other = lax.ppermute(end, "context", [(i, i ^ span) for i in range(size)])
        if near is None:
            near, query, gains = pl.pallas_call(
                near_kernel,
                grid=(groups,),
                in_specs=[
                    stream_spec(0), filter_spec, whole(mode_shape), column_spec(modes), column_spec(1), whole(kv_shape),
                ],
                out_specs=[whole(kv_shape), whole(kv_shape), whole(gains_shape)],
                out_shape=[shape(kv_shape), shape(kv_shape), shape(gains_shape)],
                scratch_shapes=[
                    turn, pltpu.VMEM((SUB * (modes + 2 * PAD), LANES), F32), pltpu.VMEM((CHUNK, SUB, LANES), F32),
                ],
                compiler_params=params(),
                cost_estimate=cost(24 * tokens * channels, 7 * 2**20),
                name="near",
            )(by_stream, short_filter, rate, residue_rows, bias_row, key_value)
        right = (rank & span) != 0
        ahead = (rank & (span - 1)).astype(F32)
        entering = jnp.where(right, entering + jnp.exp(-(tokens * ahead) * rate) * other, entering)
        if 2 * span < size:
            late, early = jnp.where(right, end, other), jnp.where(right, other, end)
            end = late + jnp.exp(-(1.0 * tokens * span) * rate) * early
        span *= 2

    return pl.pallas_call(
        emit_kernel,
        grid=(groups,),
        in_specs=[
            whole(kv_shape), whole(kv_shape), whole(states_shape), whole(mode_shape), whole(mode_shape), whole(gains_shape),
            pl.BlockSpec((4, 1, SUB, LANES), lambda g: (0, g, 0, 0)),
        ],
        out_specs=pl.BlockSpec((tokens, GROUP), lambda g: (0, g)),
        out_shape=jax.ShapeDtypeStruct((tokens, channels), BF16),
        scratch_shapes=[
            pltpu.VMEM((modes, SUB, LANES), F32),
            pltpu.VMEM((modes, SUB, LANES), F32),
            pltpu.VMEM((SUB * (CHUNK + PAD), LANES), F32),
        ],
        compiler_params=params(),
        cost_estimate=cost(40 * tokens * channels, 7 * 2**20),
        name="emit",
    )(near, query, states, entering, rate, gains, rim_terms)


def solution(mesh):
    in_specs = (
        P(("dp", "context"), None, "tensor"),
        P(None, None, "tensor"),
        P("tensor", None),
        P("tensor", None),
        P("tensor"),
    )
    out_specs = P(("dp", "context"), "tensor")
    return jax.shard_map(body, mesh=mesh, in_specs=in_specs, out_specs=out_specs, check_vma=False)
```

time: 571 us -> 32.2 us (0.06)
  local copies, waits for them, and re-layouts: 410 us -> 5.43 us
  matrix products: 92.3 us -> 0 us
  other arithmetic: 27 us -> 0.35 us
  waiting for transfers between devices: 24.6 us -> 4.86 us
  Pallas kernels: 0 us -> 13.8 us
  starting transfers between devices: 14.4 us -> 7.37 us
    gather x2 -> x0, local copies, waits for them, and re-layouts: 388 us -> none  [block_terms(): jnp.take(filter_taps, jnp.maximum(lag_table, 0), axis=1)]
    dot_general x3 -> x0, matrix products: 92.3 us -> none  [the longest x1 77.4 us: block_terms(): within = jnp.einsum('cab,cnb->cna', toeplitz, signal, precision=HIGH)]
    all_to_all x2 -> x0, waiting for transfers between devices: 24.6 us -> none  [the longest x1 24.5 us: body(): lax.all_to_all(mixed, 'context', split_axis=0, concat_axis=1, tiled=True)]
    convert_element_type x6 -> x1, other arithmetic: 14.7 us -> 0.02 us  [body(): head = streams[:2].astype(F32)]
    pallas_call x0 -> x3, Pallas kernels: none -> 13.8 us  [the longest x1 5.27 us: body(): pl.pallas_call(emit_kernel, grid=(groups,), in_specs=[whole(kv_shape), wh...]
    reduce_sum x1 -> x0, other arithmetic: 11.1 us -> none  [block_terms(): jnp.sum(residue[:, None, :] * jnp.exp(positions[None, :, None] * log_pole...]
    all_to_all x2 -> x0, starting transfers between devices: 9.3 us -> none  [the longest x1 4.86 us: body(): lax.all_to_all(mixed, 'context', split_axis=0, concat_axis=1, tiled=True)]
  transfers between devices with their start and end apart: 3 -> 3, of which waited for: 1 -> 2; matrix products, arithmetic and copies ran while one was open for 72% -> 0% of each run, Pallas kernels for 0% -> 27%
where the time goes in v1:
time: 32.2 us; the launch traced here: 31.9 us
  Pallas kernels  13.8 us (43%)
  starting transfers between devices  7.37 us (23%)
  local copies, waits for them, and re-layouts  5.43 us (17%)
  waiting for transfers between devices  4.86 us (15%)
  other arithmetic  0.35 us (1%)
    pallas_call x1, Pallas kernels, body(): pl.pallas_call(emit_kernel, grid=(groups,), in_specs=[whole(kv_shape), wh...  5.27 us
    pallas_call x1, Pallas kernels, body(): pl.pallas_call(state_kernel, grid=(groups,), in_specs=[stream_spec(1), st...  5.1 us
    ppermute x2, waiting for transfers between devices, body(): other = lax.ppermute(end, 'context', [(i, i ^ span) for i in range(size)])  4.85 us
    unnamed x15, local copies, waits for them, and re-layouts  4.45 us
    ppermute x2, starting transfers between devices, body(): other = lax.ppermute(end, 'context', [(i, i ^ span) for i in range(size)])  4.3 us
    pallas_call x1, Pallas kernels, body(): pl.pallas_call(near_kernel, grid=(groups,), in_specs=[stream_spec(0), fil...  3.43 us
    ppermute x1, starting transfers between devices, body(): rim = lax.ppermute(streams[-2:], 'context', ring)  3.08 us
    slice x1, local copies, waits for them, and re-layouts, body(): rim = lax.ppermute(streams[-2:], 'context', ring)  0.98 us
  transfers between devices with their start and end apart: 3, of which 2 were waited for; matrix products, arithmetic and copies ran while one was open for 0% of the time, Pallas kernels for 27%

profile of v1, /device:TPU:0, one launch (start us, length us, event | category | flops | bytes accessed | tf_op | source)
XLA Modules:
  0.0 31.9 jit_solution(1156973515269223641)
XLA Ops:
  0.0 1.0 %fusion.9 = (bf16[2,3,2048]{2,0,1:T(2,128)(2,1)S(1)}, bf16[2,3,2048]{2,0,1:T(2,128)(2,1)S(1)}) fusion(bf16[256,3,2048]{2,0,1:T(8,128)(2,1)} %param.5), kind=kLoop, calls=%fused_computation.22 | loop fusion | bytes 98304 | tf_op jit(solution)/shard_map/slice | solution.py:189
  1.0 3.1 %collective-permute-start = (bf16[2,3,2048]{2,1,0:T(4,128)(2,1)S(1)}, bf16[2,3,2048]{2,1,0:T(4,128)(2,1)S(1)}, u32[]{:S(2)}, u32[]{:S(2)}) collective-permute-start(bf16[2,3,2048]{2,1,0:T(4,128)(2,1)S(1)} %copy.9), channel_id=1, source_target_pairs={{0,4},{4,8},{8,12},{12,0},{1,5},{5,9},{9,13},{13,1},{2,6},{6,10},{... | collective-permute-start | bytes 73736 | tf_op jit(solution)/shard_map/ppermute | solution.py:189
  4.1 0.0 copy-start.2
  4.1 0.9 %copy-done.2 = f32[3,3,2048]{2,1,0:T(4,128)S(1)} copy-done((f32[3,3,2048]{2,1,0:T(4,128)S(1)}, f32[3,3,2048]{2,1,0:T(4,128)}, u32[]{:S(2)}) %copy-start.2) | copy-done | bytes 73752
  5.0 0.0 copy-start.4
  5.0 0.9 %copy-done.4 = f32[2048,16]{0,1:T(8,128)S(1)} copy-done((f32[2048,16]{0,1:T(8,128)S(1)}, f32[2048,16]{0,1:T(8,128)}, u32[]{:S(2)}) %copy-start.4) | copy-done | bytes 131096
  5.9 0.0 copy-start.3
  5.9 0.0 copy-start.5
  5.9 0.0 copy-start.6
  5.9 5.1 %states.1 = (f32[2,256,8,128]{3,2,1,0:T(8,128)S(1)}, f32[2,16,16,8,128]{4,3,2,1,0:T(8,128)S(1)}, f32[2,16,8,128]{3,2,1,0:T(8,128)S(1)}, f32[2,16,8,128]{3,2,1,0:T(8,128)S(1)}) custom-call(bf16[3,256,2048]{2,1,0:T(8,128)(2,1)} %bitcast.13, bf16[3,256,2048]{2,1,0:T(8,128)(2,1)} %bitcast.14, f32[3,3,2048]{2,1,0:T(4,128)S(1)} %copy-done.2, f32[16,2048]{1,0:T(8,128)S(1)} %bitcast.10), custom_call_target="tpu_custom_call" | custom-call | flops 25165824 | bytes 6291456 | tf_op jit(solution)/shard_map/states/pallas_call | solution.py:205
  11.0 0.0 copy-start
  11.0 1.3 %copy-done = f32[2,16,16,8,128]{4,3,2,1,0:T(8,128)} copy-done((f32[2,16,16,8,128]{4,3,2,1,0:T(8,128)}, f32[2,16,16,8,128]{4,3,2,1,0:T(8,128)S(1)}, u32[]{:S(2)}) %copy-start) | copy-done | bytes 2097176
  12.4 0.0 copy-start.1
  12.4 1.3 %copy-done.1 = f32[2,256,8,128]{3,2,1,0:T(8,128)} copy-done((f32[2,256,8,128]{3,2,1,0:T(8,128)}, f32[2,256,8,128]{3,2,1,0:T(8,128)S(1)}, u32[]{:S(2)}) %copy-start.1) | copy-done | bytes 2097176
  13.7 0.0 collective-permute-done
  13.7 0.1 multiply_reduce-precision_fusion
  13.8 0.1 fusion
  13.9 0.1 multiply_add_fusion.1
  13.9 1.6 %collective-permute-start.1 = (f32[2,16,8,128]{3,2,1,0:T(8,128)S(1)}, f32[2,16,8,128]{3,2,1,0:T(8,128)S(1)}, u32[]{:S(2)}, u32[]{:S(2)}) collective-permute-start(f32[2,16,8,128]{3,2,1,0:T(8,128)S(1)} %multiply_add_fusion.1), channel_id=1, source_target_pairs={{0,4},{4,0},{8,12},{12,8},{1,5},{5,1},{9,13},{13,9},{2,6},{6,2},{1... | collective-permute-start | bytes 393224 | tf_op jit(solution)/shard_map/ppermute | solution.py:240
  15.6 3.4 %collective-permute-done.1 = f32[2,16,8,128]{3,2,1,0:T(8,128)S(1)} collective-permute-done((f32[2,16,8,128]{3,2,1,0:T(8,128)S(1)}, f32[2,16,8,128]{3,2,1,0:T(8,128)S(1)}, u32[]{:S(2)}, u32[]{:S(2)}) %collective-permute-start.1) | collective-permute-done | bytes 131104 | tf_op jit(solution)/shard_map/ppermute | solution.py:240
  19.0 2.7 %collective-permute-start.2 = (f32[2,16,8,128]{3,2,1,0:T(8,128)S(1)}, f32[2,16,8,128]{3,2,1,0:T(8,128)S(1)}, u32[]{:S(2)}, u32[]{:S(2)}) collective-permute-start(f32[2,16,8,128]{3,2,1,0:T(8,128)S(1)} %multiply_add_fusion), channel_id=1, source_target_pairs={{0,8},{4,12},{8,0},{12,4},{1,9},{5,13},{9,1},{13,5},{2,10},{6,14},... | collective-permute-start | bytes 393224 | tf_op jit(solution)/shard_map/ppermute | solution.py:240
  21.7 0.0 copy-done.3
  21.7 0.0 copy-done.5
  21.7 0.0 copy-done.6
  21.7 3.4 %near.1 = (f32[2,256,8,128]{3,2,1,0:T(8,128)S(1)}, f32[2,256,8,128]{3,2,1,0:T(8,128)S(1)}, f32[2,17,8,128]{3,2,1,0:T(8,128)S(1)}) custom-call(bf16[3,256,2048]{2,1,0:T(8,128)(2,1)} %bitcast.15, f32[3,3,2048]{2,1,0:T(4,128)S(1)} %copy-done.3, f32[2,16,8,128]{3,2,1,0:T(8,128)S(1)} %get-tuple-element.12.rate_ref, f32[16,2048]{1,0:T(8,128)S(1)} %bitcast.11, ...), custom_call_target="tpu_custom_call" | custom-call | flops 12582912 | bytes 7340032 | tf_op jit(solution)/shard_map/near/pallas_call | solution.py:242
  25.1 1.5 %collective-permute-done.2 = f32[2,16,8,128]{3,2,1,0:T(8,128)S(1)} collective-permute-done((f32[2,16,8,128]{3,2,1,0:T(8,128)S(1)}, f32[2,16,8,128]{3,2,1,0:T(8,128)S(1)}, u32[]{:S(2)}, u32[]{:S(2)}) %collective-permute-start.2) | collective-permute-done | bytes 131104 | tf_op jit(solution)/shard_map/ppermute | solution.py:240
  26.6 0.1 add_select_fusion.entering_ref
  26.7 5.3 %emit.1 = bf16[256,2048]{1,0:T(8,128)(2,1)} custom-call(f32[2,256,8,128]{3,2,1,0:T(8,128)S(1)} %get-tuple-element.14.near_ref, f32[2,256,8,128]{3,2,1,0:T(8,128)S(1)} %get-tuple-element.15.query_ref, f32[2,16,16,8,128]{4,3,2,1,0:T(8,128)} %copy-done, f32[2,16,8,128]{3,2,1,0:T(8,128)S(1)} %add_select_fusion.entering_ref, ...), custom_call_target="tpu_custom_call" | custom-call | flops 20971520 | bytes 7340032 | tf_op jit(solution)/shard_map/emit/pallas_call | solution.py:265
  (5 shorter events, 0.1 us)
Async XLA Ops:
  1.0 12.7 %collective-permute-start = (bf16[2,3,2048]{2,1,0:T(4,128)(2,1)S(1)}, bf16[2,3,2048]{2,1,0:T(4,128)(2,1)S(1)}, u32[]{:S(2)}, u32[]{:S(2)}) collective-permute-start(bf16[2,3,2048]{2,1,0:T(4,128)(2,1)S(1)} %copy.9), channel_id=1, source_target_pairs={{0,4},{4,8},{8,12},{12,0},{1,5},{5,9},{9,13},{13,1},{2,6},{6,10},{... | collective-permute-start | bytes 73736 | tf_op jit(solution)/shard_map/ppermute | solution.py:189
  4.1 0.9 %copy-start.2 = (f32[3,3,2048]{2,1,0:T(4,128)S(1)}, f32[3,3,2048]{2,1,0:T(4,128)}, u32[]{:S(2)}) copy-start(f32[3,3,2048]{2,1,0:T(4,128)} %w_ref.3) | copy-start | bytes 221188
  5.0 0.9 %copy-start.4 = (f32[2048,16]{0,1:T(8,128)S(1)}, f32[2048,16]{0,1:T(8,128)}, u32[]{:S(2)}) copy-start(f32[2048,16]{0,1:T(8,128)} %param.7) | copy-start | bytes 393220
  5.9 15.8 %copy-start.3 = (f32[3,3,2048]{2,1,0:T(4,128)S(1)}, f32[3,3,2048]{2,1,0:T(4,128)}, u32[]{:S(2)}) copy-start(f32[3,3,2048]{2,1,0:T(4,128)} %w_ref.3) | copy-start | bytes 221188
  5.9 15.8 %copy-start.5 = (f32[2048,16]{0,1:T(8,128)S(1)}, f32[2048,16]{0,1:T(8,128)}, u32[]{:S(2)}) copy-start(f32[2048,16]{0,1:T(8,128)} %param.8) | copy-start | bytes 393220
  5.9 15.8 %copy-start.6 = (f32[2048]{0:T(1024)S(1)}, f32[2048]{0:T(1024)}, u32[]{:S(2)}) copy-start(f32[2048]{0:T(1024)} %param.9) | copy-start | bytes 24580
  11.0 1.3 %copy-start = (f32[2,16,16,8,128]{4,3,2,1,0:T(8,128)}, f32[2,16,16,8,128]{4,3,2,1,0:T(8,128)S(1)}, u32[]{:S(2)}) copy-start(f32[2,16,16,8,128]{4,3,2,1,0:T(8,128)S(1)} %get-tuple-element.16.states_ref) | copy-start | bytes 6291460
  12.4 1.3 %copy-start.1 = (f32[2,256,8,128]{3,2,1,0:T(8,128)}, f32[2,256,8,128]{3,2,1,0:T(8,128)S(1)}, u32[]{:S(2)}) copy-start(f32[2,256,8,128]{3,2,1,0:T(8,128)S(1)} %get-tuple-element.13.kv_ref) | copy-start | bytes 6291460
  13.9 5.0 %collective-permute-start.1 = (f32[2,16,8,128]{3,2,1,0:T(8,128)S(1)}, f32[2,16,8,128]{3,2,1,0:T(8,128)S(1)}, u32[]{:S(2)}, u32[]{:S(2)}) collective-permute-start(f32[2,16,8,128]{3,2,1,0:T(8,128)S(1)} %multiply_add_fusion.1), channel_id=1, source_target_pairs={{0,4},{4,0},{8,12},{12,8},{1,5},{5,1},{9,13},{13,9},{2,6},{6,2},{1... | collective-permute-start | bytes 393224 | tf_op jit(solution)/shard_map/ppermute | solution.py:240
  19.0 7.6 %collective-permute-start.2 = (f32[2,16,8,128]{3,2,1,0:T(8,128)S(1)}, f32[2,16,8,128]{3,2,1,0:T(8,128)S(1)}, u32[]{:S(2)}, u32[]{:S(2)}) collective-permute-start(f32[2,16,8,128]{3,2,1,0:T(8,128)S(1)} %multiply_add_fusion), channel_id=1, source_target_pairs={{0,8},{4,12},{8,0},{12,4},{1,9},{5,13},{9,1},{13,5},{2,10},{6,14},... | collective-permute-start | bytes 393224 | tf_op jit(solution)/shard_map/ppermute | solution.py:240

commit v2 on v0

v2 whole, which is shorter than its diff:
```python
import functools

import jax
import jax.numpy as jnp
from jax import lax
from jax.experimental import pallas as pl
from jax.experimental.pallas import tpu as pltpu
from jax.sharding import PartitionSpec as P

F32 = jnp.float32
BF16 = jnp.bfloat16
LANES = 128
SUB = 8
GROUP = LANES * SUB
CHUNK = 16
PIECE = 64
STRIDE = CHUNK + 8
HEAD = 4
TAIL = 6


def total(values):
    values = list(values)
    while len(values) > 1:
        pairs = [values[i] + values[i + 1] for i in range(0, len(values) - 1, 2)]
        values = pairs + ([values[-1]] if len(values) % 2 else [])
    return values[0]


def column(g, j):
    return pl.ds(pl.multiple_of(g * GROUP + j * LANES, LANES), LANES)


def group_columns(g):
    return pl.ds(pl.multiple_of(g * GROUP, GROUP), GROUP)


def turn_in(source, turned, start, g):
    for j in range(SUB):
        turned[pl.ds(j * STRIDE, CHUNK), :] = source[pl.ds(start, CHUNK), column(g, j)].astype(F32)


def turn_rows(source, turned, rows, g):
    for j in range(SUB):
        turned[pl.ds(j * STRIDE, rows), :] = source[:, column(g, j)]


def row(turned, i):
    return turned[pl.ds(i, SUB, stride=STRIDE), :]


def state_kernel(
    streams, taps_hbm, rate_hbm, residue_hbm, bias_hbm,
    kv_ref, states_ref, own_ref, message_ref, tables_ref, q_ref,
    k_buf, v_buf, taps_buf, rate_buf, residue_buf, bias_buf, ka, kb, va, vb, table_sems, stream_sems, q_sem,
):
    tokens, modes = k_buf.shape[0], rate_buf.shape[0]
    groups = k_buf.shape[1] // GROUP
    pieces, chunks = tokens // PIECE, tokens // CHUNK

    def fetch(stream, g, n):
        rows = pl.ds(pl.multiple_of(n * PIECE, PIECE), PIECE)
        return pltpu.make_async_copy(
            streams.at[stream, rows, group_columns(g)],
            (k_buf, v_buf)[stream - 1].at[rows, group_columns(g)],
            stream_sems.at[stream - 1, g, n],
        )

    tables = [
        pltpu.make_async_copy(src, dst, table_sems.at[i])
        for i, (src, dst) in enumerate(
            [(rate_hbm, rate_buf), (taps_hbm, taps_buf), (residue_hbm, residue_buf), (bias_hbm, bias_buf)]
        )
    ]
    for copy in tables[:2]:
        copy.start()
    for g in range(groups):
        for n in range(pieces):
            fetch(1, g, n).start()
            fetch(2, g, n).start()
    fetch_q = pltpu.make_async_copy(streams.at[0], q_ref, q_sem)
    fetch_q.start()
    for copy in tables[2:]:
        copy.start()
    tables[0].wait()
    tables[1].wait()
    zero = jnp.zeros((SUB, LANES), F32)

    def one_group(g, none):
        turn_rows(rate_buf, ka, modes, g)
        for stream in range(3):
            turn_rows(taps_buf.at[stream], (kb, va, vb)[stream], 3, g)
        p = []
        for m in range(modes):
            rate = row(ka, m)
            tables_ref[g, m] = rate
            p.append(jnp.exp(-rate))
        w = []
        for i in range(9):
            w.append(row((kb, va, vb)[i // 3], i % 3))
            tables_ref[g, modes + i] = w[i]
        wk, wv = w[3:6], w[6:9]
        fetch(1, g, 0).wait()
        fetch(2, g, 0).wait()
        turn_in(k_buf, ka, 0, g)
        turn_in(v_buf, va, 0, g)
        for i in range(2):
            own_ref[g, modes + 2 * i] = row(ka, i)
            own_ref[g, modes + 2 * i + 1] = row(va, i)

        def one_chunk(c, ks, vs, acc, last):
            k1, k2, v1, v2 = last
            for m in range(modes):
                states_ref[g, c, m] = acc[m]
            for i in range(CHUNK):
                k, v = row(ks, i), row(vs, i)
                key = wk[0] * k + wk[1] * k1 + wk[2] * k2
                value = wv[0] * v + wv[1] * v1 + wv[2] * v2
                k1, k2, v1, v2 = k, k1, v, v1
                product = (key * value).astype(BF16).astype(F32)
                if i < 2:
                    product = jnp.where(c > 0, product, 0.0)
                kv_ref[g, c * CHUNK + i] = product
                acc = [a * b + product for a, b in zip(acc, p)]
            return acc, (k1, k2, v1, v2)

        def two_chunks(it, carry):
            acc, last = carry

            @pl.when(((it & 1) == 1) & (it < chunks // 2 - 1))
            def _():
                n = (it + 1) * 2 * CHUNK // PIECE
                fetch(1, g, n).wait()
                fetch(2, g, n).wait()

            c = 2 * it
            here = pl.multiple_of((c + 1) * CHUNK, CHUNK)
            turn_in(k_buf, kb, here, g)
            turn_in(v_buf, vb, here, g)
            acc, last = one_chunk(c, ka, va, acc, last)
            ahead = pl.multiple_of(jnp.minimum(c + 2, chunks - 1) * CHUNK, CHUNK)
            turn_in(k_buf, ka, ahead, g)
            turn_in(v_buf, va, ahead, g)
            return one_chunk(c + 1, kb, vb, acc, last)

        acc, last = lax.fori_loop(0, chunks // 2, two_chunks, ([zero] * modes, (zero,) * 4))
        for m in range(modes):
            own_ref[g, m] = acc[m]
        k1, k2, v1, v2 = last
        for i, value in ((1, k2), (2, v2), (4, k1), (5, v1)):
            own_ref[g, modes + HEAD + i] = value
        return none

    lax.fori_loop(0, groups, one_group, 0)
    fetch_q.wait()
    tables[2].wait()
    tables[3].wait()

    def rest(g, none):
        turn_rows(residue_buf, ka, modes, g)
        for m in range(modes):
            tables_ref[g, modes + 9 + m] = row(ka, m)
        tables_ref[g, 2 * modes + 9] = bias_buf[g]
        turn_in(q_ref, va, tokens - CHUNK, g)
        for i in range(2):
            own_ref[g, modes + HEAD + 3 * i] = row(va, CHUNK - 2 + i)
        pack(message_ref, g, [own_ref[g, i] for i in range(modes + HEAD + TAIL)])
        return none

    lax.fori_loop(0, groups, rest, 0)


def pack(message_ref, g, rows):
    for i in range(0, len(rows), 2):
        message_ref[g, i // 2] = jnp.concatenate(rows[i : i + 2], axis=0).astype(BF16)


def unpack(message_ref, g, first, count):
    rows = []
    for i in range(first // 2, (first + count) // 2):
        pair = message_ref[g, i].astype(F32)
        rows += [pair[:SUB], pair[SUB:]]
    return rows


def first_products(w, head, tail):
    features = []
    for s, rows in ((1, (tail[1], tail[4], head[0], head[2])), (2, (tail[2], tail[5], head[1], head[3]))):
        features.append([w[3 * s] * rows[2 + t] + w[3 * s + 1] * rows[1 + t] + w[3 * s + 2] * rows[t] for t in range(2)])
    return [(features[0][t] * features[1][t]).astype(BF16).astype(F32) for t in range(2)]


def first_terms(rate, products, steps):
    return jnp.exp((1.0 - steps) * rate) * products[0] + jnp.exp((2.0 - steps) * rate) * products[1]


def enter(tokens, span, rank, tables_ref, g, state, head, other, other_head, other_tail, entering):
    modes = len(other)
    rate = [tables_ref[g, m] for m in range(modes)]
    w = [tables_ref[g, modes + i] for i in range(9)]
    right = (rank & span) != 0
    ahead = rank & (span - 1)
    steps = (tokens * ahead).astype(F32)
    products = first_products(w, head, other_tail)
    result = []
    for m in range(modes):
        missing = jnp.where(ahead > 0, first_terms(rate[m], products, jnp.maximum(steps, 2.0)), 0.0)
        result.append(jnp.where(right, entering[m] + jnp.exp(-steps * rate[m]) * other[m] + missing, entering[m]))
    return result


def merge_kernel(span, tokens, own_ref, got_ref, tables_ref, entering_ref, rim_ref, *outs):
    next_ref, message_ref, entering_out, rim_out = outs
    groups = tables_ref.shape[0]
    modes = (tables_ref.shape[1] - 10) // 2
    rank = lax.axis_index("context")
    right = (rank & span) != 0
    ahead = rank & (span - 1)
    length = 1.0 * tokens * span
    zero = jnp.zeros((SUB, LANES), F32)

    def one_group(g, none):
        rate = [tables_ref[g, m] for m in range(modes)]
        w = [tables_ref[g, modes + i] for i in range(9)]
        state = [own_ref[g, m] for m in range(modes)]
        head = [own_ref[g, modes + i] for i in range(HEAD)]
        tail = [own_ref[g, modes + HEAD + i] for i in range(TAIL)]
        other = unpack(got_ref, g, 0, modes)
        other_head = unpack(got_ref, g, modes, HEAD)
        other_tail = unpack(got_ref, g, modes + HEAD, TAIL)

        def pick(a, b):
            return [jnp.where(right, x, y) for x, y in zip(a, b)]

        left_state, right_state = pick(other, state), pick(state, other)
        left_head, right_head = pick(other_head, head), pick(head, other_head)
        left_tail, right_tail = pick(other_tail, tail), pick(tail, other_tail)
        if span == 1:
            products = first_products(w, left_head, [zero] * TAIL)
            left_state = [
                a + jnp.where(rank < 2, first_terms(rate[m], products, length), 0.0) for m, a in enumerate(left_state)
            ]
        entering = [zero] * modes if entering_ref is None else [entering_ref[g, m] for m in range(modes)]
        entering = enter(tokens, span, rank, tables_ref, g, state, head, left_state, None, other_tail, entering)
        products = first_products(w, right_head, left_tail)
        rows = [
            right_state[m] + jnp.exp(-length * rate[m]) * left_state[m] + first_terms(rate[m], products, length)
            for m in range(modes)
        ]
        rows = rows + left_head + right_tail
        pack(message_ref, g, rows)
        for i, value in enumerate(rows):
            next_ref[g, i] = value
        for m in range(modes):
            entering_out[g, m] = entering[m]
        for i in range(TAIL):
            old = zero if rim_ref is None else rim_ref[g, i]
            rim_out[g, i] = jnp.where(right & (ahead == 0), other_tail[i], old)
        return none

    lax.fori_loop(0, groups, one_group, 0)


def near_kernel(q_ref, tables_ref, kv_ref, near_ref, query_ref, taps, qa, qb):
    tokens, groups = kv_ref.shape[1], kv_ref.shape[0]
    modes = (tables_ref.shape[1] - 10) // 2
    chunks = tokens // CHUNK
    zero = jnp.zeros((SUB, LANES), F32)

    def one_group(g, none):
        p = [jnp.exp(-tables_ref[g, m]) for m in range(modes)]
        gain = [tables_ref[g, modes + 9 + m] for m in range(modes)]
        taps[0] = total(gain) + tables_ref[g, 2 * modes + 9]
        for i in range(1, CHUNK):
            gain = [a * b for a, b in zip(gain, p)]
            taps[i] = total(gain)
        w = [tables_ref[g, modes + i] for i in range(3)]
        h = [taps[i] for i in range(CHUNK)]
        turn_in(q_ref, qa, 0, g)

        def one_chunk(c, qs, last):
            q1, q2 = last
            window = []
            for i in range(CHUNK):
                t = c * CHUNK + i
                q = row(qs, i)
                query_ref[g, t] = w[0] * q + w[1] * q1 + w[2] * q2
                q1, q2 = q, q1
                window.append(kv_ref[g, t])
                near_ref[g, t] = total(h[n] * window[i - n] for n in range(i + 1))
            return q1, q2

        def two_chunks(it, last):
            c = 2 * it
            turn_in(q_ref, qb, pl.multiple_of((c + 1) * CHUNK, CHUNK), g)
            last = one_chunk(c, qa, last)
            turn_in(q_ref, qa, pl.multiple_of(jnp.minimum(c + 2, chunks - 1) * CHUNK, CHUNK), g)
            return one_chunk(c + 1, qb, last)

        lax.fori_loop(0, chunks // 2, two_chunks, (zero, zero))
        return none

    lax.fori_loop(0, groups, one_group, 0)


def emit_kernel(
    span, near_ref, query_ref, states_ref, tables_ref, own_ref, merged_ref, got_ref, entering_ref, old_rim_ref,
    out_hbm, out_buf, power, state, rim_ref, ta, tb, out_sems,
):
    groups, tokens = near_ref.shape[:2]
    modes = (tables_ref.shape[1] - 10) // 2
    pieces, chunks = tokens // PIECE, tokens // CHUNK
    rank = lax.axis_index("context")

    def send(g, n):
        rows = pl.ds(pl.multiple_of(n * PIECE, PIECE), PIECE)
        return pltpu.make_async_copy(
            out_buf.at[rows, group_columns(g)], out_hbm.at[rows, group_columns(g)], out_sems.at[g, n]
        )

    def one_group(g, none):
        p = []
        for m in range(modes):
            rate = tables_ref[g, m]
            p.append(jnp.exp(-rate))
            power[m] = jnp.exp(-CHUNK * rate)
        w = [tables_ref[g, modes + i] for i in range(9)]
        other_tail = unpack(got_ref, g, modes + HEAD, TAIL)
        entering = enter(
            tokens, span, rank, tables_ref, g, None, [merged_ref[g, modes + i] for i in range(HEAD)],
            unpack(got_ref, g, 0, modes), None, other_tail, [entering_ref[g, m] for m in range(modes)],
        )
        for m in range(modes):
            state[m] = entering[m]
        begins = ((rank & span) != 0) & ((rank & (span - 1)) == 0)
        rim = [jnp.where(begins, other_tail[i], old_rim_ref[g, i]) for i in range(TAIL)]
        products = first_products(w, [own_ref[g, modes + i] for i in range(HEAD)], rim)
        rim_ref[0], rim_ref[1] = products
        rim_ref[2] = w[1] * rim[3] + w[2] * rim[0]
        rim_ref[3] = w[2] * rim[3]

        def one_chunk(c, turned, first):
            gains = [tables_ref[g, modes + 9 + m] for m in range(modes)]
            x = [gain * (states_ref[g, c, m] + state[m]) for m, gain in enumerate(gains)]
            for i in range(CHUNK):
                t = c * CHUNK + i
                x = [a * b for a, b in zip(x, p)]
                near, query = near_ref[g, t], query_ref[g, t]
                if first and i < 2:
                    x = [a + tables_ref[g, modes + 9 + m] * rim_ref[i] for m, a in enumerate(x)]
                    near = near + tables_ref[g, 2 * modes + 9] * rim_ref[i]
                    query = query + rim_ref[2 + i]
                mixed = (near + total(x)).astype(BF16).astype(F32)
                turned[pl.ds(i, SUB, stride=STRIDE), :] = query * mixed
            for m in range(modes):
                if first:
                    held = (state[m] * p[m] + rim_ref[0]) * p[m] + rim_ref[1]
                    state[m] = held * jnp.exp(-(CHUNK - 2) * tables_ref[g, m])
                else:
                    state[m] = state[m] * power[m]

        def turn_out(turned, c):
            rows = pl.ds(pl.multiple_of(c * CHUNK, CHUNK), CHUNK)
            for j in range(SUB):
                out_buf[rows, column(g, j)] = turned[pl.ds(j * STRIDE, CHUNK), :].astype(BF16)

        one_chunk(0, ta, True)
        one_chunk(1, tb, False)
        turn_out(ta, 0)

        def two_chunks(it, none):
            c = 2 * it
            one_chunk(c, ta, False)
            turn_out(tb, c - 1)
            one_chunk(c + 1, tb, False)
            turn_out(ta, c)

            @pl.when((it & 1) == 0)
            def _():
                send(g, it * 2 * CHUNK // PIECE - 1).start()

            return none

        lax.fori_loop(1, chunks // 2, two_chunks, 0)
        turn_out(tb, chunks - 1)
        send(g, pieces - 1).start()
        return none

    lax.fori_loop(0, groups, one_group, 0)
    for g in range(groups):
        for n in range(pieces):
            send(g, n).wait()


VM = pl.BlockSpec(memory_space=pltpu.VMEM)
HB = pl.BlockSpec(memory_space=pltpu.HBM)


def in_vmem(x):
    return pltpu.with_memory_space_constraint(x, pltpu.VMEM)


def in_hbm(x):
    return pltpu.with_memory_space_constraint(x, pltpu.HBM)


def params(mib):
    return pltpu.CompilerParams(vmem_limit_bytes=mib * 2**20)


def cost(flops, nbytes):
    return pl.CostEstimate(flops=flops, bytes_accessed=nbytes, transcendentals=0)


def body(streams, short_filter, decay_rate, residue, bias):
    tokens, _, channels = streams.shape
    modes = decay_rate.shape[1]
    groups = channels // GROUP
    chunks, pieces = tokens // CHUNK, tokens // PIECE
    size = lax.axis_size("context")
    rank = lax.axis_index("context")
    turned = pltpu.VMEM((SUB * STRIDE, LANES), F32)
    vector = (SUB, LANES)
    kv_shape = (groups, tokens) + vector
    table_rows = 2 * modes + 10
    dma = pltpu.SemaphoreType.DMA

    message_rows = modes + HEAD + TAIL
    own_shape, message_shape = (groups, message_rows) + vector, (groups, message_rows // 2, 2 * SUB, LANES)
    mode_shape, rim_shape = (groups, modes) + vector, (groups, TAIL) + vector
    key_value, states, own, message, tables, q = pl.pallas_call(
        state_kernel,
        in_specs=[HB] * 5,
        out_specs=[VM] * 6,
        out_shape=[
            pltpu.VMEM(kv_shape, F32),
            pltpu.VMEM((groups, chunks, modes) + vector, F32),
            pltpu.VMEM(own_shape, F32),
            pltpu.VMEM(message_shape, BF16),
            pltpu.VMEM((groups, table_rows) + vector, F32),
            pltpu.VMEM((tokens, channels), BF16),
        ],
        scratch_shapes=[
            pltpu.VMEM((tokens, channels), BF16),
            pltpu.VMEM((tokens, channels), BF16),
            pltpu.VMEM((3, 3, channels), F32),
            pltpu.VMEM((modes, channels), F32),
            pltpu.VMEM((modes, channels), F32),
            pltpu.VMEM((groups,) + vector, F32),
            turned, turned, turned, turned,
            dma((4,)), dma((2, groups, pieces)), dma(()),
        ],
        compiler_params=params(8),
        cost_estimate=cost(48 * tokens * channels, 6 * 2**20),
        name="states",
    )(
        in_hbm(streams.transpose(1, 0, 2)), in_hbm(short_filter), in_hbm(decay_rate.T), in_hbm(residue.T),
        in_hbm(bias.reshape((groups,) + vector)),
    )

    merged, entering, rim, near = own, None, None, None
    span = 1
    while span < size:
        got = lax.ppermute(message, "context", [(i, i ^ span) for i in range(size)])
        if near is None:
            near, query = pl.pallas_call(
                near_kernel,
                in_specs=[VM] * 3,
                out_specs=[VM] * 2,
                out_shape=[pltpu.VMEM(kv_shape, F32)] * 2,
                scratch_shapes=[pltpu.VMEM((CHUNK,) + vector, F32), turned, turned],
                compiler_params=params(4),
                cost_estimate=cost(24 * tokens * channels, 7 * 2**20),
                name="near",
            )(in_vmem(q), in_vmem(tables), in_vmem(key_value))
        if 2 * span >= size:
            break
        operands = [merged, got, tables] + ([] if entering is None else [entering, rim])

        def merge(*refs, span=span, first=entering is None):
            refs = refs[:3] + (None, None) + refs[3:] if first else refs
            merge_kernel(span, tokens, *refs)

        merged, message, entering, rim = pl.pallas_call(
            merge,
            in_specs=[VM] * len(operands),
            out_specs=[VM] * 4,
            out_shape=[
                pltpu.VMEM(own_shape, F32), pltpu.VMEM(message_shape, BF16), pltpu.VMEM(mode_shape, F32),
                pltpu.VMEM(rim_shape, F32),
            ],
            compiler_params=params(4),
            cost_estimate=cost(2**20, 2**20),
            name="merge",
        )(*[in_vmem(x) for x in operands])
        span *= 2

    return pl.pallas_call(
        functools.partial(emit_kernel, span),
        in_specs=[VM] * 9,
        out_specs=HB,
        out_shape=pltpu.HBM((tokens, channels), BF16),
        scratch_shapes=[
            pltpu.VMEM((tokens, channels), BF16),
            pltpu.VMEM((modes,) + vector, F32),
            pltpu.VMEM((modes,) + vector, F32),
            pltpu.VMEM((4,) + vector, F32),
            turned, turned, dma((groups, pieces)),
        ],
        compiler_params=params(4),
        cost_estimate=cost(40 * tokens * channels, 7 * 2**20),
        name="emit",
    )(*[in_vmem(x) for x in (near, query, states, tables, own, merged, got, entering, rim)])


def solution(mesh):
    in_specs = (
        P(("dp", "context"), None, "tensor"),
        P(None, None, "tensor"),
        P("tensor", None),
        P("tensor", None),
        P("tensor"),
    )
    out_specs = P(("dp", "context"), "tensor")
    return jax.shard_map(body, mesh=mesh, in_specs=in_specs, out_specs=out_specs, check_vma=False)
```

time: 571 us -> 23.5 us (0.04)
  local copies, waits for them, and re-layouts: 410 us -> 0 us
  matrix products: 92.3 us -> 0 us
  other arithmetic: 27 us -> 0 us
  waiting for transfers between devices: 24.6 us -> 5.65 us
  Pallas kernels: 0 us -> 11.8 us
  starting transfers between devices: 14.4 us -> 5.91 us
    gather x2 -> x0, local copies, waits for them, and re-layouts: 388 us -> none  [block_terms(): jnp.take(filter_taps, jnp.maximum(lag_table, 0), axis=1)]
    dot_general x3 -> x0, matrix products: 92.3 us -> none  [the longest x1 77.4 us: block_terms(): within = jnp.einsum('cab,cnb->cna', toeplitz, signal, precision=HIGH)]
    all_to_all x2 -> x0, waiting for transfers between devices: 24.6 us -> none  [the longest x1 24.5 us: body(): lax.all_to_all(mixed, 'context', split_axis=0, concat_axis=1, tiled=True)]
    convert_element_type x6 -> x0, other arithmetic: 14.7 us -> none  [the longest x1 4.94 us: body(): product_rows = (key_feat * value_feat).astype(jnp.bfloat16)]
    pallas_call x0 -> x4, Pallas kernels: none -> 11.8 us  [the longest x1 5.85 us: body(): pl.pallas_call(state_kernel, in_specs=[HB] * 5, out_specs=[VM] * 6, out_s...]
    reduce_sum x1 -> x0, other arithmetic: 11.1 us -> none  [block_terms(): jnp.sum(residue[:, None, :] * jnp.exp(positions[None, :, None] * log_pole...]
    all_to_all x2 -> x0, starting transfers between devices: 9.3 us -> none  [the longest x1 4.86 us: body(): lax.all_to_all(mixed, 'context', split_axis=0, concat_axis=1, tiled=True)]
  transfers between devices with their start and end apart: 3 -> 2, of which waited for: 1 -> 2; matrix products, arithmetic and copies ran while one was open for 72% -> 0% of each run, Pallas kernels for 0% -> 8%
where the time goes in v2:
time: 23.5 us; the launch traced here: 23.4 us
  Pallas kernels  11.8 us (50%)
  starting transfers between devices  5.91 us (25%)
  waiting for transfers between devices  5.65 us (24%)
    ppermute x2, starting transfers between devices, body(): got = lax.ppermute(message, 'context', [(i, i ^ span) for i in range(size)])  5.91 us
    pallas_call x1, Pallas kernels, body(): pl.pallas_call(state_kernel, in_specs=[HB] * 5, out_specs=[VM] * 6, out_s...  5.85 us
    ppermute x2, waiting for transfers between devices, body(): got = lax.ppermute(message, 'context', [(i, i ^ span) for i in range(size)])  5.65 us
    pallas_call x1, Pallas kernels, body(): pl.pallas_call(functools.partial(emit_kernel, span), in_specs=[VM] * 9, o...  3.88 us
    pallas_call x1, Pallas kernels, body(): pl.pallas_call(near_kernel, in_specs=[VM] * 3, out_specs=[VM] * 2, out_sh...  1.89 us
  transfers between devices with their start and end apart: 2, of which 2 were waited for; matrix products, arithmetic and copies ran while one was open for 0% of the time, Pallas kernels for 8%

profile of v2, /device:TPU:0, one launch (start us, length us, event | category | flops | bytes accessed | tf_op | source)
XLA Modules:
  0.0 23.4 jit_solution(2648735495832366980)
XLA Ops:
  0.0 5.9 %states.1 = (f32[2,256,8,128]{3,2,1,0:T(8,128)S(1)}, f32[2,16,16,8,128]{4,3,2,1,0:T(8,128)S(1)}, f32[2,26,8,128]{3,2,1,0:T(8,128)S(1)}, bf16[2,13,16,128]{3,2,1,...) custom-call(bf16[3,256,2048]{2,1,0:T(8,128)(2,1)} %bitcast.4, f32[3,3,2048]{2,1,0:T(4,128)} %taps_hbm.1, ...), custom_call_target="tpu_custom_call" | custom-call | flops 25165824 | bytes 6291456 | tf_op jit(solution)/shard_map/states/pallas_call | solution.py:431
  5.9 3.1 %collective-permute-start = (bf16[2,13,16,128]{3,2,1,0:T(8,128)(2,1)S(1)}, bf16[2,13,16,128]{3,2,1,0:T(8,128)(2,1)S(1)}, u32[]{:S(2)}, u32[]{:S(2)}) collective-permute-start(bf16[2,13,16,128]{3,2,1,0:T(8,128)(2,1)S(1)} %get-tuple-element.24), channel_id=1, source_target_pairs={{0,4},{4,0},{8,12},{12,8},{1,5},{5,1},{9,13},{13,9},{2,6},{6,2},{1... | collective-permute-start | bytes 319496 | tf_op jit(solution)/shard_map/ppermute | solution.py:464
  8.9 3.0 %collective-permute-done.refs_1_ = bf16[2,13,16,128]{3,2,1,0:T(8,128)(2,1)S(1)} collective-permute-done((bf16[2,13,16,128]{3,2,1,0:T(8,128)(2,1)S(1)}, bf16[2,13,16,128]{3,2,1,0:T(8,128)(2,1)S(1)}, u32[]{:S(2)}, u32[]{:S(2)}) %collective-permute-start) | collective-permute-done | bytes 106528 | tf_op jit(solution)/shard_map/ppermute | solution.py:464
  11.9 0.2 merge.1
  12.1 2.8 %collective-permute-start.1 = (bf16[2,13,16,128]{3,2,1,0:T(8,128)(2,1)S(1)}, bf16[2,13,16,128]{3,2,1,0:T(8,128)(2,1)S(1)}, u32[]{:S(2)}, u32[]{:S(2)}) collective-permute-start(bf16[2,13,16,128]{3,2,1,0:T(8,128)(2,1)S(1)} %get-tuple-element.26), channel_id=1, source_target_pairs={{0,8},{4,12},{8,0},{12,4},{1,9},{5,13},{9,1},{13,5},{2,10},{6,14},... | collective-permute-start | bytes 319496 | tf_op jit(solution)/shard_map/ppermute | solution.py:464
  14.9 1.9 %near.1 = (f32[2,256,8,128]{3,2,1,0:T(8,128)S(1)}, f32[2,256,8,128]{3,2,1,0:T(8,128)S(1)}) custom-call(bf16[256,2048]{1,0:T(8,128)(2,1)S(1)} %get-tuple-element.17.q_ref, f32[2,42,8,128]{3,2,1,0:T(8,128)S(1)} %get-tuple-element.18.tables_ref.refs_2_, f32[2,256,8,128]{3,2,1,0:T(8,128)S(1)} %get-tuple-element.19.kv_ref), custom_call_target="tpu_custom_call" | custom-call | flops 12582912 | bytes 7340032 | tf_op jit(solution)/shard_map/near/pallas_call | solution.py:466
  16.8 2.7 %collective-permute-done.1.got_ref = bf16[2,13,16,128]{3,2,1,0:T(8,128)(2,1)S(1)} collective-permute-done((bf16[2,13,16,128]{3,2,1,0:T(8,128)(2,1)S(1)}, bf16[2,13,16,128]{3,2,1,0:T(8,128)(2,1)S(1)}, u32[]{:S(2)}, u32[]{:S(2)}) %collective-permute-start.1) | collective-permute-done | bytes 106528 | tf_op jit(solution)/shard_map/ppermute | solution.py:464
  19.5 3.9 %emit.1 = bf16[256,2048]{1,0:T(8,128)(2,1)} custom-call(f32[2,256,8,128]{3,2,1,0:T(8,128)S(1)} %get-tuple-element.20.near_ref, f32[2,256,8,128]{3,2,1,0:T(8,128)S(1)} %get-tuple-element.21.query_ref, f32[2,16,16,8,128]{4,3,2,1,0:T(8,128)S(1)} %get-tuple-element.22.states_ref, f32[2,42,8,128]{3,2,1,0:T(8,128)S(1)} %get-tuple-element.18.tables_ref.refs_2_, ...), custom_call_target="tpu_custom_call" | custom-call | flops 20971520 | bytes 7340032 | tf_op jit(solution)/shard_map/emit/pallas_call | solution.py:498
Async XLA Ops:
  5.9 6.1 %collective-permute-start = (bf16[2,13,16,128]{3,2,1,0:T(8,128)(2,1)S(1)}, bf16[2,13,16,128]{3,2,1,0:T(8,128)(2,1)S(1)}, u32[]{:S(2)}, u32[]{:S(2)}) collective-permute-start(bf16[2,13,16,128]{3,2,1,0:T(8,128)(2,1)S(1)} %get-tuple-element.24), channel_id=1, source_target_pairs={{0,4},{4,0},{8,12},{12,8},{1,5},{5,1},{9,13},{13,9},{2,6},{6,2},{1... | collective-permute-start | bytes 319496 | tf_op jit(solution)/shard_map/ppermute | solution.py:464
  12.1 7.4 %collective-permute-start.1 = (bf16[2,13,16,128]{3,2,1,0:T(8,128)(2,1)S(1)}, bf16[2,13,16,128]{3,2,1,0:T(8,128)(2,1)S(1)}, u32[]{:S(2)}, u32[]{:S(2)}) collective-permute-start(bf16[2,13,16,128]{3,2,1,0:T(8,128)(2,1)S(1)} %get-tuple-element.26), channel_id=1, source_target_pairs={{0,8},{4,12},{8,0},{12,4},{1,9},{5,13},{9,1},{13,5},{2,10},{6,14},... | collective-permute-start | bytes 319496 | tf_op jit(solution)/shard_map/ppermute | solution.py:464

commit v3 on v0

v3 whole, which is shorter than its diff:
```python
import jax
import jax.numpy as jnp
from jax import lax
from jax.experimental import pallas as pl
from jax.experimental.pallas import tpu as pltpu
from jax.sharding import PartitionSpec as P

F32 = jnp.float32
BF16 = jnp.bfloat16
LANES = 128
SUB = 8
GROUP = LANES * SUB
CHUNK = 16
PIECE = 64
STRIDE = CHUNK + 8
HEAD = 4
TAIL = 6


def total(values):
    values = list(values)
    while len(values) > 1:
        pairs = [values[i] + values[i + 1] for i in range(0, len(values) - 1, 2)]
        values = pairs + ([values[-1]] if len(values) % 2 else [])
    return values[0]


def columns(g):
    return pl.ds(g * GROUP, GROUP)


def turn_in(source, turned, start, g):
    for j in range(SUB):
        turned[pl.ds(j * STRIDE, CHUNK), :] = source[pl.ds(start, CHUNK), pl.ds(g * GROUP + j * LANES, LANES)].astype(F32)


def turn_rows(source, turned, rows, g):
    for j in range(SUB):
        turned[pl.ds(j * STRIDE, rows), :] = source[:, pl.ds(g * GROUP + j * LANES, LANES)]


def row(turned, i):
    return turned[pl.ds(i, SUB, stride=STRIDE), :]


def chunk_rows(c):
    return pl.multiple_of(c * CHUNK, CHUNK)


def pack(message_ref, rows):
    for i in range(message_ref.shape[0]):
        message_ref[i] = jnp.concatenate(rows[2 * i : 2 * i + 2], axis=0).astype(BF16)


def unpack(message_ref, first, count):
    rows = []
    for i in range(first // 2, (first + count) // 2):
        pair = message_ref[i].astype(F32)
        rows += [pair[:SUB], pair[SUB:]]
    return rows


def first_products(w, head, tail):
    features = []
    for s, rows in ((1, (tail[1], tail[4], head[0], head[2])), (2, (tail[2], tail[5], head[1], head[3]))):
        features.append([w[3 * s] * rows[2 + t] + w[3 * s + 1] * rows[1 + t] + w[3 * s + 2] * rows[t] for t in range(2)])
    return [(features[0][t] * features[1][t]).astype(BF16).astype(F32) for t in range(2)]


def first_terms(rate, products, steps):
    return jnp.exp((1.0 - steps) * rate) * products[0] + jnp.exp((2.0 - steps) * rate) * products[1]


def enter(tokens, span, rank, rate, w, head, other, other_tail, entering):
    right = (rank & span) != 0
    ahead = rank & (span - 1)
    steps = (tokens * ahead).astype(F32)
    products = first_products(w, head, other_tail)
    result = []
    for m, r in enumerate(rate):
        missing = jnp.where(ahead > 0, first_terms(r, products, jnp.maximum(steps, 2.0)), 0.0)
        result.append(jnp.where(right, entering[m] + jnp.exp(-steps * r) * other[m] + missing, entering[m]))
    return result


def table_parts(tables_ref):
    modes = (tables_ref.shape[0] - 10) // 2
    rate = [tables_ref[m] for m in range(modes)]
    return modes, rate, [tables_ref[modes + i] for i in range(9)]


def gain_row(modes, m):
    return modes + 9 + m


def state_kernel(
    g, rate_nat, taps_nat, residue_nat, bias_nat, natural,
    kv_ref, states_ref, own_ref, message_ref, tables_ref, ka, kb, va, vb, wait_piece, wait_rest,
):
    q_nat, k_nat, v_nat = (natural.at[i] for i in range(3))
    tokens, modes = natural.shape[1], rate_nat.shape[0]
    chunks = tokens // CHUNK
    rank = lax.axis_index("context")
    zero = jnp.zeros((SUB, LANES), F32)
    turn_rows(rate_nat, ka, modes, g)
    for stream in range(3):
        turn_rows(taps_nat.at[stream], (kb, va, vb)[stream], 3, g)
    p = []
    for m in range(modes):
        rate = row(ka, m)
        tables_ref[m] = rate
        p.append(jnp.exp(-rate))
    w = []
    for i in range(9):
        w.append(row((kb, va, vb)[i // 3], i % 3))
        tables_ref[modes + i] = w[i]
    wk, wv = w[3:6], w[6:9]
    wait_piece(0)
    turn_in(k_nat, ka, 0, g)
    turn_in(v_nat, va, 0, g)
    for i in range(2):
        own_ref[modes + TAIL + 2 * i] = row(ka, i)
        own_ref[modes + TAIL + 2 * i + 1] = row(va, i)

    def one_chunk(c, ks, vs, acc, last):
        k1, k2, v1, v2 = last
        for m in range(modes):
            states_ref[c, m] = acc[m]
        for i in range(CHUNK):
            k, v = row(ks, i), row(vs, i)
            key = wk[0] * k + wk[1] * k1 + wk[2] * k2
            value = wv[0] * v + wv[1] * v1 + wv[2] * v2
            k1, k2, v1, v2 = k, k1, v, v1
            product = (key * value).astype(BF16).astype(F32)
            if i < 2:
                product = jnp.where((c > 0) | (rank == 0), product, 0.0)
            kv_ref[c * CHUNK + i] = product
            acc = [a * b + product for a, b in zip(acc, p)]
        return acc, (k1, k2, v1, v2)

    def two_chunks(it, carry):
        acc, last = carry
        c = 2 * it
        pl.when(it == PIECE // (2 * CHUNK) - 1)(lambda: wait_piece(1))
        turn_in(k_nat, kb, chunk_rows(c + 1), g)
        turn_in(v_nat, vb, chunk_rows(c + 1), g)
        acc, last = one_chunk(c, ka, va, acc, last)
        ahead = chunk_rows(jnp.minimum(c + 2, chunks - 1))
        turn_in(k_nat, ka, ahead, g)
        turn_in(v_nat, va, ahead, g)
        return one_chunk(c + 1, kb, vb, acc, last)

    acc, last = lax.fori_loop(0, chunks // 2, two_chunks, ([zero] * modes, (zero,) * 4))
    for m in range(modes):
        own_ref[m] = acc[m]
    k1, k2, v1, v2 = last
    for i, value in ((1, k2), (2, v2), (4, k1), (5, v1)):
        own_ref[modes + i] = value
    wait_rest()
    turn_rows(residue_nat, ka, modes, g)
    for m in range(modes):
        tables_ref[gain_row(modes, m)] = row(ka, m)
    tables_ref[gain_row(modes, modes)] = bias_nat[g]
    turn_in(q_nat, va, tokens - CHUNK, g)
    for i in range(2):
        own_ref[modes + 3 * i] = row(va, CHUNK - 2 + i)
    pack(message_ref, [own_ref[i] for i in range(modes + TAIL + HEAD)])


def first_states_kernel(
    streams, taps_hbm, rate_hbm, residue_hbm, bias_hbm,
    kv_ref, states_ref, own_ref, message_ref, tables_ref, rate_nat, taps_nat, residue_nat, bias_nat, natural,
    ka, kb, va, vb, table_sems, stream_sems,
):
    _, tokens, channels = natural.shape
    groups = channels // GROUP

    def fetch(i, *where):
        return pltpu.make_async_copy(streams.at[where], natural.at[where], stream_sems.at[i])

    keys_values = pl.ds(1, 2)
    pieces = [
        fetch(0, keys_values, pl.ds(0, PIECE), columns(0)),
        fetch(1, keys_values, pl.ds(PIECE, tokens - PIECE), columns(0)),
    ]
    rest = [fetch(2, pl.ds(0, 1), slice(None), columns(0))]
    rest += [fetch(2 + g, slice(None), slice(None), columns(g)) for g in range(1, groups)]
    tables = [
        pltpu.make_async_copy(src, dst, table_sems.at[i])
        for i, (src, dst) in enumerate(
            [(rate_hbm, rate_nat), (taps_hbm, taps_nat), (residue_hbm, residue_nat), (bias_hbm, bias_nat)]
        )
    ]
    for copy in tables[:2] + pieces + rest + tables[2:]:
        copy.start()
    for copy in tables[:2]:
        copy.wait()

    def wait_rest():
        for copy in tables[2:] + rest:
            copy.wait()

    state_kernel(
        0, rate_nat, taps_nat, residue_nat, bias_nat, natural,
        kv_ref, states_ref, own_ref, message_ref, tables_ref, ka, kb, va, vb, lambda n: pieces[n].wait(), wait_rest,
    )


def later_states_kernel(g, *refs):
    state_kernel(g, *refs, lambda n: None, lambda: None)


def near_group(g, q_nat, tables_ref, kv_ref, near_ref, query_ref, taps, qa, qb):
    tokens = kv_ref.shape[0]
    chunks = tokens // CHUNK
    zero = jnp.zeros((SUB, LANES), F32)
    modes, rate, w = table_parts(tables_ref)
    p = [jnp.exp(-r) for r in rate]
    gain = [tables_ref[gain_row(modes, m)] for m in range(modes)]
    taps[0] = total(gain) + tables_ref[gain_row(modes, modes)]
    for i in range(1, CHUNK):
        gain = [a * b for a, b in zip(gain, p)]
        taps[i] = total(gain)
    h = [taps[i] for i in range(CHUNK)]
    turn_in(q_nat, qa, 0, g)

    def one_chunk(c, qs, last):
        q1, q2 = last
        window = []
        for i in range(CHUNK):
            t = c * CHUNK + i
            q = row(qs, i)
            query_ref[t] = w[0] * q + w[1] * q1 + w[2] * q2
            q1, q2 = q, q1
            window.append(kv_ref[t])
            near_ref[t] = total(h[n] * window[i - n] for n in range(i + 1))
        return q1, q2

    def two_chunks(it, last):
        c = 2 * it
        turn_in(q_nat, qb, chunk_rows(c + 1), g)
        last = one_chunk(c, qa, last)
        turn_in(q_nat, qa, chunk_rows(jnp.minimum(c + 2, chunks - 1)), g)
        return one_chunk(c + 1, qb, last)

    lax.fori_loop(0, chunks // 2, two_chunks, (zero, zero))


def merge_group(span, tokens, own_ref, got_ref, tables_ref, entering_ref, rim_ref, next_ref, message_ref, entering_out, rim_out):
    modes, rate, w = table_parts(tables_ref)
    rank = lax.axis_index("context")
    right = (rank & span) != 0
    ahead = rank & (span - 1)
    length = 1.0 * tokens * span
    zero = jnp.zeros((SUB, LANES), F32)
    state = [own_ref[m] for m in range(modes)]
    tail = [own_ref[modes + i] for i in range(TAIL)]
    head = [own_ref[modes + TAIL + i] for i in range(HEAD)]
    other = unpack(got_ref, 0, modes)
    other_tail = unpack(got_ref, modes, TAIL)
    other_head = unpack(got_ref, modes + TAIL, HEAD)

    def pick(a, b):
        return [jnp.where(right, x, y) for x, y in zip(a, b)]

    left_state, right_state = pick(other, state), pick(state, other)
    left_head, right_head = pick(other_head, head), pick(head, other_head)
    left_tail, right_tail = pick(other_tail, tail), pick(tail, other_tail)
    products = first_products(w, right_head, left_tail)
    rows = [
        right_state[m] + jnp.exp(-length * rate[m]) * left_state[m] + first_terms(rate[m], products, length)
        for m in range(modes)
    ]
    rows = rows + right_tail + left_head
    pack(message_ref, rows)
    for i, value in enumerate(rows):
        next_ref[i] = value
    entering = [zero if entering_ref is None else entering_ref[m] for m in range(modes)]
    entering = enter(tokens, span, rank, rate, w, head, other, other_tail, entering)
    for m in range(modes):
        entering_out[m] = entering[m]
    for i in range(TAIL):
        old = zero if rim_ref is None else rim_ref[i]
        rim_out[i] = jnp.where(right & (ahead == 0), other_tail[i], old)


def emit_group(
    near_ref, query_ref, states_ref, tables_ref, own_ref, entering, rim, out_ref, power, state, rim_ref, ta, tb, piece_done
):
    tokens = near_ref.shape[0]
    chunks = tokens // CHUNK
    rank = lax.axis_index("context")
    modes, rate, w = table_parts(tables_ref)
    p = [jnp.exp(-r) for r in rate]
    for m in range(modes):
        power[m] = jnp.exp(-CHUNK * rate[m])
        state[m] = entering[m]
    products = first_products(w, [own_ref[modes + TAIL + i] for i in range(HEAD)], rim)
    for i in range(2):
        rim_ref[i] = jnp.where(rank == 0, 0.0, products[i])
    rim_ref[2] = w[1] * rim[3] + w[2] * rim[0]
    rim_ref[3] = w[2] * rim[3]

    def one_chunk(c, turned, first):
        x = [tables_ref[gain_row(modes, m)] * (states_ref[c, m] + state[m]) for m in range(modes)]
        for i in range(CHUNK):
            t = c * CHUNK + i
            x = [a * b for a, b in zip(x, p)]
            near, query = near_ref[t], query_ref[t]
            if first and i < 2:
                x = [a + tables_ref[gain_row(modes, m)] * rim_ref[i] for m, a in enumerate(x)]
                near = near + tables_ref[gain_row(modes, modes)] * rim_ref[i]
                query = query + rim_ref[2 + i]
            mixed = (near + total(x)).astype(BF16).astype(F32)
            turned[pl.ds(i, SUB, stride=STRIDE), :] = query * mixed
        for m in range(modes):
            if first:
                held = (state[m] * p[m] + rim_ref[0]) * p[m] + rim_ref[1]
                state[m] = held * jnp.exp(-(CHUNK - 2) * tables_ref[m])
            else:
                state[m] = state[m] * power[m]

    def turn_out(turned, c):
        for j in range(SUB):
            out_ref[pl.ds(chunk_rows(c), CHUNK), pl.ds(j * LANES, LANES)] = turned[pl.ds(j * STRIDE, CHUNK), :].astype(BF16)

    one_chunk(0, ta, True)
    one_chunk(1, tb, False)
    turn_out(ta, 0)

    def two_chunks(it, none):
        c = 2 * it
        one_chunk(c, ta, False)
        turn_out(tb, c - 1)
        one_chunk(c + 1, tb, False)
        turn_out(ta, c)
        pl.when((it & 1) == 0)(lambda: piece_done(it * 2 * CHUNK // PIECE - 1))
        return none

    lax.fori_loop(1, chunks // 2, two_chunks, 0)
    turn_out(tb, chunks - 1)
    piece_done(tokens // PIECE - 1)


def emit_out(emit, halves, out_hbm, out_ref, half_sems, sems):
    tokens, last = out_ref.shape[0], len(halves)
    copies = [pltpu.make_async_copy(half, out_hbm.at[:, columns(g)], half_sems.at[g]) for g, half in enumerate(halves)]
    for copy in copies:
        copy.start()

    def send(n):
        rows = pl.ds(pl.multiple_of(n * PIECE, PIECE), PIECE)
        return pltpu.make_async_copy(out_ref.at[rows], out_hbm.at[rows, columns(last)], sems.at[n])

    emit(out_ref, lambda n: send(n).start())
    for copy in copies + [send(n) for n in range(tokens // PIECE)]:
        copy.wait()


def is_early(span):
    return (lax.axis_index("context") & span) == 0


def emit_known(near_ref, query_ref, states_ref, tables_ref, own_ref, entering_ref, rim_ref, out_ref, scratch, piece_done):
    entering = [entering_ref[m] for m in range(entering_ref.shape[0])]
    rim = [rim_ref[i] for i in range(TAIL)]
    emit_group(near_ref, query_ref, states_ref, tables_ref, own_ref, entering, rim, out_ref, *scratch, piece_done)


def emit_merged(
    span, near_ref, query_ref, states_ref, tables_ref, own_ref, entering_ref, rim_ref, head, got_ref, out_ref, scratch, piece_done
):
    tokens, modes = near_ref.shape[0], entering_ref.shape[0]
    rank = lax.axis_index("context")
    _, rate, w = table_parts(tables_ref)
    other_tail = unpack(got_ref, modes, TAIL)
    entering = enter(
        tokens, span, rank, rate, w, head, unpack(got_ref, 0, modes), other_tail, [entering_ref[m] for m in range(modes)]
    )
    begins = (rank & (span - 1)) == 0
    rim = [jnp.where(begins, other_tail[i], rim_ref[i]) for i in range(TAIL)]
    emit_group(near_ref, query_ref, states_ref, tables_ref, own_ref, entering, rim, out_ref, *scratch, piece_done)


def early_kernel(span, inputs, out_hbm, out_refs, scratch, half_sems, sems):
    @pl.when(is_early(span))
    def _():
        for g in range(len(inputs) - 1):
            emit_known(*inputs[g], out_refs[g], scratch, lambda n: None)

        def emit(out, piece_done):
            emit_known(*inputs[-1], out, scratch, piece_done)

        emit_out(emit, out_refs[:-1], out_hbm, out_refs[-1], half_sems, sems)


def late_kernel(span, inputs, merged_ref, got_ref, halves, outs, scratch, half_sems=None, sems=None):
    modes = inputs[-2].shape[0]

    @pl.when(jnp.logical_not(is_early(span)))
    def _():
        def emit(out, piece_done):
            head = [merged_ref[modes + TAIL + i] for i in range(HEAD)]
            emit_merged(span, *inputs, head, got_ref, out, scratch, piece_done)

        if sems is None:
            emit(outs[0], lambda n: None)
        else:
            emit_out(emit, halves, outs[0], outs[1], half_sems, sems)


VM = pl.BlockSpec(memory_space=pltpu.VMEM)
HB = pl.BlockSpec(memory_space=pltpu.HBM)


def call(kernel, name, operands, outs, scratch, mib, flops, in_specs=None, out_specs=None, aliases=None):
    in_specs = in_specs or [VM] * len(operands)
    operands = [
        pltpu.with_memory_space_constraint(x, pltpu.VMEM if spec is VM else pltpu.HBM) for x, spec in zip(operands, in_specs)
    ]
    return pl.pallas_call(
        kernel,
        in_specs=in_specs,
        out_specs=[VM] * len(outs) if out_specs is None else out_specs,
        out_shape=outs,
        scratch_shapes=scratch,
        input_output_aliases=aliases or {},
        compiler_params=pltpu.CompilerParams(vmem_limit_bytes=mib * 2**20),
        cost_estimate=pl.CostEstimate(flops=flops, bytes_accessed=2**20, transcendentals=0),
        name=name,
    )(*operands)


def body(streams, short_filter, decay_rate, residue, bias):
    tokens, _, channels = streams.shape
    modes = decay_rate.shape[1]
    groups = channels // GROUP
    chunks, pieces = tokens // CHUNK, tokens // PIECE
    size = lax.axis_size("context")
    vector = (SUB, LANES)
    turned = pltpu.VMEM((SUB * STRIDE, LANES), F32)
    dma = pltpu.SemaphoreType.DMA
    work = tokens * channels
    rows = modes + TAIL + HEAD

    def vectors(*shape):
        return pltpu.VMEM(shape + vector, F32)

    def message_type(count):
        return pltpu.VMEM((count // 2, 2 * SUB, LANES), BF16)

    def swap(message, span):
        return lax.ppermute(message, "context", [(i, i ^ span) for i in range(size)])

    state_types = [vectors(tokens), vectors(chunks, modes), vectors(rows), message_type(rows), vectors(2 * modes + 10)]
    input_types = [
        pltpu.VMEM((modes, channels), F32), pltpu.VMEM((3, 3, channels), F32), pltpu.VMEM((modes, channels), F32),
        vectors(groups), pltpu.VMEM((3, tokens, channels), BF16),
    ]
    made = call(
        first_states_kernel, "states",
        [streams.transpose(1, 0, 2), short_filter, decay_rate.T, residue.T, bias.reshape((groups,) + vector)],
        state_types + input_types, [turned] * 4 + [dma((4,)), dma((groups + 2,))], 4, 24 * work, in_specs=[HB] * 5,
    )
    made, inputs = [made[:5]], made[5:]
    for g in range(1, groups):

        def kernel(*refs, g=g):
            later_states_kernel(g, *refs)

        made.append(call(kernel, "states", inputs, state_types, [turned] * 4, 4, 24 * work))
    key_value, states, own, message, tables = zip(*made)

    def near_of(g, after):
        def kernel(*refs):
            natural, tables_ref, kv_ref = refs[:3]
            near_group(g, natural.at[0], tables_ref, kv_ref, *refs[3 + len(after) :])

        return call(
            kernel, "near", [inputs[-1], tables[g], key_value[g]] + after, [vectors(tokens)] * 2,
            [vectors(CHUNK), turned, turned], 4, 12 * work,
        )

    merged, message = list(own), list(message)
    entering, rim, near = [None] * groups, [None] * groups, [None] * groups
    span = 1
    while True:
        got = [swap(message[g], span) for g in range(groups)]
        if 2 * span >= size:
            break
        for g in range(groups):
            first = entering[g] is None
            after = []
            if first and g == 1:
                near[0] = near_of(0, [rim[0]])
                near[1] = near_of(1, [near[0][0]])
                after = [near[1][0]]
            count = rows if 4 * span < size else modes + TAIL

            def kernel(*refs, span=span, skip=len(after), first=first):
                refs = refs[skip:]
                refs = refs[:3] + (None, None) + refs[3:] if first else refs
                merge_group(span, tokens, *refs)

            merged[g], message[g], entering[g], rim[g] = call(
                kernel, "merge", after + [merged[g], got[g], tables[g]] + ([] if first else [entering[g], rim[g]]),
                [vectors(rows), message_type(count), vectors(modes), vectors(TAIL)], [], 4, 2**20,
            )
        span *= 2

    half = pltpu.VMEM((tokens, GROUP), BF16)
    emit_scratch = [vectors(modes), vectors(modes), vectors(4), turned, turned]
    out_type = pltpu.HBM((tokens, channels), BF16)
    operands = [[*near[g], states[g], tables[g], own[g], entering[g], rim[g]] for g in range(groups)]
    count = len(operands[0])

    def kernel(*refs):
        ins, refs = [refs[i * count : (i + 1) * count] for i in range(groups)], refs[groups * count :]
        out_hbm, out_refs, scratch = refs[0], refs[1 : 1 + groups], refs[1 + groups :]
        early_kernel(span, ins, out_hbm, out_refs, scratch[:5], *scratch[5:])

    out = call(
        kernel, "early", sum(operands, []), [out_type], [half] * groups + emit_scratch + [dma((groups,)), dma((pieces,))],
        4, 40 * work, out_specs=[HB],
    )[0]
    halves = []
    for g in range(groups - 1):

        def kernel(*refs):
            ins, (merged_ref, got_ref, out, *scratch) = refs[:count], refs[count:]
            late_kernel(span, ins, merged_ref, got_ref, (), [out], scratch)

        halves += call(kernel, "late", operands[g] + [merged[g], got[g]], [half], emit_scratch, 4, 20 * work)

    def kernel(*refs):
        ins, (merged_ref, got_ref, *refs) = refs[:count], refs[count:]
        done, (_, out_hbm, out_ref, *scratch) = refs[: groups - 1], refs[groups - 1 :]
        late_kernel(span, ins, merged_ref, got_ref, done, (out_hbm, out_ref), scratch[:5], *scratch[5:])

    operands = operands[-1] + [merged[-1], got[-1]] + halves + [out]
    return call(
        kernel, "late", operands, [out_type], [half] + emit_scratch + [dma((groups,)), dma((pieces,))], 4, 20 * work,
        in_specs=[VM] * (len(operands) - 1) + [HB], out_specs=[HB], aliases={len(operands) - 1: 0},
    )[0]


def solution(mesh):
    in_specs = (
        P(("dp", "context"), None, "tensor"),
        P(None, None, "tensor"),
        P("tensor", None),
        P("tensor", None),
        P("tensor"),
    )
    out_specs = P(("dp", "context"), "tensor")
    return jax.shard_map(body, mesh=mesh, in_specs=in_specs, out_specs=out_specs, check_vma=False)
```

time: 571 us -> 19 us (0.03)
  local copies, waits for them, and re-layouts: 410 us -> 0 us
  matrix products: 92.3 us -> 0 us
  other arithmetic: 27 us -> 0 us
  waiting for transfers between devices: 24.6 us -> 0.11 us
  Pallas kernels: 0 us -> 10.8 us
  starting transfers between devices: 14.4 us -> 7.89 us
    gather x2 -> x0, local copies, waits for them, and re-layouts: 388 us -> none  [block_terms(): jnp.take(filter_taps, jnp.maximum(lag_table, 0), axis=1)]
    dot_general x3 -> x0, matrix products: 92.3 us -> none  [the longest x1 77.4 us: block_terms(): within = jnp.einsum('cab,cnb->cna', toeplitz, signal, precision=HIGH)]
    all_to_all x2 -> x0, waiting for transfers between devices: 24.6 us -> none  [the longest x1 24.5 us: body(): lax.all_to_all(mixed, 'context', split_axis=0, concat_axis=1, tiled=True)]
    convert_element_type x6 -> x0, other arithmetic: 14.7 us -> none  [the longest x1 4.94 us: body(): product_rows = (key_feat * value_feat).astype(jnp.bfloat16)]
    reduce_sum x1 -> x0, other arithmetic: 11.1 us -> none  [block_terms(): jnp.sum(residue[:, None, :] * jnp.exp(positions[None, :, None] * log_pole...]
    pallas_call x0 -> x9, Pallas kernels: none -> 10.8 us  [call(): pl.pallas_call(kernel, in_specs=in_specs, out_specs=[VM] * len(outs) if o...]
    all_to_all x2 -> x0, starting transfers between devices: 9.3 us -> none  [the longest x1 4.86 us: body(): lax.all_to_all(mixed, 'context', split_axis=0, concat_axis=1, tiled=True)]
  transfers between devices with their start and end apart: 3 -> 4, of which waited for: 1 -> 1; matrix products, arithmetic and copies ran while one was open for 72% -> 0% of each run, Pallas kernels for 0% -> 41%
where the time goes in v3:
time: 19 us; the launch traced here: 18.9 us
  Pallas kernels  10.8 us (57%)
  starting transfers between devices  7.89 us (42%)
    pallas_call x9, Pallas kernels, call(): pl.pallas_call(kernel, in_specs=in_specs, out_specs=[VM] * len(outs) if o...  10.8 us
    ppermute x4, starting transfers between devices, swap(): lax.ppermute(message, 'context', [(i, i ^ span) for i in range(size)])  7.89 us
  transfers between devices with their start and end apart: 4, of which 1 were waited for; matrix products, arithmetic and copies ran while one was open for 0% of the time, Pallas kernels for 41%

profile of v3, /device:TPU:0, one launch (start us, length us, event | category | flops | bytes accessed | tf_op | source)
XLA Modules:
  0.0 18.9 jit_solution(6914076814081125202)
XLA Ops:
  0.0 3.1 %states.2 = (f32[256,8,128]{2,1,0:T(8,128)S(1)}, f32[16,16,8,128]{3,2,1,0:T(8,128)S(1)}, f32[26,8,128]{2,1,0:T(8,128)S(1)}, bf16[13,16,128]{2,1,0:T(8,128)(2,1)S...) custom-call(bf16[3,256,2048]{2,1,0:T(8,128)(2,1)} %bitcast.4, ...), custom_call_target="tpu_custom_call" | custom-call | flops 12582912 | bytes 1048576 | tf_op jit(solution)/shard_map/states/pallas_call | solution.py:421
  3.1 3.1 %collective-permute-start = (bf16[13,16,128]{2,1,0:T(8,128)(2,1)S(1)}, bf16[13,16,128]{2,1,0:T(8,128)(2,1)S(1)}, u32[]{:S(2)}, u32[]{:S(2)}) collective-permute-start(bf16[13,16,128]{2,1,0:T(8,128)(2,1)S(1)} %get-tuple-element.42), channel_id=1, source_target_pairs={{0,4},{4,0},{8,12},{12,8},{1,5},{5,1},{9,13},{13,9},{2,6},{6,2},{1... | collective-permute-start | bytes 159752 | tf_op jit(solution)/shard_map/ppermute | solution.py:453
  6.2 1.9 %states.3 = (f32[256,8,128]{2,1,0:T(8,128)S(1)}, f32[16,16,8,128]{3,2,1,0:T(8,128)S(1)}, f32[26,8,128]{2,1,0:T(8,128)S(1)}, bf16[13,16,128]{2,1,0:T(8,128)(2,1)S(1)}, f32[42,8,128]{2,1,0:T(8,128)S(1)}) custom-call(f32[16,2048]{1,0:T(8,128)S(1)} %get-tuple-element.33.refs_0_, f32[3,3,2048]{2,1,0:T(4,128)S(1)} %get-tuple-element.34.refs_1_, ...), custom_call_target="tpu_custom_call" | custom-call | flops 12582912 | bytes 1048576 | tf_op jit(solution)/shard_map/states/pallas_call | solution.py:421
  8.1 0.1 collective-permute-start.1
  8.2 0.1 collective-permute-done.refs_1_
  8.3 0.1 merge.2
  8.3 3.1 %collective-permute-start.3 = (bf16[11,16,128]{2,1,0:T(8,128)(2,1)S(1)}, bf16[11,16,128]{2,1,0:T(8,128)(2,1)S(1)}, u32[]{:S(2)}, u32[]{:S(2)}) collective-permute-start(bf16[11,16,128]{2,1,0:T(8,128)(2,1)S(1)} %get-tuple-element.58), channel_id=1, source_target_pairs={{0,8},{4,12},{8,0},{12,4},{1,9},{5,13},{9,1},{13,5},{2,10},{6,14},... | collective-permute-start | bytes 135176 | tf_op jit(solution)/shard_map/ppermute | solution.py:453
  11.4 0.9 %near.2 = (f32[256,8,128]{2,1,0:T(8,128)S(1)}, f32[256,8,128]{2,1,0:T(8,128)S(1)}) custom-call(bf16[3,256,2048]{2,1,0:T(8,128)(2,1)S(1)} %get-tuple-element.32.refs_4_.refs_0_, f32[42,8,128]{2,1,0:T(8,128)S(1)} %get-tuple-element.39.refs_2_.refs_1_.refs_3_, f32[256,8,128]{2,1,0:T(8,128)S(1)} %get-tuple-element.40.refs_2_, ...), custom_call_target="tpu_custom_call" | custom-call | flops 6291456 | bytes 1048576 | tf_op jit(solution)/shard_map/near/pallas_call | solution.py:421
  12.4 0.9 %near.3 = (f32[256,8,128]{2,1,0:T(8,128)S(1)}, f32[256,8,128]{2,1,0:T(8,128)S(1)}) custom-call(bf16[3,256,2048]{2,1,0:T(8,128)(2,1)S(1)} %get-tuple-element.32.refs_4_.refs_0_, f32[42,8,128]{2,1,0:T(8,128)S(1)} %get-tuple-element.37.refs_1_.refs_3_.refs_10_, f32[256,8,128]{2,1,0:T(8,128)S(1)} %get-tuple-element.38.refs_2_, ...), custom_call_target="tpu_custom_call" | custom-call | flops 6291456 | bytes 1048576 | tf_op jit(solution)/shard_map/near/pallas_call | solution.py:421
  13.3 0.0 collective-permute-done.1.refs_2_
  13.3 0.1 merge.3
  13.4 1.6 %collective-permute-start.2 = (bf16[11,16,128]{2,1,0:T(8,128)(2,1)S(1)}, bf16[11,16,128]{2,1,0:T(8,128)(2,1)S(1)}, u32[]{:S(2)}, u32[]{:S(2)}) collective-permute-start(bf16[11,16,128]{2,1,0:T(8,128)(2,1)S(1)} %get-tuple-element.53), channel_id=1, source_target_pairs={{0,8},{4,12},{8,0},{12,4},{1,9},{5,13},{9,1},{13,5},{2,10},{6,14},... | collective-permute-start | bytes 135176 | tf_op jit(solution)/shard_map/ppermute | solution.py:453
  15.0 3.8 %early.1.refs_10_ = bf16[256,2048]{1,0:T(8,128)(2,1)} custom-call(f32[256,8,128]{2,1,0:T(8,128)S(1)} %get-tuple-element.44.refs_3_.refs_0_, f32[256,8,128]{2,1,0:T(8,128)S(1)} %get-tuple-element.54.refs_1_, f32[16,16,8,128]{3,2,1,0:T(8,128)S(1)} %get-tuple-element.55.refs_2_, f32[42,8,128]{2,1,0:T(8,128)S(1)} %get-tuple-element.39.refs_2_.refs_1_.refs_3_, ...), custom_call_target="tpu_custom_call" | custom-call | flops 20971520 | bytes 1048576 | tf_op jit(solution)/shard_map/early/pallas_call | solution.py:421
  18.8 0.0 collective-permute-done.3.refs_8_
  18.8 0.0 collective-permute-done.2.refs_8_
  18.8 0.1 late.3
  (1 shorter events, 0.0 us)
Async XLA Ops:
  3.1 5.2 %collective-permute-start = (bf16[13,16,128]{2,1,0:T(8,128)(2,1)S(1)}, bf16[13,16,128]{2,1,0:T(8,128)(2,1)S(1)}, u32[]{:S(2)}, u32[]{:S(2)}) collective-permute-start(bf16[13,16,128]{2,1,0:T(8,128)(2,1)S(1)} %get-tuple-element.42), channel_id=1, source_target_pairs={{0,4},{4,0},{8,12},{12,8},{1,5},{5,1},{9,13},{13,9},{2,6},{6,2},{1... | collective-permute-start | bytes 159752 | tf_op jit(solution)/shard_map/ppermute | solution.py:453
  8.1 5.2 %collective-permute-start.1 = (bf16[13,16,128]{2,1,0:T(8,128)(2,1)S(1)}, bf16[13,16,128]{2,1,0:T(8,128)(2,1)S(1)}, u32[]{:S(2)}, u32[]{:S(2)}) collective-permute-start(bf16[13,16,128]{2,1,0:T(8,128)(2,1)S(1)} %get-tuple-element.49), channel_id=1, source_target_pairs={{0,4},{4,0},{8,12},{12,8},{1,5},{5,1},{9,13},{13,9},{2,6},{6,2},{1... | collective-permute-start | bytes 159752 | tf_op jit(solution)/shard_map/ppermute | solution.py:453
  8.3 10.4 %collective-permute-start.3 = (bf16[11,16,128]{2,1,0:T(8,128)(2,1)S(1)}, bf16[11,16,128]{2,1,0:T(8,128)(2,1)S(1)}, u32[]{:S(2)}, u32[]{:S(2)}) collective-permute-start(bf16[11,16,128]{2,1,0:T(8,128)(2,1)S(1)} %get-tuple-element.58), channel_id=1, source_target_pairs={{0,8},{4,12},{8,0},{12,4},{1,9},{5,13},{9,1},{13,5},{2,10},{6,14},... | collective-permute-start | bytes 135176 | tf_op jit(solution)/shard_map/ppermute | solution.py:453
  13.4 5.4 %collective-permute-start.2 = (bf16[11,16,128]{2,1,0:T(8,128)(2,1)S(1)}, bf16[11,16,128]{2,1,0:T(8,128)(2,1)S(1)}, u32[]{:S(2)}, u32[]{:S(2)}) collective-permute-start(bf16[11,16,128]{2,1,0:T(8,128)(2,1)S(1)} %get-tuple-element.53), channel_id=1, source_target_pairs={{0,8},{4,12},{8,0},{12,4},{1,9},{5,13},{9,1},{13,5},{2,10},{6,14},... | collective-permute-start | bytes 135176 | tf_op jit(solution)/shard_map/ppermute | solution.py:453

commit v4 on v3

--- a/solution.py
+++ b/solution.py
@@ -13,6 +13,7 @@
 CHUNK = 16
 PIECE = 64
 STRIDE = CHUNK + 8
+EARLY = (4, 8)
 HEAD = 4
 TAIL = 6
 
@@ -95,7 +96,7 @@
 
 def state_kernel(
     g, rate_nat, taps_nat, residue_nat, bias_nat, natural,
-    kv_ref, states_ref, own_ref, message_ref, tables_ref, ka, kb, va, vb, wait_piece, wait_rest,
+    kv_ref, states_ref, own_ref, tables_ref, ka, kb, va, vb, wait_piece, wait_rest,
 ):
     q_nat, k_nat, v_nat = (natural.at[i] for i in range(3))
     tokens, modes = natural.shape[1], rate_nat.shape[0]
@@ -118,10 +119,6 @@
     wait_piece(0)
     turn_in(k_nat, ka, 0, g)
     turn_in(v_nat, va, 0, g)
-    for i in range(2):
-        own_ref[modes + TAIL + 2 * i] = row(ka, i)
-        own_ref[modes + TAIL + 2 * i + 1] = row(va, i)
-
     def one_chunk(c, ks, vs, acc, last):
         k1, k2, v1, v2 = last
         for m in range(modes):
@@ -150,26 +147,41 @@
         turn_in(v_nat, va, ahead, g)
         return one_chunk(c + 1, kb, vb, acc, last)
 
-    acc, last = lax.fori_loop(0, chunks // 2, two_chunks, ([zero] * modes, (zero,) * 4))
+    acc, _ = lax.fori_loop(0, chunks // 2, two_chunks, ([zero] * modes, (zero,) * 4))
     for m in range(modes):
         own_ref[m] = acc[m]
-    k1, k2, v1, v2 = last
-    for i, value in ((1, k2), (2, v2), (4, k1), (5, v1)):
-        own_ref[modes + i] = value
     wait_rest()
     turn_rows(residue_nat, ka, modes, g)
     for m in range(modes):
         tables_ref[gain_row(modes, m)] = row(ka, m)
     tables_ref[gain_row(modes, modes)] = bias_nat[g]
-    turn_in(q_nat, va, tokens - CHUNK, g)
-    for i in range(2):
-        own_ref[modes + 3 * i] = row(va, CHUNK - 2 + i)
-    pack(message_ref, [own_ref[i] for i in range(modes + TAIL + HEAD)])
+
+
+def edge_rows(natural, edges_ref, turned, g):
+    tokens = natural.shape[1]
+    for stream in range(3):
+        turn_in(natural.at[stream], turned, tokens - CHUNK, g)
+        for i in range(2):
+            edges_ref[g, 3 * i + stream] = row(turned, CHUNK - 2 + i)
+        if stream:
+            turn_in(natural.at[stream], turned, 0, g)
+            for i in range(2):
+                edges_ref[g, TAIL + 2 * i + stream - 1] = row(turned, i)
+
+
+def tails_and_heads(edges, heads):
+    rows = sum([e[:TAIL] for e in edges], [])
+    return rows + sum([e[TAIL:] for e in edges], []) if heads else rows
+
+
+def other_edges(first_got, g, groups, modes, heads):
+    tail = unpack(first_got, modes + TAIL * g, TAIL)
+    return tail, unpack(first_got, modes + TAIL * groups + HEAD * g, HEAD) if heads else None
 
 
 def first_states_kernel(
     streams, taps_hbm, rate_hbm, residue_hbm, bias_hbm,
-    kv_ref, states_ref, own_ref, message_ref, tables_ref, rate_nat, taps_nat, residue_nat, bias_nat, natural,
+    kv_ref, states_ref, own_ref, tables_ref, message_ref, edges_ref, rate_nat, taps_nat, residue_nat, bias_nat, natural,
     ka, kb, va, vb, table_sems, stream_sems,
 ):
     _, tokens, channels = natural.shape
@@ -202,12 +214,22 @@
 
     state_kernel(
         0, rate_nat, taps_nat, residue_nat, bias_nat, natural,
-        kv_ref, states_ref, own_ref, message_ref, tables_ref, ka, kb, va, vb, lambda n: pieces[n].wait(), wait_rest,
+        kv_ref, states_ref, own_ref, tables_ref, ka, kb, va, vb, lambda n: pieces[n].wait(), wait_rest,
     )
-
-
-def later_states_kernel(g, *refs):
-    state_kernel(g, *refs, lambda n: None, lambda: None)
+    for g in range(groups):
+        edge_rows(natural, edges_ref, ka, g)
+    state = [own_ref[m] for m in range(own_ref.shape[0])]
+    pack(message_ref, state + tails_and_heads([[edges_ref[g, i] for i in range(TAIL + HEAD)] for g in range(groups)], True))
+
+
+def later_states_kernel(
+    g, rate_nat, taps_nat, residue_nat, bias_nat, natural, kv_ref, states_ref, own_ref, tables_ref, message_ref, *scratch
+):
+    state_kernel(
+        g, rate_nat, taps_nat, residue_nat, bias_nat, natural, kv_ref, states_ref, own_ref, tables_ref, *scratch,
+        lambda n: None, lambda: None,
+    )
+    pack(message_ref, [own_ref[m] for m in range(own_ref.shape[0])])
 
 
 def near_group(g, q_nat, tables_ref, kv_ref, near_ref, query_ref, taps, qa, qb):
@@ -246,35 +268,46 @@
     lax.fori_loop(0, chunks // 2, two_chunks, (zero, zero))
 
 
-def merge_group(span, tokens, own_ref, got_ref, tables_ref, entering_ref, rim_ref, next_ref, message_ref, entering_out, rim_out):
+def merge_group(
+    span, tokens, g, last, own_ref, edges_ref, got_ref, first_got, tables_ref, entering_ref, rim_ref,
+    message_ref, entering_out, rim_out, next_ref, edges_out,
+):
     modes, rate, w = table_parts(tables_ref)
+    groups = edges_ref.shape[0]
     rank = lax.axis_index("context")
     right = (rank & span) != 0
     ahead = rank & (span - 1)
     length = 1.0 * tokens * span
     zero = jnp.zeros((SUB, LANES), F32)
-    state = [own_ref[m] for m in range(modes)]
-    tail = [own_ref[modes + i] for i in range(TAIL)]
-    head = [own_ref[modes + TAIL + i] for i in range(HEAD)]
-    other = unpack(got_ref, 0, modes)
-    other_tail = unpack(got_ref, modes, TAIL)
-    other_head = unpack(got_ref, modes + TAIL, HEAD)
 
     def pick(a, b):
         return [jnp.where(right, x, y) for x, y in zip(a, b)]
 
+    def edge(group):
+        rows = [edges_ref[group, i] for i in range(TAIL + HEAD)]
+        return rows[:TAIL], rows[TAIL:]
+
+    state, other = [own_ref[m] for m in range(modes)], unpack(got_ref, 0, modes)
+    tail, head = edge(g)
+    other_tail, other_head = other_edges(first_got, g, groups, modes, True)
+    products = first_products(w, pick(head, other_head), pick(other_tail, tail))
     left_state, right_state = pick(other, state), pick(state, other)
-    left_head, right_head = pick(other_head, head), pick(head, other_head)
-    left_tail, right_tail = pick(other_tail, tail), pick(tail, other_tail)
-    products = first_products(w, right_head, left_tail)
     rows = [
         right_state[m] + jnp.exp(-length * rate[m]) * left_state[m] + first_terms(rate[m], products, length)
         for m in range(modes)
     ]
-    rows = rows + right_tail + left_head
+    if not last:
+        for m in range(modes):
+            next_ref[m] = rows[m]
+    if g == 0:
+        edges = []
+        for group in range(groups):
+            mine, theirs = edge(group), other_edges(first_got, group, groups, modes, True)
+            edges.append(pick(mine[0], theirs[0]) + pick(theirs[1], mine[1]))
+            for i, value in enumerate(edges[-1]):
+                edges_out[group, i] = value
+        rows = rows + tails_and_heads(edges, not last)
     pack(message_ref, rows)
-    for i, value in enumerate(rows):
-        next_ref[i] = value
     entering = [zero if entering_ref is None else entering_ref[m] for m in range(modes)]
     entering = enter(tokens, span, rank, rate, w, head, other, other_tail, entering)
     for m in range(modes):
@@ -285,21 +318,21 @@
 
 
 def emit_group(
-    near_ref, query_ref, states_ref, tables_ref, own_ref, entering, rim, out_ref, power, state, rim_ref, ta, tb, piece_done
+    which, near_ref, query_ref, states_ref, tables_ref, head, entering, rim, out_ref, state, power, rim_ref, ta, tb, piece_done
 ):
-    tokens = near_ref.shape[0]
-    chunks = tokens // CHUNK
     rank = lax.axis_index("context")
     modes, rate, w = table_parts(tables_ref)
     p = [jnp.exp(-r) for r in rate]
     for m in range(modes):
         power[m] = jnp.exp(-CHUNK * rate[m])
-        state[m] = entering[m]
-    products = first_products(w, [own_ref[modes + TAIL + i] for i in range(HEAD)], rim)
-    for i in range(2):
-        rim_ref[i] = jnp.where(rank == 0, 0.0, products[i])
-    rim_ref[2] = w[1] * rim[3] + w[2] * rim[0]
-    rim_ref[3] = w[2] * rim[3]
+    if which.start == 0:
+        for m in range(modes):
+            state[m] = entering[m]
+        products = first_products(w, head, rim)
+        for i in range(2):
+            rim_ref[i] = jnp.where(rank == 0, 0.0, products[i])
+        rim_ref[2] = w[1] * rim[3] + w[2] * rim[0]
+        rim_ref[3] = w[2] * rim[3]
 
     def one_chunk(c, turned, first):
         x = [tables_ref[gain_row(modes, m)] * (states_ref[c, m] + state[m]) for m in range(modes)]
@@ -324,9 +357,10 @@
         for j in range(SUB):
             out_ref[pl.ds(chunk_rows(c), CHUNK), pl.ds(j * LANES, LANES)] = turned[pl.ds(j * STRIDE, CHUNK), :].astype(BF16)
 
-    one_chunk(0, ta, True)
-    one_chunk(1, tb, False)
-    turn_out(ta, 0)
+    begin = which.start
+    one_chunk(begin, ta, begin == 0)
+    one_chunk(begin + 1, tb, False)
+    turn_out(ta, begin)
 
     def two_chunks(it, none):
         c = 2 * it
@@ -337,14 +371,17 @@
         pl.when((it & 1) == 0)(lambda: piece_done(it * 2 * CHUNK // PIECE - 1))
         return none
 
-    lax.fori_loop(1, chunks // 2, two_chunks, 0)
-    turn_out(tb, chunks - 1)
-    piece_done(tokens // PIECE - 1)
-
-
-def emit_out(emit, halves, out_hbm, out_ref, half_sems, sems):
-    tokens, last = out_ref.shape[0], len(halves)
-    copies = [pltpu.make_async_copy(half, out_hbm.at[:, columns(g)], half_sems.at[g]) for g, half in enumerate(halves)]
+    lax.fori_loop(begin // 2 + 1, which.stop // 2, two_chunks, 0)
+    turn_out(tb, which.stop - 1)
+    piece_done(which.stop * CHUNK // PIECE - 1)
+
+
+def emit_out(emit, ready, out_hbm, out_ref, ready_sems, sems):
+    tokens, last = out_ref.shape[0], out_hbm.shape[1] // GROUP - 1
+    copies = [
+        pltpu.make_async_copy(buffer.at[rows], out_hbm.at[rows, columns(g)], ready_sems.at[i])
+        for i, (rows, g, buffer) in enumerate(ready)
+    ]
     for copy in copies:
         copy.start()
 
@@ -361,52 +398,26 @@
     return (lax.axis_index("context") & span) == 0
 
 
-def emit_known(near_ref, query_ref, states_ref, tables_ref, own_ref, entering_ref, rim_ref, out_ref, scratch, piece_done):
+def emit_known(which, g, fixed, edges_ref, entering_ref, rim_ref, out_ref, scratch, piece_done):
     entering = [entering_ref[m] for m in range(entering_ref.shape[0])]
     rim = [rim_ref[i] for i in range(TAIL)]
-    emit_group(near_ref, query_ref, states_ref, tables_ref, own_ref, entering, rim, out_ref, *scratch, piece_done)
-
-
-def emit_merged(
-    span, near_ref, query_ref, states_ref, tables_ref, own_ref, entering_ref, rim_ref, head, got_ref, out_ref, scratch, piece_done
-):
-    tokens, modes = near_ref.shape[0], entering_ref.shape[0]
+    head = [edges_ref[g, TAIL + i] for i in range(HEAD)]
+    emit_group(which, *fixed, head, entering, rim, out_ref, *scratch, piece_done)
+
+
+def emit_merged(span, g, fixed, edges_ref, entering_ref, rim_ref, merged_edges, got_ref, first_got, out_ref, scratch, piece_done):
+    tokens, modes = fixed[0].shape[0], entering_ref.shape[0]
     rank = lax.axis_index("context")
-    _, rate, w = table_parts(tables_ref)
-    other_tail = unpack(got_ref, modes, TAIL)
+    _, rate, w = table_parts(fixed[3])
+    other_tail, _ = other_edges(first_got, g, edges_ref.shape[0], modes, False)
     entering = enter(
-        tokens, span, rank, rate, w, head, unpack(got_ref, 0, modes), other_tail, [entering_ref[m] for m in range(modes)]
+        tokens, span, rank, rate, w, [merged_edges[g, TAIL + i] for i in range(HEAD)],
+        unpack(got_ref, 0, modes), other_tail, [entering_ref[m] for m in range(modes)],
     )
     begins = (rank & (span - 1)) == 0
     rim = [jnp.where(begins, other_tail[i], rim_ref[i]) for i in range(TAIL)]
-    emit_group(near_ref, query_ref, states_ref, tables_ref, own_ref, entering, rim, out_ref, *scratch, piece_done)
-
-
-def early_kernel(span, inputs, out_hbm, out_refs, scratch, half_sems, sems):
-    @pl.when(is_early(span))
-    def _():
-        for g in range(len(inputs) - 1):
-            emit_known(*inputs[g], out_refs[g], scratch, lambda n: None)
-
-        def emit(out, piece_done):
-            emit_known(*inputs[-1], out, scratch, piece_done)
-
-        emit_out(emit, out_refs[:-1], out_hbm, out_refs[-1], half_sems, sems)
-
-
-def late_kernel(span, inputs, merged_ref, got_ref, halves, outs, scratch, half_sems=None, sems=None):
-    modes = inputs[-2].shape[0]
-
-    @pl.when(jnp.logical_not(is_early(span)))
-    def _():
-        def emit(out, piece_done):
-            head = [merged_ref[modes + TAIL + i] for i in range(HEAD)]
-            emit_merged(span, *inputs, head, got_ref, out, scratch, piece_done)
-
-        if sems is None:
-            emit(outs[0], lambda n: None)
-        else:
-            emit_out(emit, halves, outs[0], outs[1], half_sems, sems)
+    head = [edges_ref[g, TAIL + i] for i in range(HEAD)]
+    emit_group(range(tokens // CHUNK), *fixed, head, entering, rim, out_ref, *scratch, piece_done)
 
 
 VM = pl.BlockSpec(memory_space=pltpu.VMEM)
@@ -441,7 +452,6 @@
     turned = pltpu.VMEM((SUB * STRIDE, LANES), F32)
     dma = pltpu.SemaphoreType.DMA
     work = tokens * channels
-    rows = modes + TAIL + HEAD
 
     def vectors(*shape):
         return pltpu.VMEM(shape + vector, F32)
@@ -452,94 +462,168 @@
     def swap(message, span):
         return lax.ppermute(message, "context", [(i, i ^ span) for i in range(size)])
 
-    state_types = [vectors(tokens), vectors(chunks, modes), vectors(rows), message_type(rows), vectors(2 * modes + 10)]
+    edge = TAIL + HEAD
+    state_types = [vectors(tokens), vectors(chunks, modes), vectors(modes), vectors(2 * modes + 10)]
     input_types = [
         pltpu.VMEM((modes, channels), F32), pltpu.VMEM((3, 3, channels), F32), pltpu.VMEM((modes, channels), F32),
         vectors(groups), pltpu.VMEM((3, tokens, channels), BF16),
     ]
-    made = call(
+    *first, first_message, own_edges, rates, taps, residues, biases, natural = call(
         first_states_kernel, "states",
         [streams.transpose(1, 0, 2), short_filter, decay_rate.T, residue.T, bias.reshape((groups,) + vector)],
-        state_types + input_types, [turned] * 4 + [dma((4,)), dma((groups + 2,))], 4, 24 * work, in_specs=[HB] * 5,
+        state_types + [message_type(modes + groups * edge), vectors(groups, edge)] + input_types,
+        [turned] * 4 + [dma((4,)), dma((groups + 2,))], 4, 24 * work, in_specs=[HB] * 5,
     )
-    made, inputs = [made[:5]], made[5:]
+    made, message = [first], [first_message]
     for g in range(1, groups):
 
         def kernel(*refs, g=g):
             later_states_kernel(g, *refs)
 
-        made.append(call(kernel, "states", inputs, state_types, [turned] * 4, 4, 24 * work))
-    key_value, states, own, message, tables = zip(*made)
-
-    def near_of(g, after):
+        *later, later_message = call(
+            kernel, "states", [rates, taps, residues, biases, natural], state_types + [message_type(modes)], [turned] * 4, 4, 24 * work
+        )
+        made.append(later)
+        message.append(later_message)
+    key_value, states, own, tables = zip(*made)
+
+    def near_all(early, after):
         def kernel(*refs):
-            natural, tables_ref, kv_ref = refs[:3]
-            near_group(g, natural.at[0], tables_ref, kv_ref, *refs[3 + len(after) :])
-
-        return call(
-            kernel, "near", [inputs[-1], tables[g], key_value[g]] + after, [vectors(tokens)] * 2,
-            [vectors(CHUNK), turned, turned], 4, 12 * work,
+            natural, refs = refs[0], refs[1 + len(after) :]
+            ins, outs, scratch = refs[: 2 * groups], refs[2 * groups : 4 * groups], refs[4 * groups :]
+
+            @pl.when(is_early(size // 2) == early)
+            def _():
+                for g in range(groups):
+                    near_group(g, natural.at[0], *ins[2 * g : 2 * g + 2], *outs[2 * g : 2 * g + 2], *scratch)
+
+        operands = sum([[tables[g], key_value[g]] for g in range(groups)], [])
+        outs = call(
+            kernel, "near", [natural] + after + operands, [vectors(tokens)] * (2 * groups),
+            [vectors(CHUNK), turned, turned], 4, 24 * work,
         )
-
-    merged, message = list(own), list(message)
-    entering, rim, near = [None] * groups, [None] * groups, [None] * groups
+        return [list(outs[2 * g : 2 * g + 2]) for g in range(groups)]
+
+    half = pltpu.VMEM((tokens, GROUP), BF16)
+    emit_scratch = [vectors(modes), vectors(4), turned, turned]
+
+    merged, edges = list(own), own_edges
+    entering, rim = [None] * groups, [None] * groups
+    begun, begun_state = [], []
     span = 1
     while True:
         got = [swap(message[g], span) for g in range(groups)]
         if 2 * span >= size:
             break
+        last, first = 4 * span >= size, entering[0] is None
+        if first:
+            near = near_all(True, [])
+        old_edges = edges
         for g in range(groups):
-            first = entering[g] is None
-            after = []
-            if first and g == 1:
-                near[0] = near_of(0, [rim[0]])
-                near[1] = near_of(1, [near[0][0]])
-                after = [near[1][0]]
-            count = rows if 4 * span < size else modes + TAIL
-
-            def kernel(*refs, span=span, skip=len(after), first=first):
-                refs = refs[skip:]
-                refs = refs[:3] + (None, None) + refs[3:] if first else refs
-                merge_group(span, tokens, *refs)
-
-            merged[g], message[g], entering[g], rim[g] = call(
-                kernel, "merge", after + [merged[g], got[g], tables[g]] + ([] if first else [entering[g], rim[g]]),
-                [vectors(rows), message_type(count), vectors(modes), vectors(TAIL)], [], 4, 2**20,
-            )
+            part = range(EARLY[g - 1] if g else 0, EARLY[g]) if last and g < len(EARLY) else range(0)
+            early = []
+            if part:
+                early = [*near[0], states[0], tables[0], own_edges] + ([entering[0], rim[0], begun_state[-1]] if g else [])
+            operands = [merged[g], old_edges, got[g], got[0], tables[g]] + ([] if first else [entering[g], rim[g]])
+            count = modes + (groups * (TAIL if last else edge) if g == 0 else 0)
+            outs = [message_type(count), vectors(modes), vectors(TAIL)]
+            outs += [] if last else [vectors(modes)]
+            outs += [vectors(groups, edge)] if g == 0 else []
+            outs += [half, vectors(modes)] if part else []
+
+            def kernel(*refs, g=g, span=span, last=last, first=first, part=part, extra=len(early), results=len(outs)):
+                refs = list(refs)
+                ins = [refs.pop(0) for _ in range(5)] + ([None, None] if first else [refs.pop(0) for _ in range(2)])
+                more = [refs.pop(0) for _ in range(extra)]
+                produced = [refs.pop(0) for _ in range(results)]
+                state_out = None if last else produced[3]
+                edges_out = produced[3 if last else 4] if g == 0 else None
+                merge_group(span, tokens, g, last, *ins, *produced[:3], state_out, edges_out)
+                if part:
+
+                    @pl.when(is_early(2 * span))
+                    def _():
+                        out_ref, state_ref = produced[-2:]
+                        for m in range(modes if g else 0):
+                            state_ref[m] = more[7][m]
+                        known = more[5:7] if g else produced[1:3]
+                        emit_known(part, 0, more[:4], more[4], *known, out_ref, [state_ref] + refs, lambda n: None)
+
+            made = list(call(kernel, "merge", operands + early, outs, emit_scratch if part else [], 4, 2**20))
+            message[g], entering[g], rim[g] = made[:3]
+            if not last:
+                merged[g] = made[3]
+            if g == 0:
+                edges = made[3 if last else 4]
+            if part:
+                begun.append((pl.ds(part.start * CHUNK, len(part) * CHUNK), made[-2]))
+                begun_state.append(made[-1])
         span *= 2
 
-    half = pltpu.VMEM((tokens, GROUP), BF16)
-    emit_scratch = [vectors(modes), vectors(modes), vectors(4), turned, turned]
     out_type = pltpu.HBM((tokens, channels), BF16)
-    operands = [[*near[g], states[g], tables[g], own[g], entering[g], rim[g]] for g in range(groups)]
-    count = len(operands[0])
-
-    def kernel(*refs):
-        ins, refs = [refs[i * count : (i + 1) * count] for i in range(groups)], refs[groups * count :]
-        out_hbm, out_refs, scratch = refs[0], refs[1 : 1 + groups], refs[1 + groups :]
-        early_kernel(span, ins, out_hbm, out_refs, scratch[:5], *scratch[5:])
+    pair = [[entering[g], rim[g]] for g in range(groups)]
+    begin = EARLY[len(begun) - 1] if begun else 0
+
+    def kernel(own_edges, *refs):
+        refs = list(refs)
+        ready = [refs.pop(0) for _ in begun]
+        begun_state = refs.pop(0) if begun else None
+        ins, refs = [refs[i * 6 : i * 6 + 6] for i in range(groups)], refs[groups * 6 :]
+        out_hbm, out_refs, state, scratch = refs[0], refs[1 : 1 + groups], refs[1 + groups], refs[2 + groups : 6 + groups]
+
+        @pl.when(is_early(span))
+        def _():
+            for m in range(modes if begun else 0):
+                state[m] = begun_state[m]
+            for g in range(groups - 1):
+                which = range(0 if g else begin, chunks)
+                emit_known(which, g, ins[g][:4], own_edges, *ins[g][4:], out_refs[g], [state, *scratch], lambda n: None)
+
+            def emit(out, piece_done):
+                emit_known(range(chunks), groups - 1, ins[-1][:4], own_edges, *ins[-1][4:], out, [state, *scratch], piece_done)
+
+            done = [(rows, 0, buffer) for (rows, _), buffer in zip(begun, ready)]
+            done += [(pl.ds(begin * CHUNK, tokens - begin * CHUNK), 0, out_refs[0])]
+            done += [(pl.ds(0, tokens), g, out_refs[g]) for g in range(1, groups - 1)]
+            emit_out(emit, done, out_hbm, out_refs[-1], *refs[6 + groups :])
 
     out = call(
-        kernel, "early", sum(operands, []), [out_type], [half] * groups + emit_scratch + [dma((groups,)), dma((pieces,))],
+        kernel, "early",
+        [own_edges] + [buffer for _, buffer in begun] + begun_state[-1:]
+        + sum([[*near[g], states[g], tables[g], *pair[g]] for g in range(groups)], []),
+        [out_type], [half] * groups + [vectors(modes)] + emit_scratch + [dma((groups + 1,)), dma((pieces,))],
         4, 40 * work, out_specs=[HB],
     )[0]
+    near = near_all(False, [entering[-1]])
+    fixed = [[*near[g], states[g], tables[g]] for g in range(groups)]
     halves = []
-    for g in range(groups - 1):
-
-        def kernel(*refs):
-            ins, (merged_ref, got_ref, out, *scratch) = refs[:count], refs[count:]
-            late_kernel(span, ins, merged_ref, got_ref, (), [out], scratch)
-
-        halves += call(kernel, "late", operands[g] + [merged[g], got[g]], [half], emit_scratch, 4, 20 * work)
-
-    def kernel(*refs):
-        ins, (merged_ref, got_ref, *refs) = refs[:count], refs[count:]
-        done, (_, out_hbm, out_ref, *scratch) = refs[: groups - 1], refs[groups - 1 :]
-        late_kernel(span, ins, merged_ref, got_ref, done, (out_hbm, out_ref), scratch[:5], *scratch[5:])
-
-    operands = operands[-1] + [merged[-1], got[-1]] + halves + [out]
+    for g in range(groups):
+        final = g + 1 == groups
+        operands = fixed[g] + [own_edges] + pair[g] + [edges, got[g], got[0]] + (halves + [out] if final else [])
+
+        def kernel(*refs, g=g, final=final):
+            ins, refs = refs[:10], refs[10:]
+            if final:
+                done, (_, out_hbm, out_ref, *scratch) = refs[: groups - 1], refs[groups - 1 :]
+            else:
+                out_ref, *scratch = refs
+
+            @pl.when(jnp.logical_not(is_early(span)))
+            def _():
+                def emit(out, piece_done):
+                    emit_merged(span, g, ins[:4], *ins[4:], out, scratch[:5], piece_done)
+
+                if final:
+                    ready = [(pl.ds(0, tokens), i, x) for i, x in enumerate(done)]
+                    emit_out(emit, ready, out_hbm, out_ref, *scratch[5:])
+                else:
+                    emit(out_ref, lambda n: None)
+
+        if not final:
+            halves += call(kernel, "late", operands, [half], [vectors(modes)] + emit_scratch, 4, 20 * work)
     return call(
-        kernel, "late", operands, [out_type], [half] + emit_scratch + [dma((groups,)), dma((pieces,))], 4, 20 * work,
+        kernel, "late", operands, [out_type],
+        [half, vectors(modes)] + emit_scratch + [dma((groups,)), dma((pieces,))], 4, 20 * work,
         in_specs=[VM] * (len(operands) - 1) + [HB], out_specs=[HB], aliases={len(operands) - 1: 0},
     )[0]
 

time: 19 us -> 18.1 us (0.953)
  starting transfers between devices: 7.89 us -> 6.59 us
  waiting for transfers between devices: 0.11 us -> 0.4 us
    ppermute x4, starting transfers between devices: 7.89 us -> 6.59 us  [swap(): lax.ppermute(message, 'context', [(i, i ^ span) for i in range(size)])]
    ppermute x4, waiting for transfers between devices: 0.11 us -> 0.4 us  [swap(): lax.ppermute(message, 'context', [(i, i ^ span) for i in range(size)])]
  transfers between devices with their start and end apart: 4 -> 4, of which waited for: 1 -> 1; matrix products, arithmetic and copies ran while one was open for 0% -> 0% of each run, Pallas kernels for 41% -> 43%
where the time goes in v4:
time: 18.1 us; the launch traced here: 17.9 us
  Pallas kernels  10.9 us (60%)
  starting transfers between devices  6.59 us (36%)
  waiting for transfers between devices  0.4 us (2%)
    pallas_call x9, Pallas kernels, call(): pl.pallas_call(kernel, in_specs=in_specs, out_specs=[VM] * len(outs) if o...  10.9 us
    ppermute x4, starting transfers between devices, swap(): lax.ppermute(message, 'context', [(i, i ^ span) for i in range(size)])  6.59 us
    ppermute x4, waiting for transfers between devices, swap(): lax.ppermute(message, 'context', [(i, i ^ span) for i in range(size)])  0.4 us
  transfers between devices with their start and end apart: 4, of which 1 were waited for; matrix products, arithmetic and copies ran while one was open for 0% of the time, Pallas kernels for 43%

profile of v4, /device:TPU:0, one launch (start us, length us, event | category | flops | bytes accessed | tf_op | source)
XLA Modules:
  0.0 17.9 jit_solution(11358593520025784378)
XLA Ops:
  0.0 3.1 %states.2 = (f32[256,8,128]{2,1,0:T(8,128)S(1)}, f32[16,16,8,128]{3,2,1,0:T(8,128)S(1)}, f32[16,8,128]{2,1,0:T(8,128)S(1)}, f32[42,8,128]{2,1,0:T(8,128)S(1)}, b...) custom-call(bf16[3,256,2048]{2,1,0:T(8,128)(2,1)} %bitcast.4, ...), custom_call_target="tpu_custom_call" | custom-call | flops 12582912 | bytes 1048576 | tf_op jit(solution)/shard_map/states/pallas_call | solution.py:432
  3.1 3.1 %collective-permute-start.1 = (bf16[18,16,128]{2,1,0:T(8,128)(2,1)S(1)}, bf16[18,16,128]{2,1,0:T(8,128)(2,1)S(1)}, u32[]{:S(2)}, u32[]{:S(2)}) collective-permute-start(bf16[18,16,128]{2,1,0:T(8,128)(2,1)S(1)} %get-tuple-element.48), channel_id=1, source_target_pairs={{0,4},{4,0},{8,12},{12,8},{1,5},{5,1},{9,13},{13,9},{2,6},{6,2},{1... | collective-permute-start | bytes 221192 | tf_op jit(solution)/shard_map/ppermute | solution.py:463
  6.2 1.9 %states.3 = (f32[256,8,128]{2,1,0:T(8,128)S(1)}, f32[16,16,8,128]{3,2,1,0:T(8,128)S(1)}, f32[16,8,128]{2,1,0:T(8,128)S(1)}, f32[42,8,128]{2,1,0:T(8,128)S(1)}, bf16[8,16,128]{2,1,0:T(8,128)(2,1)S(1)}) custom-call(f32[16,2048]{1,0:T(8,128)S(1)} %get-tuple-element.41.refs_0_, f32[3,3,2048]{2,1,0:T(4,128)S(1)} %get-tuple-element.42.refs_1_, ...), custom_call_target="tpu_custom_call" | custom-call | flops 12582912 | bytes 1048576 | tf_op jit(solution)/shard_map/states/pallas_call | solution.py:432
  8.1 0.1 collective-permute-start
  8.2 1.9 %near.2 = (f32[256,8,128]{2,1,0:T(8,128)S(1)}, f32[256,8,128]{2,1,0:T(8,128)S(1)}, f32[256,8,128]{2,1,0:T(8,128)S(1)}, f32[256,8,128]{2,1,0:T(8,128)S(1)}) custom-call(bf16[3,256,2048]{2,1,0:T(8,128)(2,1)S(1)} %get-tuple-element.40.refs_4_.refs_0_, f32[42,8,128]{2,1,0:T(8,128)S(1)} %get-tuple-element.50.refs_1_.refs_4_.refs_8_.refs_2_.refs_3_.refs_6_, ...), custom_call_target="tpu_custom_call" | custom-call | flops 12582912 | bytes 1048576 | tf_op jit(solution)/shard_map/near/pallas_call | solution.py:432
  10.1 0.0 collective-permute-done.1.refs_2_.refs_3_
  10.1 0.5 %merge.2 = (bf16[14,16,128]{2,1,0:T(8,128)(2,1)S(1)}, f32[16,8,128]{2,1,0:T(8,128)S(1)}, f32[6,8,128]{2,1,0:T(8,128)S(1)}, f32[2,10,8,128]{3,2,1,0:T(8,128)S(1)}...) custom-call(f32[16,8,128]{2,1,0:T(8,128)S(1)} %get-tuple-element.56.refs_0_, ...), custom_call_target="tpu_custom_call" | custom-call | flops 1048576 | bytes 1048576 | tf_op jit(solution)/shard_map/merge/pallas_call | solution.py:432
  10.6 1.1 %collective-permute-start.3 = (bf16[14,16,128]{2,1,0:T(8,128)(2,1)S(1)}, bf16[14,16,128]{2,1,0:T(8,128)(2,1)S(1)}, u32[]{:S(2)}, u32[]{:S(2)}) collective-permute-start(bf16[14,16,128]{2,1,0:T(8,128)(2,1)S(1)} %get-tuple-element.67), channel_id=1, source_target_pairs={{0,8},{4,12},{8,0},{12,4},{1,9},{5,13},{9,1},{13,5},{2,10},{6,14},... | collective-permute-start | bytes 172040 | tf_op jit(solution)/shard_map/ppermute | solution.py:463
  11.7 0.4 %collective-permute-done.refs_2_ = bf16[8,16,128]{2,1,0:T(8,128)(2,1)S(1)} collective-permute-done((bf16[8,16,128]{2,1,0:T(8,128)(2,1)S(1)}, bf16[8,16,128]{2,1,0:T(8,128)(2,1)S(1)}, u32[]{:S(2)}, u32[]{:S(2)}) %collective-permute-start) | collective-permute-done | bytes 32800 | tf_op jit(solution)/shard_map/ppermute | solution.py:463
  12.1 0.4 %merge.3 = (bf16[8,16,128]{2,1,0:T(8,128)(2,1)S(1)}, f32[16,8,128]{2,1,0:T(8,128)S(1)}, f32[6,8,128]{2,1,0:T(8,128)S(1)}, bf16[256,1024]{1,0:T(8,128)(2,1)S(1)}, f32[16,8,128]{2,1,0:T(8,128)S(1)}) custom-call(f32[16,8,128]{2,1,0:T(8,128)S(1)} %get-tuple-element.45.refs_0_, f32[2,10,8,128]{3,2,1,0:T(8,128)S(1)} %get-tuple-element.46.refs_1_.refs_9_.refs_4_.own_edges, ...), custom_call_target="tpu_custom_call" | custom-call | flops 1048576 | bytes 1048576 | tf_op jit(solution)/shard_map/merge/pallas_call | solution.py:432
  12.5 2.3 %collective-permute-start.2 = (bf16[8,16,128]{2,1,0:T(8,128)(2,1)S(1)}, bf16[8,16,128]{2,1,0:T(8,128)(2,1)S(1)}, u32[]{:S(2)}, u32[]{:S(2)}) collective-permute-start(bf16[8,16,128]{2,1,0:T(8,128)(2,1)S(1)} %get-tuple-element.66), channel_id=1, source_target_pairs={{0,8},{4,12},{8,0},{12,4},{1,9},{5,13},{9,1},{13,5},{2,10},{6,14},... | collective-permute-start | bytes 98312 | tf_op jit(solution)/shard_map/ppermute | solution.py:463
  14.8 3.0 %early.1.refs_11_ = bf16[256,2048]{1,0:T(8,128)(2,1)} custom-call(f32[2,10,8,128]{3,2,1,0:T(8,128)S(1)} %get-tuple-element.46.refs_1_.refs_9_.refs_4_.own_edges, bf16[256,1024]{1,0:T(8,128)(2,1)S(1)} %get-tuple-element.70.refs_0_, bf16[256,1024]{1,0:T(8,128)(2,1)S(1)} %get-tuple-element.71.refs_1_, f32[16,8,128]{2,1,0:T(8,128)S(1)} %get-tuple-element.72.refs_2_, ...), custom_call_target="tpu_custom_call" | custom-call | flops 20971520 | bytes 1048576 | tf_op jit(solution)/shard_map/early/pallas_call | solution.py:432
  17.8 0.0 collective-permute-done.3.refs_8_.refs_9_
  17.9 0.0 collective-permute-done.2.refs_8_
  17.9 0.1 late.3
  (2 shorter events, 0.0 us)
Async XLA Ops:
  3.1 7.0 %collective-permute-start.1 = (bf16[18,16,128]{2,1,0:T(8,128)(2,1)S(1)}, bf16[18,16,128]{2,1,0:T(8,128)(2,1)S(1)}, u32[]{:S(2)}, u32[]{:S(2)}) collective-permute-start(bf16[18,16,128]{2,1,0:T(8,128)(2,1)S(1)} %get-tuple-element.48), channel_id=1, source_target_pairs={{0,4},{4,0},{8,12},{12,8},{1,5},{5,1},{9,13},{13,9},{2,6},{6,2},{1... | collective-permute-start | bytes 221192 | tf_op jit(solution)/shard_map/ppermute | solution.py:463
  8.1 4.0 %collective-permute-start = (bf16[8,16,128]{2,1,0:T(8,128)(2,1)S(1)}, bf16[8,16,128]{2,1,0:T(8,128)(2,1)S(1)}, u32[]{:S(2)}, u32[]{:S(2)}) collective-permute-start(bf16[8,16,128]{2,1,0:T(8,128)(2,1)S(1)} %get-tuple-element.47), channel_id=1, source_target_pairs={{0,4},{4,0},{8,12},{12,8},{1,5},{5,1},{9,13},{13,9},{2,6},{6,2},{1... | collective-permute-start | bytes 98312 | tf_op jit(solution)/shard_map/ppermute | solution.py:463
  10.6 7.3 %collective-permute-start.3 = (bf16[14,16,128]{2,1,0:T(8,128)(2,1)S(1)}, bf16[14,16,128]{2,1,0:T(8,128)(2,1)S(1)}, u32[]{:S(2)}, u32[]{:S(2)}) collective-permute-start(bf16[14,16,128]{2,1,0:T(8,128)(2,1)S(1)} %get-tuple-element.67), channel_id=1, source_target_pairs={{0,8},{4,12},{8,0},{12,4},{1,9},{5,13},{9,1},{13,5},{2,10},{6,14},... | collective-permute-start | bytes 172040 | tf_op jit(solution)/shard_map/ppermute | solution.py:463
  12.5 5.3 %collective-permute-start.2 = (bf16[8,16,128]{2,1,0:T(8,128)(2,1)S(1)}, bf16[8,16,128]{2,1,0:T(8,128)(2,1)S(1)}, u32[]{:S(2)}, u32[]{:S(2)}) collective-permute-start(bf16[8,16,128]{2,1,0:T(8,128)(2,1)S(1)} %get-tuple-element.66), channel_id=1, source_target_pairs={{0,8},{4,12},{8,0},{12,4},{1,9},{5,13},{9,1},{13,5},{2,10},{6,14},... | collective-permute-start | bytes 98312 | tf_op jit(solution)/shard_map/ppermute | solution.py:463

commit v5 on v4

--- a/solution.py
+++ b/solution.py
@@ -13,7 +13,7 @@
 CHUNK = 16
 PIECE = 64
 STRIDE = CHUNK + 8
-EARLY = (4, 8)
+EARLY = (4, 6)
 HEAD = 4
 TAIL = 6
 
@@ -212,24 +212,50 @@
         for copy in tables[2:] + rest:
             copy.wait()
 
-    state_kernel(
-        0, rate_nat, taps_nat, residue_nat, bias_nat, natural,
-        kv_ref, states_ref, own_ref, tables_ref, ka, kb, va, vb, lambda n: pieces[n].wait(), wait_rest,
-    )
-    for g in range(groups):
-        edge_rows(natural, edges_ref, ka, g)
-    state = [own_ref[m] for m in range(own_ref.shape[0])]
-    pack(message_ref, state + tails_and_heads([[edges_ref[g, i] for i in range(TAIL + HEAD)] for g in range(groups)], True))
-
-
-def later_states_kernel(
-    g, rate_nat, taps_nat, residue_nat, bias_nat, natural, kv_ref, states_ref, own_ref, tables_ref, message_ref, *scratch
-):
-    state_kernel(
-        g, rate_nat, taps_nat, residue_nat, bias_nat, natural, kv_ref, states_ref, own_ref, tables_ref, *scratch,
-        lambda n: None, lambda: None,
-    )
-    pack(message_ref, [own_ref[m] for m in range(own_ref.shape[0])])
+
+    @pl.when(jnp.logical_not(is_last()))
+    def _():
+        state_kernel(
+            0, rate_nat, taps_nat, residue_nat, bias_nat, natural,
+            kv_ref, states_ref, own_ref, tables_ref, ka, kb, va, vb, lambda n: pieces[n].wait(), wait_rest,
+        )
+        for g in range(groups):
+            edge_rows(natural, edges_ref, ka, g)
+        state = [own_ref[m] for m in range(own_ref.shape[0])]
+        edges = [[edges_ref[g, i] for i in range(TAIL + HEAD)] for g in range(groups)]
+        pack(message_ref, state + tails_and_heads(edges, True))
+
+    @pl.when(is_last())
+    def _():
+        for copy in pieces:
+            copy.wait()
+        wait_rest()
+        message_ref[...] = jnp.zeros(message_ref.shape, BF16)
+
+
+def is_last():
+    return lax.axis_index("context") == lax.axis_size("context") - 1
+
+
+def later_states_kernel(g, inputs, before, own_edges, outs, scratch):
+    def states(group, refs):
+        state_kernel(group, *inputs, *refs, *scratch, lambda n: None, lambda: None)
+
+    if outs:
+
+        @pl.when(jnp.logical_not(is_last()))
+        def _():
+            states(g, outs[:4])
+            pack(outs[4], [outs[2][m] for m in range(outs[2].shape[0])])
+
+    @pl.when(is_last())
+    def _():
+        states(g - 1, before)
+        if own_edges is not None:
+            for group in range(own_edges.shape[0]):
+                edge_rows(inputs[-1], own_edges, scratch[0], group)
+        if outs:
+            outs[4][...] = jnp.zeros(outs[4].shape, BF16)
 
 
 def near_group(g, q_nat, tables_ref, kv_ref, near_ref, query_ref, taps, qa, qb):
@@ -475,16 +501,25 @@
         [turned] * 4 + [dma((4,)), dma((groups + 2,))], 4, 24 * work, in_specs=[HB] * 5,
     )
     made, message = [first], [first_message]
-    for g in range(1, groups):
-
-        def kernel(*refs, g=g):
-            later_states_kernel(g, *refs)
-
-        *later, later_message = call(
-            kernel, "states", [rates, taps, residues, biases, natural], state_types + [message_type(modes)], [turned] * 4, 4, 24 * work
+    inputs = [rates, taps, residues, biases, natural]
+    for g in range(1, groups + 1):
+        held = made[-1] + ([own_edges] if g == 1 else [])
+        outs = state_types + [message_type(modes)] if g < groups else []
+
+        def kernel(*refs, g=g, count=len(held), fresh=len(outs)):
+            ins, refs = refs[:5], refs[5 + count :]
+            before, outs, scratch = refs[:count], refs[count : count + fresh], refs[count + fresh :]
+            later_states_kernel(g, ins, before[:4], before[4] if g == 1 else None, outs, scratch)
+
+        results = call(
+            kernel, "states", inputs + held, state_types + ([vectors(groups, edge)] if g == 1 else []) + outs,
+            [turned] * 4, 4, 24 * work, aliases={5 + i: i for i in range(len(held))},
         )
-        made.append(later)
-        message.append(later_message)
+        made[-1] = list(results[:4])
+        own_edges = results[4] if g == 1 else own_edges
+        if outs:
+            made.append(list(results[len(held) : len(held) + 4]))
+            message.append(results[-1])
     key_value, states, own, tables = zip(*made)
 
     def near_all(early, after):

time: 18.1 us -> 17.9 us (0.989); the launches traced: 17.9 us -> 17.6 us
  starting transfers between devices: 6.59 us -> 5.78 us
  waiting for transfers between devices: 0.4 us -> 0.83 us
    ppermute x4, starting transfers between devices: 6.59 us -> 5.78 us  [swap(): lax.ppermute(message, 'context', [(i, i ^ span) for i in range(size)])]
    ppermute x4, waiting for transfers between devices: 0.4 us -> 0.83 us  [swap(): lax.ppermute(message, 'context', [(i, i ^ span) for i in range(size)])]
    pallas_call x9 -> x10, Pallas kernels: 10.9 us -> 10.9 us  [call(): pl.pallas_call(kernel, in_specs=in_specs, out_specs=[VM] * len(outs) if o...]
  transfers between devices with their start and end apart: 4 -> 4, of which waited for: 1 -> 2; matrix products, arithmetic and copies ran while one was open for 0% -> 0% of each run, Pallas kernels for 43% -> 44%
where the time goes in v5:
time: 17.9 us; the launch traced here: 17.6 us
  Pallas kernels  10.9 us (61%)
  starting transfers between devices  5.78 us (32%)
  waiting for transfers between devices  0.83 us (5%)
    pallas_call x10, Pallas kernels, call(): pl.pallas_call(kernel, in_specs=in_specs, out_specs=[VM] * len(outs) if o...  10.9 us
    ppermute x4, starting transfers between devices, swap(): lax.ppermute(message, 'context', [(i, i ^ span) for i in range(size)])  5.78 us
    ppermute x4, waiting for transfers between devices, swap(): lax.ppermute(message, 'context', [(i, i ^ span) for i in range(size)])  0.83 us
  transfers between devices with their start and end apart: 4, of which 2 were waited for; matrix products, arithmetic and copies ran while one was open for 0% of the time, Pallas kernels for 44%

profile of v5, /device:TPU:0, one launch (start us, length us, event | category | flops | bytes accessed | tf_op | source)
XLA Modules:
  0.0 17.6 jit_solution(17421850185200321355)
XLA Ops:
  0.0 3.1 %states.3 = (f32[256,8,128]{2,1,0:T(8,128)S(1)}, f32[16,16,8,128]{3,2,1,0:T(8,128)S(1)}, f32[16,8,128]{2,1,0:T(8,128)S(1)}, f32[42,8,128]{2,1,0:T(8,128)S(1)}, b...) custom-call(bf16[3,256,2048]{2,1,0:T(8,128)(2,1)} %bitcast.4, ...), custom_call_target="tpu_custom_call" | custom-call | flops 12582912 | bytes 1048576 | tf_op jit(solution)/shard_map/states/pallas_call | solution.py:458
  3.1 3.1 %collective-permute-start.1 = (bf16[18,16,128]{2,1,0:T(8,128)(2,1)S(1)}, bf16[18,16,128]{2,1,0:T(8,128)(2,1)S(1)}, u32[]{:S(2)}, u32[]{:S(2)}) collective-permute-start(bf16[18,16,128]{2,1,0:T(8,128)(2,1)S(1)} %get-tuple-element.66), channel_id=1, source_target_pairs={{0,4},{4,0},{8,12},{12,8},{1,5},{5,1},{9,13},{13,9},{2,6},{6,2},{1... | collective-permute-start | bytes 221192 | tf_op jit(solution)/shard_map/ppermute | solution.py:489
  6.2 1.9 %states.4 = (f32[256,8,128]{2,1,0:T(8,128)S(1)}, f32[16,16,8,128]{3,2,1,0:T(8,128)S(1)}, f32[16,8,128]{2,1,0:T(8,128)S(1)}, f32[42,8,128]{2,1,0:T(8,128)S(1)}, f...) custom-call(f32[16,2048]{1,0:T(8,128)S(1)} %get-tuple-element.50.ref, ...), custom_call_target="tpu_custom_call", output_to_operand_aliasing={{0}: (5, {}), {1}: (6, {}), {2}: (7, {}), {3}: (8, {}), {4}... | custom-call | flops 12582912 | bytes 1048576 | tf_op jit(solution)/shard_map/states/pallas_call | solution.py:458
  8.1 0.1 collective-permute-start
  8.2 1.9 %near.2 = (f32[256,8,128]{2,1,0:T(8,128)S(1)}, f32[256,8,128]{2,1,0:T(8,128)S(1)}, f32[256,8,128]{2,1,0:T(8,128)S(1)}, f32[256,8,128]{2,1,0:T(8,128)S(1)}) custom-call(bf16[3,256,2048]{2,1,0:T(8,128)(2,1)S(1)} %get-tuple-element.49.refs_4_.refs_0_, f32[42,8,128]{2,1,0:T(8,128)S(1)} %get-tuple-element.68.refs_1_.refs_4_.refs_8_.refs_2_.refs_3_.refs_6_, ...), custom_call_target="tpu_custom_call" | custom-call | flops 12582912 | bytes 1048576 | tf_op jit(solution)/shard_map/near/pallas_call | solution.py:458
  10.1 0.0 collective-permute-done.1.refs_2_.refs_3_
  10.1 0.5 %merge.2 = (bf16[14,16,128]{2,1,0:T(8,128)(2,1)S(1)}, f32[16,8,128]{2,1,0:T(8,128)S(1)}, f32[6,8,128]{2,1,0:T(8,128)S(1)}, f32[2,10,8,128]{3,2,1,0:T(8,128)S(1)}...) custom-call(f32[16,8,128]{2,1,0:T(8,128)S(1)} %get-tuple-element.74.refs_0_, ...), custom_call_target="tpu_custom_call" | custom-call | flops 1048576 | bytes 1048576 | tf_op jit(solution)/shard_map/merge/pallas_call | solution.py:458
  10.6 1.1 %collective-permute-start.3 = (bf16[14,16,128]{2,1,0:T(8,128)(2,1)S(1)}, bf16[14,16,128]{2,1,0:T(8,128)(2,1)S(1)}, u32[]{:S(2)}, u32[]{:S(2)}) collective-permute-start(bf16[14,16,128]{2,1,0:T(8,128)(2,1)S(1)} %get-tuple-element.85), channel_id=1, source_target_pairs={{0,8},{4,12},{8,0},{12,4},{1,9},{5,13},{9,1},{13,5},{2,10},{6,14},... | collective-permute-start | bytes 172040 | tf_op jit(solution)/shard_map/ppermute | solution.py:489
  11.7 0.4 %collective-permute-done.refs_2_ = bf16[8,16,128]{2,1,0:T(8,128)(2,1)S(1)} collective-permute-done((bf16[8,16,128]{2,1,0:T(8,128)(2,1)S(1)}, bf16[8,16,128]{2,1,0:T(8,128)(2,1)S(1)}, u32[]{:S(2)}, u32[]{:S(2)}) %collective-permute-start) | collective-permute-done | bytes 32800 | tf_op jit(solution)/shard_map/ppermute | solution.py:489
  12.1 0.3 %merge.3 = (bf16[8,16,128]{2,1,0:T(8,128)(2,1)S(1)}, f32[16,8,128]{2,1,0:T(8,128)S(1)}, f32[6,8,128]{2,1,0:T(8,128)S(1)}, bf16[256,1024]{1,0:T(8,128)(2,1)S(1)}, f32[16,8,128]{2,1,0:T(8,128)S(1)}) custom-call(f32[16,8,128]{2,1,0:T(8,128)S(1)} %get-tuple-element.63.refs_0_, f32[2,10,8,128]{3,2,1,0:T(8,128)S(1)} %get-tuple-element.64.refs_1_.refs_9_.refs_4_.own_edges, ...), custom_call_target="tpu_custom_call" | custom-call | flops 1048576 | bytes 1048576 | tf_op jit(solution)/shard_map/merge/pallas_call | solution.py:458
  12.4 1.5 %collective-permute-start.2 = (bf16[8,16,128]{2,1,0:T(8,128)(2,1)S(1)}, bf16[8,16,128]{2,1,0:T(8,128)(2,1)S(1)}, u32[]{:S(2)}, u32[]{:S(2)}) collective-permute-start(bf16[8,16,128]{2,1,0:T(8,128)(2,1)S(1)} %get-tuple-element.84), channel_id=1, source_target_pairs={{0,8},{4,12},{8,0},{12,4},{1,9},{5,13},{9,1},{13,5},{2,10},{6,14},... | collective-permute-start | bytes 98312 | tf_op jit(solution)/shard_map/ppermute | solution.py:489
  13.9 3.2 %early.1.refs_11_ = bf16[256,2048]{1,0:T(8,128)(2,1)} custom-call(f32[2,10,8,128]{3,2,1,0:T(8,128)S(1)} %get-tuple-element.64.refs_1_.refs_9_.refs_4_.own_edges, bf16[256,1024]{1,0:T(8,128)(2,1)S(1)} %get-tuple-element.88.refs_0_, bf16[256,1024]{1,0:T(8,128)(2,1)S(1)} %get-tuple-element.89.refs_1_, f32[16,8,128]{2,1,0:T(8,128)S(1)} %get-tuple-element.90.refs_2_, ...), custom_call_target="tpu_custom_call" | custom-call | flops 20971520 | bytes 1048576 | tf_op jit(solution)/shard_map/early/pallas_call | solution.py:458
  17.0 0.0 collective-permute-done.3.refs_8_.refs_9_
  17.1 0.4 %collective-permute-done.2.refs_8_ = bf16[8,16,128]{2,1,0:T(8,128)(2,1)S(1)} collective-permute-done((bf16[8,16,128]{2,1,0:T(8,128)(2,1)S(1)}, bf16[8,16,128]{2,1,0:T(8,128)(2,1)S(1)}, u32[]{:S(2)}, u32[]{:S(2)}) %collective-permute-start.2) | collective-permute-done | bytes 32800 | tf_op jit(solution)/shard_map/ppermute | solution.py:489
  17.5 0.1 late.3
  (3 shorter events, 0.0 us)
Async XLA Ops:
  3.1 7.0 %collective-permute-start.1 = (bf16[18,16,128]{2,1,0:T(8,128)(2,1)S(1)}, bf16[18,16,128]{2,1,0:T(8,128)(2,1)S(1)}, u32[]{:S(2)}, u32[]{:S(2)}) collective-permute-start(bf16[18,16,128]{2,1,0:T(8,128)(2,1)S(1)} %get-tuple-element.66), channel_id=1, source_target_pairs={{0,4},{4,0},{8,12},{12,8},{1,5},{5,1},{9,13},{13,9},{2,6},{6,2},{1... | collective-permute-start | bytes 221192 | tf_op jit(solution)/shard_map/ppermute | solution.py:489
  8.1 4.0 %collective-permute-start = (bf16[8,16,128]{2,1,0:T(8,128)(2,1)S(1)}, bf16[8,16,128]{2,1,0:T(8,128)(2,1)S(1)}, u32[]{:S(2)}, u32[]{:S(2)}) collective-permute-start(bf16[8,16,128]{2,1,0:T(8,128)(2,1)S(1)} %get-tuple-element.65), channel_id=1, source_target_pairs={{0,4},{4,0},{8,12},{12,8},{1,5},{5,1},{9,13},{13,9},{2,6},{6,2},{1... | collective-permute-start | bytes 98312 | tf_op jit(solution)/shard_map/ppermute | solution.py:489
  10.6 6.4 %collective-permute-start.3 = (bf16[14,16,128]{2,1,0:T(8,128)(2,1)S(1)}, bf16[14,16,128]{2,1,0:T(8,128)(2,1)S(1)}, u32[]{:S(2)}, u32[]{:S(2)}) collective-permute-start(bf16[14,16,128]{2,1,0:T(8,128)(2,1)S(1)} %get-tuple-element.85), channel_id=1, source_target_pairs={{0,8},{4,12},{8,0},{12,4},{1,9},{5,13},{9,1},{13,5},{2,10},{6,14},... | collective-permute-start | bytes 172040 | tf_op jit(solution)/shard_map/ppermute | solution.py:489
  12.4 5.1 %collective-permute-start.2 = (bf16[8,16,128]{2,1,0:T(8,128)(2,1)S(1)}, bf16[8,16,128]{2,1,0:T(8,128)(2,1)S(1)}, u32[]{:S(2)}, u32[]{:S(2)}) collective-permute-start(bf16[8,16,128]{2,1,0:T(8,128)(2,1)S(1)} %get-tuple-element.84), channel_id=1, source_target_pairs={{0,8},{4,12},{8,0},{12,4},{1,9},{5,13},{9,1},{13,5},{2,10},{6,14},... | collective-permute-start | bytes 98312 | tf_op jit(solution)/shard_map/ppermute | solution.py:489

commit v6 on v5

--- a/solution.py
+++ b/solution.py
@@ -186,35 +186,31 @@
 ):
     _, tokens, channels = natural.shape
     groups = channels // GROUP
-
-    def fetch(i, *where):
-        return pltpu.make_async_copy(streams.at[where], natural.at[where], stream_sems.at[i])
-
     keys_values = pl.ds(1, 2)
     pieces = [
-        fetch(0, keys_values, pl.ds(0, PIECE), columns(0)),
-        fetch(1, keys_values, pl.ds(PIECE, tokens - PIECE), columns(0)),
+        fetch(streams, natural, stream_sems.at[0], keys_values, pl.ds(0, PIECE), columns(0)),
+        fetch(streams, natural, stream_sems.at[1], keys_values, pl.ds(PIECE, tokens - PIECE), columns(0)),
     ]
-    rest = [fetch(2, pl.ds(0, 1), slice(None), columns(0))]
-    rest += [fetch(2 + g, slice(None), slice(None), columns(g)) for g in range(1, groups)]
+    rest = other_inputs(streams, natural, stream_sems, 2)
     tables = [
         pltpu.make_async_copy(src, dst, table_sems.at[i])
         for i, (src, dst) in enumerate(
             [(rate_hbm, rate_nat), (taps_hbm, taps_nat), (residue_hbm, residue_nat), (bias_hbm, bias_nat)]
         )
     ]
-    for copy in tables[:2] + pieces + rest + tables[2:]:
+    for copy in tables[:2] + pieces + tables[2:]:
         copy.start()
-    for copy in tables[:2]:
-        copy.wait()
 
     def wait_rest():
         for copy in tables[2:] + rest:
             copy.wait()
 
-
     @pl.when(jnp.logical_not(is_last()))
     def _():
+        for copy in rest:
+            copy.start()
+        for copy in tables[:2]:
+            copy.wait()
         state_kernel(
             0, rate_nat, taps_nat, residue_nat, bias_nat, natural,
             kv_ref, states_ref, own_ref, tables_ref, ka, kb, va, vb, lambda n: pieces[n].wait(), wait_rest,
@@ -227,17 +223,28 @@
 
     @pl.when(is_last())
     def _():
-        for copy in pieces:
+        for copy in tables + pieces:
             copy.wait()
-        wait_rest()
         message_ref[...] = jnp.zeros(message_ref.shape, BF16)
+
+
+def fetch(streams, natural, sem, *where):
+    return pltpu.make_async_copy(streams.at[where], natural.at[where], sem)
+
+
+def other_inputs(streams, natural, sems, first):
+    groups = natural.shape[2] // GROUP
+    copies = [fetch(streams, natural, sems.at[first], pl.ds(0, 1), slice(None), columns(0))]
+    for g in range(1, groups):
+        copies.append(fetch(streams, natural, sems.at[first + g], slice(None), slice(None), columns(g)))
+    return copies
 
 
 def is_last():
     return lax.axis_index("context") == lax.axis_size("context") - 1
 
 
-def later_states_kernel(g, inputs, before, own_edges, outs, scratch):
+def later_states_kernel(g, inputs, before, own_edges, streams, sems, outs, scratch):
     def states(group, refs):
         state_kernel(group, *inputs, *refs, *scratch, lambda n: None, lambda: None)
 
@@ -250,8 +257,13 @@
 
     @pl.when(is_last())
     def _():
+        rest = other_inputs(streams, inputs[-1], sems, 0) if g == 1 else []
+        for copy in rest:
+            copy.start()
         states(g - 1, before)
-        if own_edges is not None:
+        for copy in rest:
+            copy.wait()
+        if g == 1:
             for group in range(own_edges.shape[0]):
                 edge_rows(inputs[-1], own_edges, scratch[0], group)
         if outs:
@@ -424,6 +436,11 @@
     return (lax.axis_index("context") & span) == 0
 
 
+def is_first(span):
+    rank = lax.axis_index("context")
+    return is_early(span) & ((rank & (span // 2)) == 0)
+
+
 def emit_known(which, g, fixed, edges_ref, entering_ref, rim_ref, out_ref, scratch, piece_done):
     entering = [entering_ref[m] for m in range(entering_ref.shape[0])]
     rim = [rim_ref[i] for i in range(TAIL)]
@@ -475,7 +492,7 @@
     chunks, pieces = tokens // CHUNK, tokens // PIECE
     size = lax.axis_size("context")
     vector = (SUB, LANES)
-    turned = pltpu.VMEM((SUB * STRIDE, LANES), F32)
+    turned = pltpu.VMEM(((SUB + 1) * STRIDE, LANES), F32)
     dma = pltpu.SemaphoreType.DMA
     work = tokens * channels
 
@@ -494,57 +511,66 @@
         pltpu.VMEM((modes, channels), F32), pltpu.VMEM((3, 3, channels), F32), pltpu.VMEM((modes, channels), F32),
         vectors(groups), pltpu.VMEM((3, tokens, channels), BF16),
     ]
+    by_stream = streams.transpose(1, 0, 2)
     *first, first_message, own_edges, rates, taps, residues, biases, natural = call(
         first_states_kernel, "states",
-        [streams.transpose(1, 0, 2), short_filter, decay_rate.T, residue.T, bias.reshape((groups,) + vector)],
+        [by_stream, short_filter, decay_rate.T, residue.T, bias.reshape((groups,) + vector)],
         state_types + [message_type(modes + groups * edge), vectors(groups, edge)] + input_types,
         [turned] * 4 + [dma((4,)), dma((groups + 2,))], 4, 24 * work, in_specs=[HB] * 5,
     )
     made, message = [first], [first_message]
-    inputs = [rates, taps, residues, biases, natural]
-    for g in range(1, groups + 1):
-        held = made[-1] + ([own_edges] if g == 1 else [])
+    def state_slot(g, after=()):
+        nonlocal own_edges, natural
+        held = made[-1] + ([own_edges, natural] if g == 1 else [])
         outs = state_types + [message_type(modes)] if g < groups else []
+        ins = [rates, taps, residues, biases] + ([by_stream] if g == 1 else [natural])
 
         def kernel(*refs, g=g, count=len(held), fresh=len(outs)):
-            ins, refs = refs[:5], refs[5 + count :]
+            ins, refs = refs[:5], refs[5 + count + len(after) :]
             before, outs, scratch = refs[:count], refs[count : count + fresh], refs[count + fresh :]
-            later_states_kernel(g, ins, before[:4], before[4] if g == 1 else None, outs, scratch)
+            if g == 1:
+                later_states_kernel(g, ins[:4] + (before[5],), before[:4], before[4], ins[4], scratch[4], outs, scratch[:4])
+            else:
+                later_states_kernel(g, ins, before, None, None, None, outs, scratch)
 
         results = call(
-            kernel, "states", inputs + held, state_types + ([vectors(groups, edge)] if g == 1 else []) + outs,
-            [turned] * 4, 4, 24 * work, aliases={5 + i: i for i in range(len(held))},
+            kernel, "states", ins + held + list(after),
+            state_types + ([vectors(groups, edge), pltpu.VMEM((3, tokens, channels), BF16)] if g == 1 else []) + outs,
+            [turned] * 4 + ([dma((groups,))] if g == 1 else []), 4, 24 * work,
+            in_specs=[VM] * 4 + [HB if g == 1 else VM] + [VM] * (len(held) + len(after)), aliases={5 + i: i for i in range(len(held))},
         )
         made[-1] = list(results[:4])
-        own_edges = results[4] if g == 1 else own_edges
+        if g == 1:
+            own_edges, natural = results[4:6]
         if outs:
             made.append(list(results[len(held) : len(held) + 4]))
             message.append(results[-1])
-    key_value, states, own, tables = zip(*made)
-
-    def near_all(early, after):
+    for g in range(1, groups):
+        state_slot(g)
+
+    def near_all(condition, after, held):
         def kernel(*refs):
             natural, refs = refs[0], refs[1 + len(after) :]
-            ins, outs, scratch = refs[: 2 * groups], refs[2 * groups : 4 * groups], refs[4 * groups :]
-
-            @pl.when(is_early(size // 2) == early)
+            ins, refs = refs[: 2 * groups], refs[2 * groups + len(held) :]
+            outs, scratch = refs[: 2 * groups], refs[2 * groups :]
+
+            @pl.when(condition())
             def _():
                 for g in range(groups):
                     near_group(g, natural.at[0], *ins[2 * g : 2 * g + 2], *outs[2 * g : 2 * g + 2], *scratch)
 
-        operands = sum([[tables[g], key_value[g]] for g in range(groups)], [])
+        operands = [natural] + after + sum([[made[g][3], made[g][0]] for g in range(groups)], [])
         outs = call(
-            kernel, "near", [natural] + after + operands, [vectors(tokens)] * (2 * groups),
-            [vectors(CHUNK), turned, turned], 4, 24 * work,
+            kernel, "near", operands + held, [vectors(tokens)] * (2 * groups), [vectors(CHUNK), turned, turned], 4, 24 * work,
+            aliases={len(operands) + i: i for i in range(len(held))},
         )
-        return [list(outs[2 * g : 2 * g + 2]) for g in range(groups)]
+        return list(outs)
 
     half = pltpu.VMEM((tokens, GROUP), BF16)
     emit_scratch = [vectors(modes), vectors(4), turned, turned]
 
-    merged, edges = list(own), own_edges
+    merged, edges = [m[2] for m in made], own_edges
     entering, rim = [None] * groups, [None] * groups
-    begun, begun_state = [], []
     span = 1
     while True:
         got = [swap(message[g], span) for g in range(groups)]
@@ -552,63 +578,67 @@
             break
         last, first = 4 * span >= size, entering[0] is None
         if first:
-            near = near_all(True, [])
+            near = near_all(lambda: is_first(size // 2), [], [])
         old_edges = edges
         for g in range(groups):
+            if first and g == 1:
+                state_slot(groups, [rim[0]])
+                near = near_all(lambda: is_early(size // 2) & jnp.logical_not(is_first(size // 2)), [rim[0]], near)
             part = range(EARLY[g - 1] if g else 0, EARLY[g]) if last and g < len(EARLY) else range(0)
-            early = []
+            early, held = [], []
             if part:
-                early = [*near[0], states[0], tables[0], own_edges] + ([entering[0], rim[0], begun_state[-1]] if g else [])
-            operands = [merged[g], old_edges, got[g], got[0], tables[g]] + ([] if first else [entering[g], rim[g]])
+                early = [*near[:2], made[0][1], made[0][3], own_edges] + ([entering[0], rim[0]] if g else [])
+                held = [begun, begun_state] if g else []
+            operands = [merged[g], old_edges, got[g], got[0], made[g][3]] + ([] if first else [entering[g], rim[g]])
             count = modes + (groups * (TAIL if last else edge) if g == 0 else 0)
             outs = [message_type(count), vectors(modes), vectors(TAIL)]
             outs += [] if last else [vectors(modes)]
             outs += [vectors(groups, edge)] if g == 0 else []
             outs += [half, vectors(modes)] if part else []
 
-            def kernel(*refs, g=g, span=span, last=last, first=first, part=part, extra=len(early), results=len(outs)):
+            def kernel(*refs, g=g, span=span, last=last, first=first, part=part, counts=(len(early), len(held), len(outs))):
                 refs = list(refs)
                 ins = [refs.pop(0) for _ in range(5)] + ([None, None] if first else [refs.pop(0) for _ in range(2)])
-                more = [refs.pop(0) for _ in range(extra)]
-                produced = [refs.pop(0) for _ in range(results)]
+                more, _, produced = ([refs.pop(0) for _ in range(n)] for n in counts)
                 state_out = None if last else produced[3]
                 edges_out = produced[3 if last else 4] if g == 0 else None
                 merge_group(span, tokens, g, last, *ins, *produced[:3], state_out, edges_out)
+
+                def emit(which):
+                    known = more[5:7] if g else produced[1:3]
+                    emit_known(which, 0, more[:4], more[4], *known, produced[-2], [produced[-1]] + refs, lambda n: None)
+
                 if part:
-
-                    @pl.when(is_early(2 * span))
-                    def _():
-                        out_ref, state_ref = produced[-2:]
-                        for m in range(modes if g else 0):
-                            state_ref[m] = more[7][m]
-                        known = more[5:7] if g else produced[1:3]
-                        emit_known(part, 0, more[:4], more[4], *known, out_ref, [state_ref] + refs, lambda n: None)
-
-            made = list(call(kernel, "merge", operands + early, outs, emit_scratch if part else [], 4, 2**20))
-            message[g], entering[g], rim[g] = made[:3]
+                    pl.when(is_first(2 * span))(lambda: emit(part))
+                if part and g == 1:
+                    pl.when(is_early(2 * span) & jnp.logical_not(is_first(2 * span)))(lambda: emit(range(part.stop)))
+
+            results = list(
+                call(
+                    kernel, "merge", operands + early + held, outs, emit_scratch if part else [], 4, 2**20,
+                    aliases={len(operands) + len(early) + i: len(outs) - 2 + i for i in range(len(held))},
+                )
+            )
+            message[g], entering[g], rim[g] = results[:3]
             if not last:
-                merged[g] = made[3]
+                merged[g] = results[3]
             if g == 0:
-                edges = made[3 if last else 4]
+                edges = results[3 if last else 4]
             if part:
-                begun.append((pl.ds(part.start * CHUNK, len(part) * CHUNK), made[-2]))
-                begun_state.append(made[-1])
+                begun, begun_state = results[-2:]
         span *= 2
 
     out_type = pltpu.HBM((tokens, channels), BF16)
     pair = [[entering[g], rim[g]] for g in range(groups)]
-    begin = EARLY[len(begun) - 1] if begun else 0
-
-    def kernel(own_edges, *refs):
-        refs = list(refs)
-        ready = [refs.pop(0) for _ in begun]
-        begun_state = refs.pop(0) if begun else None
+    begin = EARLY[-1]
+
+    def kernel(own_edges, begun, begun_state, *refs):
         ins, refs = [refs[i * 6 : i * 6 + 6] for i in range(groups)], refs[groups * 6 :]
         out_hbm, out_refs, state, scratch = refs[0], refs[1 : 1 + groups], refs[1 + groups], refs[2 + groups : 6 + groups]
 
         @pl.when(is_early(span))
         def _():
-            for m in range(modes if begun else 0):
+            for m in range(modes):
                 state[m] = begun_state[m]
             for g in range(groups - 1):
                 which = range(0 if g else begin, chunks)
@@ -617,20 +647,20 @@
             def emit(out, piece_done):
                 emit_known(range(chunks), groups - 1, ins[-1][:4], own_edges, *ins[-1][4:], out, [state, *scratch], piece_done)
 
-            done = [(rows, 0, buffer) for (rows, _), buffer in zip(begun, ready)]
-            done += [(pl.ds(begin * CHUNK, tokens - begin * CHUNK), 0, out_refs[0])]
+            done = [(pl.ds(0, begin * CHUNK), 0, begun), (pl.ds(begin * CHUNK, tokens - begin * CHUNK), 0, out_refs[0])]
             done += [(pl.ds(0, tokens), g, out_refs[g]) for g in range(1, groups - 1)]
             emit_out(emit, done, out_hbm, out_refs[-1], *refs[6 + groups :])
 
+    def fixed_of():
+        return [[*near[2 * g : 2 * g + 2], made[g][1], made[g][3]] for g in range(groups)]
+
     out = call(
-        kernel, "early",
-        [own_edges] + [buffer for _, buffer in begun] + begun_state[-1:]
-        + sum([[*near[g], states[g], tables[g], *pair[g]] for g in range(groups)], []),
-        [out_type], [half] * groups + [vectors(modes)] + emit_scratch + [dma((groups + 1,)), dma((pieces,))],
+        kernel, "early", [own_edges, begun, begun_state] + sum([f + p for f, p in zip(fixed_of(), pair)], []),
+        [out_type], [half] * groups + [vectors(modes)] + emit_scratch + [dma((groups,)), dma((pieces,))],
         4, 40 * work, out_specs=[HB],
     )[0]
-    near = near_all(False, [entering[-1]])
-    fixed = [[*near[g], states[g], tables[g]] for g in range(groups)]
+    near = near_all(lambda: jnp.logical_not(is_early(span)), [entering[-1]], [])
+    fixed = fixed_of()
     halves = []
     for g in range(groups):
         final = g + 1 == groups

time: 17.9 us -> 17.6 us (0.983)
    pallas_call x10 -> x11, Pallas kernels: 10.9 us -> 10.8 us  [call(): pl.pallas_call(kernel, in_specs=in_specs, out_specs=[VM] * len(outs) if o...]
where the time goes in v6:
time: 17.6 us; the launch traced here: 17.3 us
  Pallas kernels  10.8 us (61%)
  starting transfers between devices  5.65 us (32%)
  waiting for transfers between devices  0.77 us (4%)
    pallas_call x11, Pallas kernels, call(): pl.pallas_call(kernel, in_specs=in_specs, out_specs=[VM] * len(outs) if o...  10.8 us
    ppermute x4, starting transfers between devices, swap(): lax.ppermute(message, 'context', [(i, i ^ span) for i in range(size)])  5.65 us
    ppermute x4, waiting for transfers between devices, swap(): lax.ppermute(message, 'context', [(i, i ^ span) for i in range(size)])  0.77 us
  transfers between devices with their start and end apart: 4, of which 2 were waited for; matrix products, arithmetic and copies ran while one was open for 0% of the time, Pallas kernels for 44%

profile of v6, /device:TPU:0, one launch (start us, length us, event | category | flops | bytes accessed | tf_op | source)
XLA Modules:
  0.0 17.3 jit_solution(14703651089744734311)
XLA Ops:
  0.0 3.1 %states.3 = (f32[256,8,128]{2,1,0:T(8,128)S(1)}, f32[16,16,8,128]{3,2,1,0:T(8,128)S(1)}, f32[16,8,128]{2,1,0:T(8,128)S(1)}, f32[42,8,128]{2,1,0:T(8,128)S(1)}, b...) custom-call(bf16[3,256,2048]{2,1,0:T(8,128)(2,1)} %bitcast.4, ...), custom_call_target="tpu_custom_call" | custom-call | flops 12582912 | bytes 1048576 | tf_op jit(solution)/shard_map/states/pallas_call | solution.py:475
  3.1 3.1 %collective-permute-start.1 = (bf16[18,16,128]{2,1,0:T(8,128)(2,1)S(1)}, bf16[18,16,128]{2,1,0:T(8,128)(2,1)S(1)}, u32[]{:S(2)}, u32[]{:S(2)}) collective-permute-start(bf16[18,16,128]{2,1,0:T(8,128)(2,1)S(1)} %get-tuple-element.67), channel_id=1, source_target_pairs={{0,4},{4,0},{8,12},{12,8},{1,5},{5,1},{9,13},{13,9},{2,6},{6,2},{1... | collective-permute-start | bytes 221192 | tf_op jit(solution)/shard_map/ppermute | solution.py:506
  6.2 1.9 %states.4 = (f32[256,8,128]{2,1,0:T(8,128)S(1)}, f32[16,16,8,128]{3,2,1,0:T(8,128)S(1)}, f32[16,8,128]{2,1,0:T(8,128)S(1)}, f32[42,8,128]{2,1,0:T(8,128)S(1)}, f...) custom-call(f32[16,2048]{1,0:T(8,128)S(1)} %get-tuple-element.53.ref, ...), custom_call_target="tpu_custom_call", output_to_operand_aliasing={{0}: (5, {}), {1}: (6, {}), {2}: (7, {}), {3}: (8, {}), {4}... | custom-call | flops 12582912 | bytes 1048576 | tf_op jit(solution)/shard_map/states/pallas_call | solution.py:475
  8.1 0.1 collective-permute-start
  8.2 1.8 %near.3 = (f32[256,8,128]{2,1,0:T(8,128)S(1)}, f32[256,8,128]{2,1,0:T(8,128)S(1)}, f32[256,8,128]{2,1,0:T(8,128)S(1)}, f32[256,8,128]{2,1,0:T(8,128)S(1)}) custom-call(bf16[3,256,2048]{2,1,0:T(8,128)(2,1)S(1)} %get-tuple-element.63.refs_0_.refs_4_, f32[42,8,128]{2,1,0:T(8,128)S(1)} %get-tuple-element.72.refs_1_.refs_4_.refs_8_.refs_2_.refs_3_, ...), custom_call_target="tpu_custom_call" | custom-call | flops 12582912 | bytes 1048576 | tf_op jit(solution)/shard_map/near/pallas_call | solution.py:475
  10.1 0.0 collective-permute-done.1.refs_2_.refs_3_
  10.1 0.5 %merge.2 = (bf16[14,16,128]{2,1,0:T(8,128)(2,1)S(1)}, f32[16,8,128]{2,1,0:T(8,128)S(1)}, f32[6,8,128]{2,1,0:T(8,128)S(1)}, f32[2,10,8,128]{3,2,1,0:T(8,128)S(1)}...) custom-call(f32[16,8,128]{2,1,0:T(8,128)S(1)} %get-tuple-element.71.refs_0_, ...), custom_call_target="tpu_custom_call" | custom-call | flops 1048576 | bytes 1048576 | tf_op jit(solution)/shard_map/merge/pallas_call | solution.py:475
  10.6 1.1 %collective-permute-start.3 = (bf16[14,16,128]{2,1,0:T(8,128)(2,1)S(1)}, bf16[14,16,128]{2,1,0:T(8,128)(2,1)S(1)}, u32[]{:S(2)}, u32[]{:S(2)}) collective-permute-start(bf16[14,16,128]{2,1,0:T(8,128)(2,1)S(1)} %get-tuple-element.94), channel_id=1, source_target_pairs={{0,8},{4,12},{8,0},{12,4},{1,9},{5,13},{9,1},{13,5},{2,10},{6,14},... | collective-permute-start | bytes 172040 | tf_op jit(solution)/shard_map/ppermute | solution.py:506
  11.7 0.4 %collective-permute-done.refs_2_ = bf16[8,16,128]{2,1,0:T(8,128)(2,1)S(1)} collective-permute-done((bf16[8,16,128]{2,1,0:T(8,128)(2,1)S(1)}, bf16[8,16,128]{2,1,0:T(8,128)(2,1)S(1)}, u32[]{:S(2)}, u32[]{:S(2)}) %collective-permute-start) | collective-permute-done | bytes 32800 | tf_op jit(solution)/shard_map/ppermute | solution.py:506
  12.1 0.3 %merge.3 = (bf16[8,16,128]{2,1,0:T(8,128)(2,1)S(1)}, f32[16,8,128]{2,1,0:T(8,128)S(1)}, f32[6,8,128]{2,1,0:T(8,128)S(1)}, bf16[256,1024]{1,0:T(8,128)(2,1)S(1)}, f32[16,8,128]{2,1,0:T(8,128)S(1)}) custom-call(f32[16,8,128]{2,1,0:T(8,128)S(1)} %get-tuple-element.64.refs_0_, ...), custom_call_target="tpu_custom_call", output_to_operand_aliasing={{3}: (12, {}), {4}: (13, {})} | custom-call | flops 1048576 | bytes 1048576 | tf_op jit(solution)/shard_map/merge/pallas_call | solution.py:475
  12.4 1.3 %collective-permute-start.2 = (bf16[8,16,128]{2,1,0:T(8,128)(2,1)S(1)}, bf16[8,16,128]{2,1,0:T(8,128)(2,1)S(1)}, u32[]{:S(2)}, u32[]{:S(2)}) collective-permute-start(bf16[8,16,128]{2,1,0:T(8,128)(2,1)S(1)} %get-tuple-element.93), channel_id=1, source_target_pairs={{0,8},{4,12},{8,0},{12,4},{1,9},{5,13},{9,1},{13,5},{2,10},{6,14},... | collective-permute-start | bytes 98312 | tf_op jit(solution)/shard_map/ppermute | solution.py:506
  13.7 3.1 %early.1.refs_11_ = bf16[256,2048]{1,0:T(8,128)(2,1)} custom-call(f32[2,10,8,128]{3,2,1,0:T(8,128)S(1)} %get-tuple-element.65.refs_1_.refs_9_.refs_4_.own_edges, bf16[256,1024]{1,0:T(8,128)(2,1)S(1)} %get-tuple-element.97.begun, f32[16,8,128]{2,1,0:T(8,128)S(1)} %get-tuple-element.98.begun_state, f32[256,8,128]{2,1,0:T(8,128)S(1)} %get-tuple-element.82.refs_5_.refs_0_, ...), custom_call_target="tpu_custom_call" | custom-call | flops 20971520 | bytes 1048576 | tf_op jit(solution)/shard_map/early/pallas_call | solution.py:475
  16.9 0.0 collective-permute-done.3.refs_8_.refs_9_
  16.9 0.4 %collective-permute-done.2.refs_8_ = bf16[8,16,128]{2,1,0:T(8,128)(2,1)S(1)} collective-permute-done((bf16[8,16,128]{2,1,0:T(8,128)(2,1)S(1)}, bf16[8,16,128]{2,1,0:T(8,128)(2,1)S(1)}, u32[]{:S(2)}, u32[]{:S(2)}) %collective-permute-start.2) | collective-permute-done | bytes 32800 | tf_op jit(solution)/shard_map/ppermute | solution.py:506
  17.3 0.1 late.3
  (5 shorter events, 0.0 us)
Async XLA Ops:
  3.1 7.0 %collective-permute-start.1 = (bf16[18,16,128]{2,1,0:T(8,128)(2,1)S(1)}, bf16[18,16,128]{2,1,0:T(8,128)(2,1)S(1)}, u32[]{:S(2)}, u32[]{:S(2)}) collective-permute-start(bf16[18,16,128]{2,1,0:T(8,128)(2,1)S(1)} %get-tuple-element.67), channel_id=1, source_target_pairs={{0,4},{4,0},{8,12},{12,8},{1,5},{5,1},{9,13},{13,9},{2,6},{6,2},{1... | collective-permute-start | bytes 221192 | tf_op jit(solution)/shard_map/ppermute | solution.py:506
  8.1 4.0 %collective-permute-start = (bf16[8,16,128]{2,1,0:T(8,128)(2,1)S(1)}, bf16[8,16,128]{2,1,0:T(8,128)(2,1)S(1)}, u32[]{:S(2)}, u32[]{:S(2)}) collective-permute-start(bf16[8,16,128]{2,1,0:T(8,128)(2,1)S(1)} %get-tuple-element.66), channel_id=1, source_target_pairs={{0,4},{4,0},{8,12},{12,8},{1,5},{5,1},{9,13},{13,9},{2,6},{6,2},{1... | collective-permute-start | bytes 98312 | tf_op jit(solution)/shard_map/ppermute | solution.py:506
  10.6 6.3 %collective-permute-start.3 = (bf16[14,16,128]{2,1,0:T(8,128)(2,1)S(1)}, bf16[14,16,128]{2,1,0:T(8,128)(2,1)S(1)}, u32[]{:S(2)}, u32[]{:S(2)}) collective-permute-start(bf16[14,16,128]{2,1,0:T(8,128)(2,1)S(1)} %get-tuple-element.94), channel_id=1, source_target_pairs={{0,8},{4,12},{8,0},{12,4},{1,9},{5,13},{9,1},{13,5},{2,10},{6,14},... | collective-permute-start | bytes 172040 | tf_op jit(solution)/shard_map/ppermute | solution.py:506
  12.4 4.9 %collective-permute-start.2 = (bf16[8,16,128]{2,1,0:T(8,128)(2,1)S(1)}, bf16[8,16,128]{2,1,0:T(8,128)(2,1)S(1)}, u32[]{:S(2)}, u32[]{:S(2)}) collective-permute-start(bf16[8,16,128]{2,1,0:T(8,128)(2,1)S(1)} %get-tuple-element.93), channel_id=1, source_target_pairs={{0,8},{4,12},{8,0},{12,4},{1,9},{5,13},{9,1},{13,5},{2,10},{6,14},... | collective-permute-start | bytes 98312 | tf_op jit(solution)/shard_map/ppermute | solution.py:506

commit v7 on v6

--- a/solution.py
+++ b/solution.py
@@ -13,7 +13,7 @@
 CHUNK = 16
 PIECE = 64
 STRIDE = CHUNK + 8
-EARLY = (4, 6)
+EARLY = 2
 HEAD = 4
 TAIL = 6
 
@@ -584,71 +584,67 @@
             if first and g == 1:
                 state_slot(groups, [rim[0]])
                 near = near_all(lambda: is_early(size // 2) & jnp.logical_not(is_first(size // 2)), [rim[0]], near)
-            part = range(EARLY[g - 1] if g else 0, EARLY[g]) if last and g < len(EARLY) else range(0)
-            early, held = [], []
-            if part:
-                early = [*near[:2], made[0][1], made[0][3], own_edges] + ([entering[0], rim[0]] if g else [])
-                held = [begun, begun_state] if g else []
-            operands = [merged[g], old_edges, got[g], got[0], made[g][3]] + ([] if first else [entering[g], rim[g]])
+            early = [*near[:2], made[0][1], made[0][3], own_edges] if last and g == 0 else []
+            after = near[:1] if first and g == 1 else []
+            operands = after + [merged[g], old_edges, got[g], got[0], made[g][3]] + ([] if first else [entering[g], rim[g]])
             count = modes + (groups * (TAIL if last else edge) if g == 0 else 0)
             outs = [message_type(count), vectors(modes), vectors(TAIL)]
             outs += [] if last else [vectors(modes)]
             outs += [vectors(groups, edge)] if g == 0 else []
-            outs += [half, vectors(modes)] if part else []
-
-            def kernel(*refs, g=g, span=span, last=last, first=first, part=part, counts=(len(early), len(held), len(outs))):
-                refs = list(refs)
+            outs += [half, vectors(modes)] if early else []
+
+            def kernel(*refs, g=g, span=span, last=last, first=first, counts=(len(early), len(outs)), skip=len(after)):
+                refs = list(refs[skip:])
                 ins = [refs.pop(0) for _ in range(5)] + ([None, None] if first else [refs.pop(0) for _ in range(2)])
-                more, _, produced = ([refs.pop(0) for _ in range(n)] for n in counts)
+                more, produced = ([refs.pop(0) for _ in range(n)] for n in counts)
                 state_out = None if last else produced[3]
                 edges_out = produced[3 if last else 4] if g == 0 else None
                 merge_group(span, tokens, g, last, *ins, *produced[:3], state_out, edges_out)
-
-                def emit(which):
-                    known = more[5:7] if g else produced[1:3]
-                    emit_known(which, 0, more[:4], more[4], *known, produced[-2], [produced[-1]] + refs, lambda n: None)
-
-                if part:
-                    pl.when(is_first(2 * span))(lambda: emit(part))
-                if part and g == 1:
-                    pl.when(is_early(2 * span) & jnp.logical_not(is_first(2 * span)))(lambda: emit(range(part.stop)))
-
-            results = list(
-                call(
-                    kernel, "merge", operands + early + held, outs, emit_scratch if part else [], 4, 2**20,
-                    aliases={len(operands) + len(early) + i: len(outs) - 2 + i for i in range(len(held))},
-                )
-            )
+                if more:
+
+                    @pl.when(is_first(2 * span))
+                    def _():
+                        out_ref, state_ref = produced[-2:]
+                        emit_known(
+                            range(EARLY), 0, more[:4], more[4], *produced[1:3], out_ref, [state_ref] + refs, lambda n: None
+                        )
+
+            results = list(call(kernel, "merge", operands + early, outs, emit_scratch if early else [], 4, 2**20))
             message[g], entering[g], rim[g] = results[:3]
             if not last:
                 merged[g] = results[3]
             if g == 0:
                 edges = results[3 if last else 4]
-            if part:
+            if early:
                 begun, begun_state = results[-2:]
         span *= 2
 
     out_type = pltpu.HBM((tokens, channels), BF16)
     pair = [[entering[g], rim[g]] for g in range(groups)]
-    begin = EARLY[-1]
-
     def kernel(own_edges, begun, begun_state, *refs):
         ins, refs = [refs[i * 6 : i * 6 + 6] for i in range(groups)], refs[groups * 6 :]
         out_hbm, out_refs, state, scratch = refs[0], refs[1 : 1 + groups], refs[1 + groups], refs[2 + groups : 6 + groups]
 
         @pl.when(is_early(span))
         def _():
-            for m in range(modes):
-                state[m] = begun_state[m]
+            @pl.when(is_first(span))
+            def _():
+                out_refs[0][pl.ds(0, EARLY * CHUNK), :] = begun[pl.ds(0, EARLY * CHUNK), :]
+                for m in range(modes):
+                    state[m] = begun_state[m]
+
+            @pl.when(jnp.logical_not(is_first(span)))
+            def _():
+                emit_known(range(EARLY), 0, ins[0][:4], own_edges, *ins[0][4:], out_refs[0], [state, *scratch], lambda n: None)
+
             for g in range(groups - 1):
-                which = range(0 if g else begin, chunks)
+                which = range(0 if g else EARLY, chunks)
                 emit_known(which, g, ins[g][:4], own_edges, *ins[g][4:], out_refs[g], [state, *scratch], lambda n: None)
 
             def emit(out, piece_done):
                 emit_known(range(chunks), groups - 1, ins[-1][:4], own_edges, *ins[-1][4:], out, [state, *scratch], piece_done)
 
-            done = [(pl.ds(0, begin * CHUNK), 0, begun), (pl.ds(begin * CHUNK, tokens - begin * CHUNK), 0, out_refs[0])]
-            done += [(pl.ds(0, tokens), g, out_refs[g]) for g in range(1, groups - 1)]
+            done = [(pl.ds(0, tokens), g, out_refs[g]) for g in range(groups - 1)]
             emit_out(emit, done, out_hbm, out_refs[-1], *refs[6 + groups :])
 
     def fixed_of():

time: 17.6 us -> 17.4 us (0.989)
  waiting for transfers between devices: 0.77 us -> 0.42 us
  starting transfers between devices: 5.65 us -> 5.84 us
    ppermute x4, waiting for transfers between devices: 0.77 us -> 0.42 us  [swap(): lax.ppermute(message, 'context', [(i, i ^ span) for i in range(size)])]
    ppermute x4, starting transfers between devices: 5.65 us -> 5.84 us  [swap(): lax.ppermute(message, 'context', [(i, i ^ span) for i in range(size)])]
  transfers between devices with their start and end apart: 4 -> 4, of which waited for: 2 -> 1; matrix products, arithmetic and copies ran while one was open for 0% -> 0% of each run, Pallas kernels for 44% -> 45%
where the time goes in v7:
time: 17.4 us; the launch traced here: 17.2 us
  Pallas kernels  10.8 us (62%)
  starting transfers between devices  5.84 us (34%)
  waiting for transfers between devices  0.42 us (2%)
    pallas_call x11, Pallas kernels, call(): pl.pallas_call(kernel, in_specs=in_specs, out_specs=[VM] * len(outs) if o...  10.8 us
    ppermute x4, starting transfers between devices, swap(): lax.ppermute(message, 'context', [(i, i ^ span) for i in range(size)])  5.84 us
    ppermute x4, waiting for transfers between devices, swap(): lax.ppermute(message, 'context', [(i, i ^ span) for i in range(size)])  0.42 us
  transfers between devices with their start and end apart: 4, of which 1 were waited for; matrix products, arithmetic and copies ran while one was open for 0% of the time, Pallas kernels for 45%

profile of v7, /device:TPU:0, one launch (start us, length us, event | category | flops | bytes accessed | tf_op | source)
XLA Modules:
  0.0 17.2 jit_solution(6085267245756260651)
XLA Ops:
  0.0 3.1 %states.3 = (f32[256,8,128]{2,1,0:T(8,128)S(1)}, f32[16,16,8,128]{3,2,1,0:T(8,128)S(1)}, f32[16,8,128]{2,1,0:T(8,128)S(1)}, f32[42,8,128]{2,1,0:T(8,128)S(1)}, b...) custom-call(bf16[3,256,2048]{2,1,0:T(8,128)(2,1)} %bitcast.4, ...), custom_call_target="tpu_custom_call" | custom-call | flops 12582912 | bytes 1048576 | tf_op jit(solution)/shard_map/states/pallas_call | solution.py:475
  3.1 3.1 %collective-permute-start = (bf16[18,16,128]{2,1,0:T(8,128)(2,1)S(1)}, bf16[18,16,128]{2,1,0:T(8,128)(2,1)S(1)}, u32[]{:S(2)}, u32[]{:S(2)}) collective-permute-start(bf16[18,16,128]{2,1,0:T(8,128)(2,1)S(1)} %get-tuple-element.64), channel_id=1, source_target_pairs={{0,4},{4,0},{8,12},{12,8},{1,5},{5,1},{9,13},{13,9},{2,6},{6,2},{1... | collective-permute-start | bytes 221192 | tf_op jit(solution)/shard_map/ppermute | solution.py:506
  6.2 1.9 %states.4 = (f32[256,8,128]{2,1,0:T(8,128)S(1)}, f32[16,16,8,128]{3,2,1,0:T(8,128)S(1)}, f32[16,8,128]{2,1,0:T(8,128)S(1)}, f32[42,8,128]{2,1,0:T(8,128)S(1)}, f...) custom-call(f32[16,2048]{1,0:T(8,128)S(1)} %get-tuple-element.51.ref, ...), custom_call_target="tpu_custom_call", output_to_operand_aliasing={{0}: (5, {}), {1}: (6, {}), {2}: (7, {}), {3}: (8, {}), {4}... | custom-call | flops 12582912 | bytes 1048576 | tf_op jit(solution)/shard_map/states/pallas_call | solution.py:475
  8.1 0.1 collective-permute-start.1
  8.2 1.8 %near.3 = (f32[256,8,128]{2,1,0:T(8,128)S(1)}, f32[256,8,128]{2,1,0:T(8,128)S(1)}, f32[256,8,128]{2,1,0:T(8,128)S(1)}, f32[256,8,128]{2,1,0:T(8,128)S(1)}) custom-call(bf16[3,256,2048]{2,1,0:T(8,128)(2,1)S(1)} %get-tuple-element.61.refs_0_.refs_4_, f32[42,8,128]{2,1,0:T(8,128)S(1)} %get-tuple-element.65.refs_1_.refs_4_.refs_8_.refs_2_.refs_3_, ...), custom_call_target="tpu_custom_call" | custom-call | flops 12582912 | bytes 1048576 | tf_op jit(solution)/shard_map/near/pallas_call | solution.py:475
  10.1 0.0 collective-permute-done.refs_2_.refs_3_.refs_4_
  10.1 0.3 %merge.2 = (bf16[14,16,128]{2,1,0:T(8,128)(2,1)S(1)}, f32[16,8,128]{2,1,0:T(8,128)S(1)}, f32[6,8,128]{2,1,0:T(8,128)S(1)}, f32[2,10,8,128]{3,2,1,0:T(8,128)S(1)}...) custom-call(f32[16,8,128]{2,1,0:T(8,128)S(1)} %get-tuple-element.62.refs_0_, ...), custom_call_target="tpu_custom_call" | custom-call | flops 1048576 | bytes 1048576 | tf_op jit(solution)/shard_map/merge/pallas_call | solution.py:475
  10.4 1.3 %collective-permute-start.3 = (bf16[14,16,128]{2,1,0:T(8,128)(2,1)S(1)}, bf16[14,16,128]{2,1,0:T(8,128)(2,1)S(1)}, u32[]{:S(2)}, u32[]{:S(2)}) collective-permute-start(bf16[14,16,128]{2,1,0:T(8,128)(2,1)S(1)} %get-tuple-element.88), channel_id=1, source_target_pairs={{0,8},{4,12},{8,0},{12,4},{1,9},{5,13},{9,1},{13,5},{2,10},{6,14},... | collective-permute-start | bytes 172040 | tf_op jit(solution)/shard_map/ppermute | solution.py:506
  11.7 0.4 %collective-permute-done.1.refs_3_ = bf16[8,16,128]{2,1,0:T(8,128)(2,1)S(1)} collective-permute-done((bf16[8,16,128]{2,1,0:T(8,128)(2,1)S(1)}, bf16[8,16,128]{2,1,0:T(8,128)(2,1)S(1)}, u32[]{:S(2)}, u32[]{:S(2)}) %collective-permute-start.1) | collective-permute-done | bytes 32800 | tf_op jit(solution)/shard_map/ppermute | solution.py:506
  12.1 0.1 merge.3
  12.2 1.4 %collective-permute-start.2 = (bf16[8,16,128]{2,1,0:T(8,128)(2,1)S(1)}, bf16[8,16,128]{2,1,0:T(8,128)(2,1)S(1)}, u32[]{:S(2)}, u32[]{:S(2)}) collective-permute-start(bf16[8,16,128]{2,1,0:T(8,128)(2,1)S(1)} %get-tuple-element.87), channel_id=1, source_target_pairs={{0,8},{4,12},{8,0},{12,4},{1,9},{5,13},{9,1},{13,5},{2,10},{6,14},... | collective-permute-start | bytes 98312 | tf_op jit(solution)/shard_map/ppermute | solution.py:506
  13.6 3.5 %early.1.refs_11_ = bf16[256,2048]{1,0:T(8,128)(2,1)} custom-call(f32[2,10,8,128]{3,2,1,0:T(8,128)S(1)} %get-tuple-element.63.refs_1_.refs_9_.refs_2_.refs_4_.own_edges, bf16[256,1024]{1,0:T(8,128)(2,1)S(1)} %get-tuple-element.92.begun, f32[16,8,128]{2,1,0:T(8,128)S(1)} %get-tuple-element.93.begun_state, f32[256,8,128]{2,1,0:T(8,128)S(1)} %get-tuple-element.79.refs_0_, ...), custom_call_target="tpu_custom_call" | custom-call | flops 20971520 | bytes 1048576 | tf_op jit(solution)/shard_map/early/pallas_call | solution.py:475
  17.1 0.0 collective-permute-done.3.refs_8_.refs_9_
  17.1 0.0 collective-permute-done.2.refs_8_
  17.1 0.1 late.3
  (5 shorter events, 0.0 us)
Async XLA Ops:
  3.1 7.0 %collective-permute-start = (bf16[18,16,128]{2,1,0:T(8,128)(2,1)S(1)}, bf16[18,16,128]{2,1,0:T(8,128)(2,1)S(1)}, u32[]{:S(2)}, u32[]{:S(2)}) collective-permute-start(bf16[18,16,128]{2,1,0:T(8,128)(2,1)S(1)} %get-tuple-element.64), channel_id=1, source_target_pairs={{0,4},{4,0},{8,12},{12,8},{1,5},{5,1},{9,13},{13,9},{2,6},{6,2},{1... | collective-permute-start | bytes 221192 | tf_op jit(solution)/shard_map/ppermute | solution.py:506
  8.1 4.0 %collective-permute-start.1 = (bf16[8,16,128]{2,1,0:T(8,128)(2,1)S(1)}, bf16[8,16,128]{2,1,0:T(8,128)(2,1)S(1)}, u32[]{:S(2)}, u32[]{:S(2)}) collective-permute-start(bf16[8,16,128]{2,1,0:T(8,128)(2,1)S(1)} %get-tuple-element.80), channel_id=1, source_target_pairs={{0,4},{4,0},{8,12},{12,8},{1,5},{5,1},{9,13},{13,9},{2,6},{6,2},{1... | collective-permute-start | bytes 98312 | tf_op jit(solution)/shard_map/ppermute | solution.py:506
  10.4 6.7 %collective-permute-start.3 = (bf16[14,16,128]{2,1,0:T(8,128)(2,1)S(1)}, bf16[14,16,128]{2,1,0:T(8,128)(2,1)S(1)}, u32[]{:S(2)}, u32[]{:S(2)}) collective-permute-start(bf16[14,16,128]{2,1,0:T(8,128)(2,1)S(1)} %get-tuple-element.88), channel_id=1, source_target_pairs={{0,8},{4,12},{8,0},{12,4},{1,9},{5,13},{9,1},{13,5},{2,10},{6,14},... | collective-permute-start | bytes 172040 | tf_op jit(solution)/shard_map/ppermute | solution.py:506
  12.2 4.9 %collective-permute-start.2 = (bf16[8,16,128]{2,1,0:T(8,128)(2,1)S(1)}, bf16[8,16,128]{2,1,0:T(8,128)(2,1)S(1)}, u32[]{:S(2)}, u32[]{:S(2)}) collective-permute-start(bf16[8,16,128]{2,1,0:T(8,128)(2,1)S(1)} %get-tuple-element.87), channel_id=1, source_target_pairs={{0,8},{4,12},{8,0},{12,4},{1,9},{5,13},{9,1},{13,5},{2,10},{6,14},... | collective-permute-start | bytes 98312 | tf_op jit(solution)/shard_map/ppermute | solution.py:506

commit v8 on v7

--- a/solution.py
+++ b/solution.py
@@ -16,6 +16,11 @@
 EARLY = 2
 HEAD = 4
 TAIL = 6
+
+
+def rounded(first, second):
+    pair = jnp.concatenate([first, second], axis=0).astype(BF16).astype(F32)
+    return pair[:SUB], pair[SUB:]
 
 
 def total(values):
@@ -123,16 +128,19 @@
         k1, k2, v1, v2 = last
         for m in range(modes):
             states_ref[c, m] = acc[m]
-        for i in range(CHUNK):
-            k, v = row(ks, i), row(vs, i)
-            key = wk[0] * k + wk[1] * k1 + wk[2] * k2
-            value = wv[0] * v + wv[1] * v1 + wv[2] * v2
-            k1, k2, v1, v2 = k, k1, v, v1
-            product = (key * value).astype(BF16).astype(F32)
-            if i < 2:
-                product = jnp.where((c > 0) | (rank == 0), product, 0.0)
-            kv_ref[c * CHUNK + i] = product
-            acc = [a * b + product for a, b in zip(acc, p)]
+        for i in range(0, CHUNK, 2):
+            products = []
+            for n in (i, i + 1):
+                k, v = row(ks, n), row(vs, n)
+                key = wk[0] * k + wk[1] * k1 + wk[2] * k2
+                value = wv[0] * v + wv[1] * v1 + wv[2] * v2
+                k1, k2, v1, v2 = k, k1, v, v1
+                products.append(key * value)
+            for n, product in enumerate(rounded(*products)):
+                if i == 0:
+                    product = jnp.where((c > 0) | (rank == 0), product, 0.0)
+                kv_ref[c * CHUNK + i + n] = product
+                acc = [a * b + product for a, b in zip(acc, p)]
         return acc, (k1, k2, v1, v2)
 
     def two_chunks(it, carry):
@@ -374,16 +382,20 @@
 
     def one_chunk(c, turned, first):
         x = [tables_ref[gain_row(modes, m)] * (states_ref[c, m] + state[m]) for m in range(modes)]
-        for i in range(CHUNK):
-            t = c * CHUNK + i
-            x = [a * b for a, b in zip(x, p)]
-            near, query = near_ref[t], query_ref[t]
-            if first and i < 2:
-                x = [a + tables_ref[gain_row(modes, m)] * rim_ref[i] for m, a in enumerate(x)]
-                near = near + tables_ref[gain_row(modes, modes)] * rim_ref[i]
-                query = query + rim_ref[2 + i]
-            mixed = (near + total(x)).astype(BF16).astype(F32)
-            turned[pl.ds(i, SUB, stride=STRIDE), :] = query * mixed
+        for i in range(0, CHUNK, 2):
+            queries, mixed = [], []
+            for n in (i, i + 1):
+                t = c * CHUNK + n
+                x = [a * b for a, b in zip(x, p)]
+                near, query = near_ref[t], query_ref[t]
+                if first and n < 2:
+                    x = [a + tables_ref[gain_row(modes, m)] * rim_ref[n] for m, a in enumerate(x)]
+                    near = near + tables_ref[gain_row(modes, modes)] * rim_ref[n]
+                    query = query + rim_ref[2 + n]
+                queries.append(query)
+                mixed.append(near + total(x))
+            for n, value in enumerate(rounded(*mixed)):
+                turned[pl.ds(i + n, SUB, stride=STRIDE), :] = queries[n] * value
         for m in range(modes):
             if first:
                 held = (state[m] * p[m] + rim_ref[0]) * p[m] + rim_ref[1]

time: 17.4 us -> 17.2 us (0.989)
    pallas_call x11, Pallas kernels: 10.8 us -> 10.7 us  [call(): pl.pallas_call(kernel, in_specs=in_specs, out_specs=[VM] * len(outs) if o...]
where the time goes in v8:
time: 17.2 us; the launch traced here: 17 us
  Pallas kernels  10.7 us (62%)
  starting transfers between devices  5.92 us (34%)
  waiting for transfers between devices  0.34 us (2%)
    pallas_call x11, Pallas kernels, call(): pl.pallas_call(kernel, in_specs=in_specs, out_specs=[VM] * len(outs) if o...  10.7 us
    ppermute x4, starting transfers between devices, swap(): lax.ppermute(message, 'context', [(i, i ^ span) for i in range(size)])  5.92 us
    ppermute x4, waiting for transfers between devices, swap(): lax.ppermute(message, 'context', [(i, i ^ span) for i in range(size)])  0.34 us
  transfers between devices with their start and end apart: 4, of which 1 were waited for; matrix products, arithmetic and copies ran while one was open for 0% of the time, Pallas kernels for 45%

profile of v8, /device:TPU:0, one launch (start us, length us, event | category | flops | bytes accessed | tf_op | source)
XLA Modules:
  0.0 17.0 jit_solution(17315688651658623698)
XLA Ops:
  0.0 3.0 %states.3 = (f32[256,8,128]{2,1,0:T(8,128)S(1)}, f32[16,16,8,128]{3,2,1,0:T(8,128)S(1)}, f32[16,8,128]{2,1,0:T(8,128)S(1)}, f32[42,8,128]{2,1,0:T(8,128)S(1)}, b...) custom-call(bf16[3,256,2048]{2,1,0:T(8,128)(2,1)} %bitcast.4, ...), custom_call_target="tpu_custom_call" | custom-call | flops 12582912 | bytes 1048576 | tf_op jit(solution)/shard_map/states/pallas_call | solution.py:487
  3.0 3.1 %collective-permute-start = (bf16[18,16,128]{2,1,0:T(8,128)(2,1)S(1)}, bf16[18,16,128]{2,1,0:T(8,128)(2,1)S(1)}, u32[]{:S(2)}, u32[]{:S(2)}) collective-permute-start(bf16[18,16,128]{2,1,0:T(8,128)(2,1)S(1)} %get-tuple-element.64), channel_id=1, source_target_pairs={{0,4},{4,0},{8,12},{12,8},{1,5},{5,1},{9,13},{13,9},{2,6},{6,2},{1... | collective-permute-start | bytes 221192 | tf_op jit(solution)/shard_map/ppermute | solution.py:518
  6.1 1.9 %states.4 = (f32[256,8,128]{2,1,0:T(8,128)S(1)}, f32[16,16,8,128]{3,2,1,0:T(8,128)S(1)}, f32[16,8,128]{2,1,0:T(8,128)S(1)}, f32[42,8,128]{2,1,0:T(8,128)S(1)}, f...) custom-call(f32[16,2048]{1,0:T(8,128)S(1)} %get-tuple-element.51.ref, ...), custom_call_target="tpu_custom_call", output_to_operand_aliasing={{0}: (5, {}), {1}: (6, {}), {2}: (7, {}), {3}: (8, {}), {4}... | custom-call | flops 12582912 | bytes 1048576 | tf_op jit(solution)/shard_map/states/pallas_call | solution.py:487
  8.0 0.1 collective-permute-start.1
  8.1 1.8 %near.3 = (f32[256,8,128]{2,1,0:T(8,128)S(1)}, f32[256,8,128]{2,1,0:T(8,128)S(1)}, f32[256,8,128]{2,1,0:T(8,128)S(1)}, f32[256,8,128]{2,1,0:T(8,128)S(1)}) custom-call(bf16[3,256,2048]{2,1,0:T(8,128)(2,1)S(1)} %get-tuple-element.61.refs_0_.refs_4_, f32[42,8,128]{2,1,0:T(8,128)S(1)} %get-tuple-element.65.refs_1_.refs_4_.refs_8_.refs_2_.refs_3_, ...), custom_call_target="tpu_custom_call" | custom-call | flops 12582912 | bytes 1048576 | tf_op jit(solution)/shard_map/near/pallas_call | solution.py:487
  9.9 0.0 collective-permute-done.refs_2_.refs_3_.refs_4_
  9.9 0.3 %merge.2 = (bf16[14,16,128]{2,1,0:T(8,128)(2,1)S(1)}, f32[16,8,128]{2,1,0:T(8,128)S(1)}, f32[6,8,128]{2,1,0:T(8,128)S(1)}, f32[2,10,8,128]{3,2,1,0:T(8,128)S(1)}...) custom-call(f32[16,8,128]{2,1,0:T(8,128)S(1)} %get-tuple-element.62.refs_0_, ...), custom_call_target="tpu_custom_call" | custom-call | flops 1048576 | bytes 1048576 | tf_op jit(solution)/shard_map/merge/pallas_call | solution.py:487
  10.2 1.4 %collective-permute-start.3 = (bf16[14,16,128]{2,1,0:T(8,128)(2,1)S(1)}, bf16[14,16,128]{2,1,0:T(8,128)(2,1)S(1)}, u32[]{:S(2)}, u32[]{:S(2)}) collective-permute-start(bf16[14,16,128]{2,1,0:T(8,128)(2,1)S(1)} %get-tuple-element.88), channel_id=1, source_target_pairs={{0,8},{4,12},{8,0},{12,4},{1,9},{5,13},{9,1},{13,5},{2,10},{6,14},... | collective-permute-start | bytes 172040 | tf_op jit(solution)/shard_map/ppermute | solution.py:518
  11.6 0.3 %collective-permute-done.1.refs_3_ = bf16[8,16,128]{2,1,0:T(8,128)(2,1)S(1)} collective-permute-done((bf16[8,16,128]{2,1,0:T(8,128)(2,1)S(1)}, bf16[8,16,128]{2,1,0:T(8,128)(2,1)S(1)}, u32[]{:S(2)}, u32[]{:S(2)}) %collective-permute-start.1) | collective-permute-done | bytes 32800 | tf_op jit(solution)/shard_map/ppermute | solution.py:518
  12.0 0.1 merge.3
  12.0 1.4 %collective-permute-start.2 = (bf16[8,16,128]{2,1,0:T(8,128)(2,1)S(1)}, bf16[8,16,128]{2,1,0:T(8,128)(2,1)S(1)}, u32[]{:S(2)}, u32[]{:S(2)}) collective-permute-start(bf16[8,16,128]{2,1,0:T(8,128)(2,1)S(1)} %get-tuple-element.87), channel_id=1, source_target_pairs={{0,8},{4,12},{8,0},{12,4},{1,9},{5,13},{9,1},{13,5},{2,10},{6,14},... | collective-permute-start | bytes 98312 | tf_op jit(solution)/shard_map/ppermute | solution.py:518
  13.4 3.5 %early.1.refs_11_ = bf16[256,2048]{1,0:T(8,128)(2,1)} custom-call(f32[2,10,8,128]{3,2,1,0:T(8,128)S(1)} %get-tuple-element.63.refs_1_.refs_9_.refs_2_.refs_4_.own_edges, bf16[256,1024]{1,0:T(8,128)(2,1)S(1)} %get-tuple-element.92.begun, f32[16,8,128]{2,1,0:T(8,128)S(1)} %get-tuple-element.93.begun_state, f32[256,8,128]{2,1,0:T(8,128)S(1)} %get-tuple-element.79.refs_0_, ...), custom_call_target="tpu_custom_call" | custom-call | flops 20971520 | bytes 1048576 | tf_op jit(solution)/shard_map/early/pallas_call | solution.py:487
  16.9 0.0 collective-permute-done.3.refs_8_.refs_9_
  16.9 0.0 collective-permute-done.2.refs_8_
  16.9 0.1 late.3
  (5 shorter events, 0.0 us)
Async XLA Ops:
  3.0 6.9 %collective-permute-start = (bf16[18,16,128]{2,1,0:T(8,128)(2,1)S(1)}, bf16[18,16,128]{2,1,0:T(8,128)(2,1)S(1)}, u32[]{:S(2)}, u32[]{:S(2)}) collective-permute-start(bf16[18,16,128]{2,1,0:T(8,128)(2,1)S(1)} %get-tuple-element.64), channel_id=1, source_target_pairs={{0,4},{4,0},{8,12},{12,8},{1,5},{5,1},{9,13},{13,9},{2,6},{6,2},{1... | collective-permute-start | bytes 221192 | tf_op jit(solution)/shard_map/ppermute | solution.py:518
  8.0 4.0 %collective-permute-start.1 = (bf16[8,16,128]{2,1,0:T(8,128)(2,1)S(1)}, bf16[8,16,128]{2,1,0:T(8,128)(2,1)S(1)}, u32[]{:S(2)}, u32[]{:S(2)}) collective-permute-start(bf16[8,16,128]{2,1,0:T(8,128)(2,1)S(1)} %get-tuple-element.80), channel_id=1, source_target_pairs={{0,4},{4,0},{8,12},{12,8},{1,5},{5,1},{9,13},{13,9},{2,6},{6,2},{1... | collective-permute-start | bytes 98312 | tf_op jit(solution)/shard_map/ppermute | solution.py:518
  10.2 6.6 %collective-permute-start.3 = (bf16[14,16,128]{2,1,0:T(8,128)(2,1)S(1)}, bf16[14,16,128]{2,1,0:T(8,128)(2,1)S(1)}, u32[]{:S(2)}, u32[]{:S(2)}) collective-permute-start(bf16[14,16,128]{2,1,0:T(8,128)(2,1)S(1)} %get-tuple-element.88), channel_id=1, source_target_pairs={{0,8},{4,12},{8,0},{12,4},{1,9},{5,13},{9,1},{13,5},{2,10},{6,14},... | collective-permute-start | bytes 172040 | tf_op jit(solution)/shard_map/ppermute | solution.py:518
  12.0 4.9 %collective-permute-start.2 = (bf16[8,16,128]{2,1,0:T(8,128)(2,1)S(1)}, bf16[8,16,128]{2,1,0:T(8,128)(2,1)S(1)}, u32[]{:S(2)}, u32[]{:S(2)}) collective-permute-start(bf16[8,16,128]{2,1,0:T(8,128)(2,1)S(1)} %get-tuple-element.87), channel_id=1, source_target_pairs={{0,8},{4,12},{8,0},{12,4},{1,9},{5,13},{9,1},{13,5},{2,10},{6,14},... | collective-permute-start | bytes 98312 | tf_op jit(solution)/shard_map/ppermute | solution.py:518

commit v9 on v8

--- a/solution.py
+++ b/solution.py
@@ -12,7 +12,7 @@
 GROUP = LANES * SUB
 CHUNK = 16
 PIECE = 64
-STRIDE = CHUNK + 8
+STRIDE = CHUNK + 1
 EARLY = 2
 HEAD = 4
 TAIL = 6

time: 17.2 us -> 17 us (0.988)
  Pallas kernels: 10.7 us -> 10.3 us
  starting transfers between devices: 5.92 us -> 6.12 us
    pallas_call x11, Pallas kernels: 10.7 us -> 10.3 us  [call(): pl.pallas_call(kernel, in_specs=in_specs, out_specs=[VM] * len(outs) if o...]
    ppermute x4, starting transfers between devices: 5.92 us -> 6.12 us  [swap(): lax.ppermute(message, 'context', [(i, i ^ span) for i in range(size)])]
  transfers between devices with their start and end apart: 4 -> 4, of which waited for: 1 -> 2; matrix products, arithmetic and copies ran while one was open for 0% -> 0% of each run, Pallas kernels for 45% -> 44%
where the time goes in v9:
time: 17 us; the launch traced here: 16.8 us
  Pallas kernels  10.3 us (61%)
  starting transfers between devices  6.12 us (36%)
  waiting for transfers between devices  0.26 us (2%)
    pallas_call x11, Pallas kernels, call(): pl.pallas_call(kernel, in_specs=in_specs, out_specs=[VM] * len(outs) if o...  10.3 us
    ppermute x4, starting transfers between devices, swap(): lax.ppermute(message, 'context', [(i, i ^ span) for i in range(size)])  6.12 us
  transfers between devices with their start and end apart: 4, of which 2 were waited for; matrix products, arithmetic and copies ran while one was open for 0% of the time, Pallas kernels for 44%

profile of v9, /device:TPU:0, one launch (start us, length us, event | category | flops | bytes accessed | tf_op | source)
XLA Modules:
  0.0 16.8 jit_solution(1151845013263881415)
XLA Ops:
  0.0 3.0 %states.3 = (f32[256,8,128]{2,1,0:T(8,128)S(1)}, f32[16,16,8,128]{3,2,1,0:T(8,128)S(1)}, f32[16,8,128]{2,1,0:T(8,128)S(1)}, f32[42,8,128]{2,1,0:T(8,128)S(1)}, b...) custom-call(bf16[3,256,2048]{2,1,0:T(8,128)(2,1)} %bitcast.4, ...), custom_call_target="tpu_custom_call" | custom-call | flops 12582912 | bytes 1048576 | tf_op jit(solution)/shard_map/states/pallas_call | solution.py:487
  3.0 3.1 %collective-permute-start = (bf16[18,16,128]{2,1,0:T(8,128)(2,1)S(1)}, bf16[18,16,128]{2,1,0:T(8,128)(2,1)S(1)}, u32[]{:S(2)}, u32[]{:S(2)}) collective-permute-start(bf16[18,16,128]{2,1,0:T(8,128)(2,1)S(1)} %get-tuple-element.64), channel_id=1, source_target_pairs={{0,4},{4,0},{8,12},{12,8},{1,5},{5,1},{9,13},{13,9},{2,6},{6,2},{1... | collective-permute-start | bytes 221192 | tf_op jit(solution)/shard_map/ppermute | solution.py:518
  6.0 1.7 %states.4 = (f32[256,8,128]{2,1,0:T(8,128)S(1)}, f32[16,16,8,128]{3,2,1,0:T(8,128)S(1)}, f32[16,8,128]{2,1,0:T(8,128)S(1)}, f32[42,8,128]{2,1,0:T(8,128)S(1)}, f...) custom-call(f32[16,2048]{1,0:T(8,128)S(1)} %get-tuple-element.51.ref, ...), custom_call_target="tpu_custom_call", output_to_operand_aliasing={{0}: (5, {}), {1}: (6, {}), {2}: (7, {}), {3}: (8, {}), {4}... | custom-call | flops 12582912 | bytes 1048576 | tf_op jit(solution)/shard_map/states/pallas_call | solution.py:487
  7.8 0.1 collective-permute-start.1
  7.9 1.8 %near.3 = (f32[256,8,128]{2,1,0:T(8,128)S(1)}, f32[256,8,128]{2,1,0:T(8,128)S(1)}, f32[256,8,128]{2,1,0:T(8,128)S(1)}, f32[256,8,128]{2,1,0:T(8,128)S(1)}) custom-call(bf16[3,256,2048]{2,1,0:T(8,128)(2,1)S(1)} %get-tuple-element.61.refs_0_.refs_4_, f32[42,8,128]{2,1,0:T(8,128)S(1)} %get-tuple-element.65.refs_1_.refs_4_.refs_8_.refs_2_.refs_3_, ...), custom_call_target="tpu_custom_call" | custom-call | flops 12582912 | bytes 1048576 | tf_op jit(solution)/shard_map/near/pallas_call | solution.py:487
  9.7 0.0 collective-permute-done.refs_2_.refs_3_.refs_4_
  9.7 0.3 %merge.2 = (bf16[14,16,128]{2,1,0:T(8,128)(2,1)S(1)}, f32[16,8,128]{2,1,0:T(8,128)S(1)}, f32[6,8,128]{2,1,0:T(8,128)S(1)}, f32[2,10,8,128]{3,2,1,0:T(8,128)S(1)}...) custom-call(f32[16,8,128]{2,1,0:T(8,128)S(1)} %get-tuple-element.62.refs_0_, ...), custom_call_target="tpu_custom_call" | custom-call | flops 1048576 | bytes 1048576 | tf_op jit(solution)/shard_map/merge/pallas_call | solution.py:487
  10.0 1.7 %collective-permute-start.3 = (bf16[14,16,128]{2,1,0:T(8,128)(2,1)S(1)}, bf16[14,16,128]{2,1,0:T(8,128)(2,1)S(1)}, u32[]{:S(2)}, u32[]{:S(2)}) collective-permute-start(bf16[14,16,128]{2,1,0:T(8,128)(2,1)S(1)} %get-tuple-element.88), channel_id=1, source_target_pairs={{0,8},{4,12},{8,0},{12,4},{1,9},{5,13},{9,1},{13,5},{2,10},{6,14},... | collective-permute-start | bytes 172040 | tf_op jit(solution)/shard_map/ppermute | solution.py:518
  11.7 0.1 collective-permute-done.1.refs_3_
  11.8 0.1 merge.3
  11.9 1.3 %collective-permute-start.2 = (bf16[8,16,128]{2,1,0:T(8,128)(2,1)S(1)}, bf16[8,16,128]{2,1,0:T(8,128)(2,1)S(1)}, u32[]{:S(2)}, u32[]{:S(2)}) collective-permute-start(bf16[8,16,128]{2,1,0:T(8,128)(2,1)S(1)} %get-tuple-element.87), channel_id=1, source_target_pairs={{0,8},{4,12},{8,0},{12,4},{1,9},{5,13},{9,1},{13,5},{2,10},{6,14},... | collective-permute-start | bytes 98312 | tf_op jit(solution)/shard_map/ppermute | solution.py:518
  13.1 3.4 %early.1.refs_11_ = bf16[256,2048]{1,0:T(8,128)(2,1)} custom-call(f32[2,10,8,128]{3,2,1,0:T(8,128)S(1)} %get-tuple-element.63.refs_1_.refs_9_.refs_2_.refs_4_.own_edges, bf16[256,1024]{1,0:T(8,128)(2,1)S(1)} %get-tuple-element.92.begun, f32[16,8,128]{2,1,0:T(8,128)S(1)} %get-tuple-element.93.begun_state, f32[256,8,128]{2,1,0:T(8,128)S(1)} %get-tuple-element.79.refs_0_, ...), custom_call_target="tpu_custom_call" | custom-call | flops 20971520 | bytes 1048576 | tf_op jit(solution)/shard_map/early/pallas_call | solution.py:487
  16.6 0.0 collective-permute-done.3.refs_8_.refs_9_
  16.6 0.1 collective-permute-done.2.refs_8_
  16.7 0.1 late.3
  (5 shorter events, 0.0 us)
Async XLA Ops:
  3.0 6.7 %collective-permute-start = (bf16[18,16,128]{2,1,0:T(8,128)(2,1)S(1)}, bf16[18,16,128]{2,1,0:T(8,128)(2,1)S(1)}, u32[]{:S(2)}, u32[]{:S(2)}) collective-permute-start(bf16[18,16,128]{2,1,0:T(8,128)(2,1)S(1)} %get-tuple-element.64), channel_id=1, source_target_pairs={{0,4},{4,0},{8,12},{12,8},{1,5},{5,1},{9,13},{13,9},{2,6},{6,2},{1... | collective-permute-start | bytes 221192 | tf_op jit(solution)/shard_map/ppermute | solution.py:518
  7.8 4.0 %collective-permute-start.1 = (bf16[8,16,128]{2,1,0:T(8,128)(2,1)S(1)}, bf16[8,16,128]{2,1,0:T(8,128)(2,1)S(1)}, u32[]{:S(2)}, u32[]{:S(2)}) collective-permute-start(bf16[8,16,128]{2,1,0:T(8,128)(2,1)S(1)} %get-tuple-element.80), channel_id=1, source_target_pairs={{0,4},{4,0},{8,12},{12,8},{1,5},{5,1},{9,13},{13,9},{2,6},{6,2},{1... | collective-permute-start | bytes 98312 | tf_op jit(solution)/shard_map/ppermute | solution.py:518
  10.0 6.6 %collective-permute-start.3 = (bf16[14,16,128]{2,1,0:T(8,128)(2,1)S(1)}, bf16[14,16,128]{2,1,0:T(8,128)(2,1)S(1)}, u32[]{:S(2)}, u32[]{:S(2)}) collective-permute-start(bf16[14,16,128]{2,1,0:T(8,128)(2,1)S(1)} %get-tuple-element.88), channel_id=1, source_target_pairs={{0,8},{4,12},{8,0},{12,4},{1,9},{5,13},{9,1},{13,5},{2,10},{6,14},... | collective-permute-start | bytes 172040 | tf_op jit(solution)/shard_map/ppermute | solution.py:518
  11.9 4.9 %collective-permute-start.2 = (bf16[8,16,128]{2,1,0:T(8,128)(2,1)S(1)}, bf16[8,16,128]{2,1,0:T(8,128)(2,1)S(1)}, u32[]{:S(2)}, u32[]{:S(2)}) collective-permute-start(bf16[8,16,128]{2,1,0:T(8,128)(2,1)S(1)} %get-tuple-element.87), channel_id=1, source_target_pairs={{0,8},{4,12},{8,0},{12,4},{1,9},{5,13},{9,1},{13,5},{2,10},{6,14},... | collective-permute-start | bytes 98312 | tf_op jit(solution)/shard_map/ppermute | solution.py:518
